TPU v7x, 32 devices: a whole 2x2x4 slice. The times are simulated.
32 devices in a mesh: head: 4 (over z), wide: 8 (over y, x, core).
Axes of the slice: x: 2, y: 2, z: 4, core: 2. Of those that a mesh axis runs over, the one named last changes fastest.
Arguments:
- hidden_in: bfloat16 [3, 8, 512, 1024], P(None, 'wide', 'head'), may hold values from -6 to 6
- cotangent: bfloat16 [3, 8, 512, 1024], P(None, 'wide', 'head'), may hold values from -6 to 6
- doc_starts: int32 [3, 4], replicated, may hold values from 0 to 4095, as said below
- gain_in: bfloat16 [1024], P(('head', 'wide')), may hold values from 0.5 to 1.5
- mamba_gate_w: bfloat16 [1024, 1536], P(('head', 'wide')), may hold values from -0.1875 to 0.1875
- mamba_in_w: bfloat16 [1024, 1536], P(('head', 'wide')), may hold values from -0.1875 to 0.1875
- mamba_bc_w: bfloat16 [1024, 256], P(('head', 'wide')), may hold values from -0.09375 to 0.09375
- mamba_dt_w: bfloat16 [1024, 24], P(('head', 'wide')), may hold values from -0.1875 to 0.1875
- dt_bias: float32 [24], replicated, may hold values from -0.5 to 1
- a_log: float32 [24], replicated, may hold values from -16 to 0
- d_skip: float32 [24], replicated, may hold values from 0.5 to 2
- conv_x: bfloat16 [4, 1536], P(None, ('head', 'wide')), may hold values from -3 to 3
- conv_bc: bfloat16 [4, 256], P(None, ('head', 'wide')), may hold values from -1.5 to 1.5
- mamba_gain: bfloat16 [1536], P(('head', 'wide')), may hold values from 0.5 to 1.5
- attn_q_w: bfloat16 [1024, 512], P(('head', 'wide')), may hold values from -0.1875 to 0.1875
- attention_key_value_weight: bfloat16 [1024, 256], P(('head', 'wide')), may hold values from -0.1875 to 0.1875
- mamba_out_w: bfloat16 [1536, 1024], P(('head', 'wide')), may hold values from -0.15625 to 0.15625
- attn_out_w: bfloat16 [512, 1024], P(('head', 'wide')), may hold values from -2 to 2
- gain_ffn: bfloat16 [1024], P(('head', 'wide')), may hold values from 0.5 to 1.5
- ffn_gate_w: bfloat16 [1024, 2048], P(('head', 'wide')), may hold values from -0.1875 to 0.1875
- ffn_up_w: bfloat16 [1024, 2048], P(('head', 'wide')), may hold values from -0.1875 to 0.1875
- ffn_down_w: bfloat16 [2048, 1024], P(('head', 'wide')), may hold values from -0.125 to 0.125
Outputs:
- out: bfloat16 [3, 8, 512, 1024], P(None, 'wide', 'head')
- grad_x: bfloat16 [3, 8, 512, 1024], P(None, 'wide', 'head')
- grad_gain_in: float32 [1024], P(('head', 'wide'))
- grad_mamba_gate_w: float32 [1024, 1536], P(('head', 'wide'))
- grad_mamba_in_w: float32 [1024, 1536], P(('head', 'wide'))
- grad_mamba_bc_w: float32 [1024, 256], P(('head', 'wide'))
- grad_mamba_dt_w: float32 [1024, 24], P(('head', 'wide'))
- grad_dt_bias: float32 [24], replicated
- grad_a_log: float32 [24], replicated
- grad_d_skip: float32 [24], replicated
- grad_conv_x: float32 [4, 1536], P(None, ('head', 'wide'))
- grad_conv_bc: float32 [4, 256], P(None, ('head', 'wide'))
- grad_mamba_gain: float32 [1536], P(('head', 'wide'))
- grad_attn_q_w: float32 [1024, 512], P(('head', 'wide'))
- grad_attn_kv_w: float32 [1024, 256], P(('head', 'wide'))
- grad_mamba_out_w: float32 [1536, 1024], P(('head', 'wide'))
- grad_attn_out_w: float32 [512, 1024], P(('head', 'wide'))
- grad_gain_ffn: float32 [1024], P(('head', 'wide'))
- grad_ffn_gate_w: float32 [1024, 2048], P(('head', 'wide'))
- grad_ffn_up_w: float32 [1024, 2048], P(('head', 'wide'))
- grad_ffn_down_w: float32 [2048, 1024], P(('head', 'wide'))
Inputs may be any that keep to these rules, and one draw needn't show every extreme that they name: `doc_starts`: each row holds 4 increasing start positions: the first 0, the second in 1 .. 511, the third in 3585 .. 3840, the fourth in 3841 .. 4095; so the second document runs from the first wide block into the last.
All inputs are finite; a program needn't handle non-finite values.
Results may differ from a plain program's by a relative error of at most 0.035.
Values may be sent and summed in bfloat16 or wider, within the bound.
No kernel may reach another device: no remote copies, remote signals or barrier semaphores. Data moves between devices by JAX's collectives and lax.ppermute only.
A program may use at most 320 MiB of HBM per device.

v0:
```python
from functools import partial

import jax
import jax.numpy as jnp
from jax import lax
from jax.sharding import PartitionSpec as P

QUERY_HEADS = 8
KEY_VALUE_HEADS = 2
HEAD_SIZE = 64


epsilon = 1e-05
highest = lax.Precision.HIGHEST
key_limit = 1024


def shifted(value, axis, steps):
    count = lax.axis_size(axis)
    initial, last = (max(0, -steps), min(count, count - steps))
    return lax.ppermute(value, axis, [(source, source + steps) for source in range(initial, last)])


def carried_in(array, axis, join, neutral, backward):
    count = lax.axis_size(axis)
    place = lax.axis_index(axis)
    ahead = count - 1 - place if backward else place
    gathered = jax.tree.map(
        lambda a, kind: lax.all_gather(a.astype(kind), axis),
        array,
        jax.tree.map(lambda a: jnp.bfloat16 if a.dtype == jnp.float32 else a.dtype, array),
    )
    state = jax.tree.map(lambda a, e: jnp.zeros_like(a) + jnp.asarray(e, a.dtype), array, neutral)

    def one(step, state):
        source = count - 1 - step if backward else step
        return join(
            state,
            jax.tree.map(
                lambda a, own: lax.dynamic_index_in_dim(a, source, 0, False).astype(own.dtype),
                gathered,
                array,
            ),
        )

    return lax.fori_loop(0, ahead, one, state)


def rms_scale(values, scales):
    return values * lax.rsqrt(jnp.mean(values * values, axis=-1, keepdims=True) + epsilon) * scales


def doc_index(starts, positions):
    passed = (starts[None, :] <= positions[:, None]).astype(jnp.int32)
    return jnp.sum(passed, axis=1) - 1


def dot_plain(left, right):
    return jnp.dot(left, right, preferred_element_type=jnp.float32)


def dot_right_t(left, right):
    return lax.dot_general(
        left, right, (((1,), (1,)), ((), ())), preferred_element_type=jnp.float32
    )


def dot_left_t(left, right):
    return lax.dot_general(
        left, right, (((0,), (0,)), ((), ())), preferred_element_type=jnp.float32
    )


def place_into(local_part, full_size, offset, along):
    full_shape = list(local_part.shape)
    full_shape[along] = full_size
    return lax.dynamic_update_slice_in_dim(
        jnp.zeros(full_shape, jnp.float32), local_part, offset, along
    )


def conv_mix(extended, taps_w, doc_ext, doc_here):
    length = doc_here.shape[0]
    result = jnp.zeros((length, extended.shape[1]), jnp.float32)
    for offset in range(taps_w.shape[0]):
        window = extended[offset : offset + length]
        same_doc = (doc_ext[offset : offset + length] == doc_here).astype(jnp.float32)
        result = result + taps_w[offset][None, :] * window * same_doc[:, None]
    return result


def section_one(
    x_ext, bc_ext, dt_raw, conv_xl, conv_bcl, bias_l, alog_l, doc_ext, doc_here, prev_doc
):
    length = doc_here.shape[0]
    head_count = bias_l.shape[0]
    x_act = jax.nn.silu(conv_mix(x_ext, conv_xl, doc_ext, doc_here)).reshape(length, head_count, -1)
    bc_act = jax.nn.silu(conv_mix(bc_ext, conv_bcl, doc_ext, doc_here))
    state_n = bc_act.shape[1] // 2
    b_mat = bc_act[:, :state_n]
    c_mat = bc_act[:, state_n:]
    step_size = jax.nn.softplus(dt_raw + bias_l[None, :])
    cum_log = jnp.cumsum(-jnp.exp(alog_l)[None, :] * step_size, axis=0)
    last_same = (doc_here == doc_here[length - 1]).astype(jnp.float32)
    tail_weight = jnp.exp(cum_log[length - 1][None, :] - cum_log) * step_size * last_same[:, None]
    state_loc = jnp.einsum("sh,shp,sn->hpn", tail_weight, x_act, b_mat, precision=highest)
    block_decay = jnp.where(doc_here[length - 1] == prev_doc, jnp.exp(cum_log[length - 1]), 0.0)
    return ((x_act, b_mat, c_mat, step_size, cum_log), state_loc, block_decay)


def section_two(feats, state_in, gate_z, skip_l, gain_l, doc_here, prev_doc):
    x_act, b_mat, c_mat, step_size, cum_log = feats
    length, head_count, head_dim = x_act.shape
    index_row = jnp.arange(length)
    allowed = (index_row[:, None] >= index_row[None, :]) & (doc_here[:, None] == doc_here[None, :])
    gram_cb = jnp.dot(c_mat, b_mat.T, precision=highest)
    log_gaps = cum_log.T[:, :, None] - cum_log.T[:, None, :]
    weights = (
        jnp.exp(jnp.where(allowed[None], log_gaps, -1e30)) * gram_cb[None] * step_size.T[:, None, :]
    )
    inside = jnp.einsum("hts,shp->thp", weights, x_act, precision=highest)
    entering = (doc_here == prev_doc).astype(jnp.float32)[:, None] * jnp.exp(cum_log)
    carried = jnp.einsum("tn,hpn->thp", c_mat, state_in, precision=highest) * entering[:, :, None]
    mixed = inside + carried + skip_l[None, :, None] * x_act
    gated_y = mixed * jax.nn.silu(gate_z).reshape(length, head_count, head_dim)
    normed = rms_scale(gated_y, gain_l.reshape(head_count, head_dim))
    return normed.reshape(length, head_count * head_dim)


def chain_state(earlier, later):
    return (earlier[0] * later[0], later[0][:, None, None] * earlier[1] + later[1])


def per_device(
    hidden_in,
    cotangent,
    doc_starts,
    gain_in,
    mamba_gate_w,
    mamba_in_w,
    mamba_bc_w,
    mamba_dt_w,
    dt_bias,
    a_log,
    d_skip,
    conv_x,
    conv_bc,
    mamba_gain,
    attn_q_w,
    attention_key_value_weight,
    mamba_out_w,
    attn_out_w,
    gain_ffn,
    ffn_gate_w,
    ffn_up_w,
    ffn_down_w,
):
    heads_dev = lax.axis_size("head")
    wide_dev = lax.axis_size("wide")
    head_number = lax.axis_index("head")
    wide_id = lax.axis_index("wide")
    micro_count = hidden_in.shape[0]
    tok_dev = hidden_in.shape[2]
    block_tok = tok_dev * heads_dev
    total_tok = block_tok * wide_dev
    tap_count = conv_x.shape[0]
    mamba_heads = dt_bias.shape[0]
    heads_here = mamba_heads // heads_dev
    head_start = head_number * heads_here
    inner_total = mamba_gate_w.shape[1]
    inner_here = inner_total // heads_dev
    col_start = head_number * inner_here
    query_total = attn_q_w.shape[1]
    query_cols = query_total // heads_dev
    query_start = head_number * query_cols
    query_local = QUERY_HEADS // heads_dev
    kv_total = attention_key_value_weight.shape[1]
    key_value_start = head_number * query_local // (QUERY_HEADS // KEY_VALUE_HEADS) * 2 * HEAD_SIZE
    score_scale = HEAD_SIZE ** (-0.5)
    key_rows = min(key_limit, total_tok)
    key_count = total_tok // key_rows
    block_starts = jnp.arange(key_count, dtype=jnp.int32) * key_rows
    bias_l = lax.dynamic_slice_in_dim(dt_bias, head_start, heads_here, 0)
    alog_l = lax.dynamic_slice_in_dim(a_log, head_start, heads_here, 0)
    skip_l = lax.dynamic_slice_in_dim(d_skip, head_start, heads_here, 0)
    totals = None
    result_out = []
    result_dx = []
    for micro in range(micro_count):
        gate_cols = lax.dynamic_slice_in_dim(
            lax.all_gather(mamba_gate_w, ("head", "wide"), axis=0, tiled=True),
            col_start,
            inner_here,
            1,
        )
        input_cols = lax.dynamic_slice_in_dim(
            lax.all_gather(mamba_in_w, ("head", "wide"), axis=0, tiled=True),
            col_start,
            inner_here,
            1,
        )
        query_part = lax.dynamic_slice_in_dim(
            lax.all_gather(attn_q_w, ("head", "wide"), axis=0, tiled=True),
            query_start,
            query_cols,
            1,
        )
        mamba_rows = lax.dynamic_slice_in_dim(
            lax.all_gather(mamba_out_w, ("head", "wide"), axis=0, tiled=True),
            col_start,
            inner_here,
            0,
        )
        attn_rows = lax.dynamic_slice_in_dim(
            lax.all_gather(attn_out_w, ("head", "wide"), axis=0, tiled=True),
            query_start,
            query_cols,
            0,
        )
        weights = dict(
            gain_in=lax.all_gather(gain_in, ("head", "wide"), axis=0, tiled=True).astype(
                jnp.float32
            ),
            gate_cols=gate_cols,
            input_cols=input_cols,
            bc_cols=lax.all_gather(mamba_bc_w, ("head", "wide"), axis=0, tiled=True),
            dt_cols=lax.dynamic_slice_in_dim(
                lax.all_gather(mamba_dt_w, ("head", "wide"), axis=0, tiled=True),
                head_start,
                heads_here,
                1,
            ),
            conv_xl=lax.dynamic_slice_in_dim(
                lax.all_gather(conv_x, ("head", "wide"), axis=1, tiled=True),
                col_start,
                inner_here,
                1,
            ).astype(jnp.float32),
            conv_bcl=lax.all_gather(conv_bc, ("head", "wide"), axis=1, tiled=True).astype(
                jnp.float32
            ),
            gain_mamba=lax.dynamic_slice_in_dim(
                lax.all_gather(mamba_gain, ("head", "wide"), axis=0, tiled=True),
                col_start,
                inner_here,
                0,
            ).astype(jnp.float32),
            query_cols=query_part,
            kv_cols=lax.dynamic_slice_in_dim(
                lax.all_gather(attention_key_value_weight, ("head", "wide"), axis=0, tiled=True),
                key_value_start,
                2 * HEAD_SIZE,
                1,
            ),
            mamba_rows=mamba_rows,
            attn_rows=attn_rows,
            gain_ffn=lax.all_gather(gain_ffn, ("head", "wide"), axis=0, tiled=True).astype(
                jnp.float32
            ),
            gate_w=lax.all_gather(ffn_gate_w, ("head", "wide"), axis=0, tiled=True),
            up_w=lax.all_gather(ffn_up_w, ("head", "wide"), axis=0, tiled=True),
            down_w=lax.all_gather(ffn_down_w, ("head", "wide"), axis=0, tiled=True),
        )
        starts = doc_starts[micro]
        block_base = wide_id * block_tok
        last_pos = block_base + block_tok - 1
        positions = block_base + jnp.arange(block_tok, dtype=jnp.int32)
        doc_here = doc_index(starts, positions)
        prev_doc = doc_index(starts, jnp.reshape(block_base - 1, (1,)))[0]
        doc_ext = doc_index(
            starts,
            block_base - (tap_count - 1) + jnp.arange(block_tok + tap_count - 1, dtype=jnp.int32),
        )
        x_tokens = hidden_in[micro, 0].astype(jnp.float32)
        normed_in, pull_in = jax.vjp(rms_scale, x_tokens, weights["gain_in"])
        block_in = lax.all_gather(normed_in.astype(jnp.bfloat16), "head", axis=0, tiled=True)
        gate_z = dot_plain(block_in, weights["gate_cols"])
        x_raw = dot_plain(block_in, weights["input_cols"])
        bc_raw = dot_plain(block_in, weights["bc_cols"])
        dt_raw = dot_plain(block_in, weights["dt_cols"])
        queries = dot_plain(block_in, weights["query_cols"]).astype(jnp.bfloat16)
        keyvals = dot_plain(block_in, weights["kv_cols"]).astype(jnp.bfloat16)
        rim_from = block_tok - tap_count + 1
        rim_got = shifted(jnp.concatenate([x_raw[rim_from:], bc_raw[rim_from:]], axis=1), "wide", 1)
        x_ext = jnp.concatenate([rim_got[:, :inner_here], x_raw], axis=0)
        bc_ext = jnp.concatenate([rim_got[:, inner_here:], bc_raw], axis=0)
        first_section = partial(section_one, doc_ext=doc_ext, doc_here=doc_here, prev_doc=prev_doc)
        (feats, state_loc, block_decay), pull_one = jax.vjp(
            first_section,
            x_ext,
            bc_ext,
            dt_raw,
            weights["conv_xl"],
            weights["conv_bcl"],
            bias_l,
            alog_l,
        )
        identity = (jnp.ones_like(block_decay), jnp.zeros_like(state_loc))
        state_in = carried_in((block_decay, state_loc), "wide", chain_state, identity, False)[1]
        second_section = partial(section_two, doc_here=doc_here, prev_doc=prev_doc)
        mamba_y, pull_two = jax.vjp(
            second_section, feats, state_in, gate_z, skip_l, weights["gain_mamba"]
        )
        mamba_low = mamba_y.astype(jnp.bfloat16)
        key_all = lax.all_gather(keyvals, "wide", axis=0, tiled=True)
        key_blocks = key_all.reshape(key_count, key_rows, key_all.shape[1])
        q_heads = queries.reshape(block_tok, query_local, HEAD_SIZE)

        def scores_of(key_piece, piece_start):
            key_pos = piece_start + jnp.arange(key_piece.shape[0], dtype=jnp.int32)
            key_doc = doc_index(starts, key_pos)
            allowed = (key_pos[None, :] <= positions[:, None]) & (
                key_doc[None, :] == doc_here[:, None]
            )
            scores = (
                jnp.einsum(
                    "qhd,kd->qhk",
                    q_heads,
                    key_piece[:, :HEAD_SIZE],
                    preferred_element_type=jnp.float32,
                )
                * score_scale
            )
            return (jnp.where(allowed[:, None, :], scores, -1e30), allowed[:, None, :])

        def max_step(running, inputs):

            def max_live():
                masked, allowed = scores_of(inputs[0], inputs[1])
                new_max = jnp.maximum(running[0], jnp.max(masked, axis=-1))
                new_sum = running[1] * jnp.exp(running[0] - new_max) + jnp.sum(
                    jnp.where(allowed, jnp.exp(masked - new_max[..., None]), 0.0), axis=-1
                )
                return (new_max, new_sum)

            return (lax.cond(inputs[1] <= last_pos, max_live, lambda: running), None)

        start_max = jnp.full((block_tok, query_local), -1e30, jnp.float32)
        (run_max, run_sum), _unused = lax.scan(
            max_step, (start_max, jnp.zeros_like(start_max)), (key_blocks, block_starts)
        )
        log_sum = run_max + jnp.log(run_sum)

        def value_step(running, inputs):

            def value_live():
                masked, allowed = scores_of(inputs[0], inputs[1])
                probs = jnp.where(allowed, jnp.exp(masked - log_sum[..., None]), 0.0).astype(
                    jnp.bfloat16
                )
                return running + jnp.einsum(
                    "qhk,kd->qhd",
                    probs,
                    inputs[0][:, HEAD_SIZE:],
                    preferred_element_type=jnp.float32,
                )

            return (lax.cond(inputs[1] <= last_pos, value_live, lambda: running), None)

        attn_raw, _unused = lax.scan(
            value_step,
            jnp.zeros((block_tok, query_local, HEAD_SIZE), jnp.float32),
            (key_blocks, block_starts),
        )
        attn_low = attn_raw.reshape(block_tok, query_local * HEAD_SIZE).astype(jnp.bfloat16)
        part_mamba = lax.slice_in_dim(mamba_low, 0, lax.axis_size("head") * tok_dev, axis=0)
        mix = lax.psum_scatter(
            (
                dot_plain(part_mamba, weights["mamba_rows"])
                + dot_plain(attn_low, weights["attn_rows"])
            ).astype(jnp.bfloat16),
            "head",
            scatter_dimension=0,
            tiled=True,
        ).astype(jnp.float32)
        resid = x_tokens + mix
        normed_ffn, pull_ffn = jax.vjp(rms_scale, resid, weights["gain_ffn"])
        ffn_in = normed_ffn.astype(jnp.bfloat16)
        gate_val = dot_plain(ffn_in, weights["gate_w"])
        up_val = dot_plain(ffn_in, weights["up_w"])
        sigma_gate = jax.nn.sigmoid(gate_val)
        silu_val = gate_val * sigma_gate
        act_low = (silu_val * up_val).astype(jnp.bfloat16)
        result_out.append((resid + dot_plain(act_low, weights["down_w"])).astype(jnp.bfloat16))
        d_out_low = cotangent[micro, 0]
        d_act = dot_right_t(d_out_low, weights["down_w"])
        grad_down = dot_left_t(act_low, d_out_low)
        d_gate = (d_act * up_val * sigma_gate * (1.0 + gate_val * (1.0 - sigma_gate))).astype(
            jnp.bfloat16
        )
        d_up = (d_act * silu_val).astype(jnp.bfloat16)
        d_ffn_in = dot_right_t(d_gate, weights["gate_w"]) + dot_right_t(d_up, weights["up_w"])
        grad_gate = dot_left_t(ffn_in, d_gate)
        grad_up = dot_left_t(ffn_in, d_up)
        d_resid_norm, grad_gain_ffn = pull_ffn(d_ffn_in)
        d_resid = d_out_low.astype(jnp.float32) + d_resid_norm
        d_block = lax.all_gather(d_resid.astype(jnp.bfloat16), "head", axis=0, tiled=True)
        d_mamba = dot_right_t(d_block, weights["mamba_rows"])
        d_attn = dot_right_t(d_block, weights["attn_rows"]).astype(jnp.bfloat16)
        grad_mamba_rows = dot_left_t(mamba_low, d_block)
        grad_attn_rows = dot_left_t(attn_low, d_block)
        d_feats, d_state_in, d_gate_z, grad_skip, grad_gain_m = pull_two(d_mamba)
        d_state_loc = carried_in((block_decay, d_state_in), "wide", chain_state, identity, True)[1]
        d_decay = jnp.sum(d_state_loc * state_in, axis=(1, 2))
        d_x_ext, d_bc_ext, d_dt_raw, grad_conv_x, grad_conv_bc, grad_bias, grad_alog = pull_one(
            (d_feats, d_state_loc, d_decay)
        )
        rim_came = shifted(
            jnp.concatenate([d_x_ext[: tap_count - 1], d_bc_ext[: tap_count - 1]], axis=1),
            "wide",
            -1,
        )
        d_x_raw = d_x_ext[tap_count - 1 :].at[rim_from:].add(rim_came[:, :inner_here])
        d_bc_raw = d_bc_ext[tap_count - 1 :].at[rim_from:].add(rim_came[:, inner_here:])
        d_gate_low = d_gate_z.astype(jnp.bfloat16)
        d_x_low = d_x_raw.astype(jnp.bfloat16)
        d_bc_low = d_bc_raw.astype(jnp.bfloat16)
        d_dt_low = d_dt_raw.astype(jnp.bfloat16)
        d_heads = d_attn.reshape(block_tok, query_local, HEAD_SIZE)
        row_dot = jnp.sum(d_heads.astype(jnp.float32) * attn_raw, axis=-1)

        def grad_step(running, inputs):

            def grad_live():
                masked, allowed = scores_of(inputs[0], inputs[1])
                probs = jnp.where(allowed, jnp.exp(masked - log_sum[..., None]), 0.0)
                probs_low = probs.astype(jnp.bfloat16)
                d_value = jnp.einsum(
                    "qhk,qhd->kd", probs_low, d_heads, preferred_element_type=jnp.float32
                )
                d_probs = jnp.einsum(
                    "qhd,kd->qhk",
                    d_heads,
                    inputs[0][:, HEAD_SIZE:],
                    preferred_element_type=jnp.float32,
                )
                d_scores = (probs * (d_probs - row_dot[..., None])).astype(jnp.bfloat16)
                d_key = (
                    jnp.einsum("qhk,qhd->kd", d_scores, q_heads, preferred_element_type=jnp.float32)
                    * score_scale
                )
                updated = running + jnp.einsum(
                    "qhk,kd->qhd",
                    d_scores,
                    inputs[0][:, :HEAD_SIZE],
                    preferred_element_type=jnp.float32,
                )
                return (updated, jnp.concatenate([d_key, d_value], axis=1))

            def skipped():
                return (running, jnp.zeros((inputs[0].shape[0], 2 * HEAD_SIZE), jnp.float32))

            return lax.cond(inputs[1] <= last_pos, grad_live, skipped)

        d_query_sum, d_kv_blocks = lax.scan(
            grad_step,
            jnp.zeros((block_tok, query_local, HEAD_SIZE), jnp.float32),
            (key_blocks, block_starts),
        )
        d_query_low = (
            (d_query_sum * score_scale)
            .reshape(block_tok, query_local * HEAD_SIZE)
            .astype(jnp.bfloat16)
        )
        d_kv_low = lax.psum_scatter(
            d_kv_blocks.reshape(total_tok, 2 * HEAD_SIZE).astype(jnp.bfloat16),
            "wide",
            scatter_dimension=0,
            tiled=True,
        )
        grad_gate_cols = dot_left_t(block_in, d_gate_low)
        grad_input_cols = dot_left_t(block_in, d_x_low)
        grad_bc_cols = dot_left_t(block_in, d_bc_low)
        grad_dt_cols = dot_left_t(block_in, d_dt_low)
        grad_query = dot_left_t(block_in, d_query_low)
        grad_kv = dot_left_t(block_in, d_kv_low)

        def take_rows(source):
            return lax.slice_in_dim(source, 0, lax.axis_size("head") * tok_dev, axis=0)

        result = dot_right_t(take_rows(d_gate_low), weights["gate_cols"])
        result = result + dot_right_t(take_rows(d_x_low), weights["input_cols"])
        result = result + dot_right_t(take_rows(d_bc_low), weights["bc_cols"])
        result = result + dot_right_t(take_rows(d_dt_low), weights["dt_cols"])
        result = result + dot_right_t(take_rows(d_query_low), weights["query_cols"])
        d_normed_in = lax.psum_scatter(
            (result + dot_right_t(take_rows(d_kv_low), weights["kv_cols"])).astype(jnp.bfloat16),
            "head",
            scatter_dimension=0,
            tiled=True,
        ).astype(jnp.float32)
        d_x_norm, grad_gain_in = pull_in(d_normed_in)
        result_dx.append((d_resid + d_x_norm).astype(jnp.bfloat16))
        local_set = (
            grad_gain_in,
            grad_gate_cols,
            grad_input_cols,
            grad_bc_cols,
            grad_dt_cols,
            grad_conv_x,
            grad_conv_bc,
            grad_gain_m,
            grad_query,
            grad_kv,
            grad_mamba_rows,
            grad_attn_rows,
            grad_gain_ffn,
            grad_gate,
            grad_up,
            grad_down,
            grad_bias,
            grad_alog,
            grad_skip,
        )
        totals = local_set if totals is None else jax.tree.map(jnp.add, totals, local_set)
    owned_part = (
        lax.psum_scatter(totals[0], ("head", "wide"), scatter_dimension=0, tiled=True),
        lax.psum_scatter(
            place_into(totals[1], inner_total, col_start, 1),
            ("head", "wide"),
            scatter_dimension=0,
            tiled=True,
        ),
        lax.psum_scatter(
            place_into(totals[2], inner_total, col_start, 1),
            ("head", "wide"),
            scatter_dimension=0,
            tiled=True,
        ),
        lax.psum_scatter(totals[3], ("head", "wide"), scatter_dimension=0, tiled=True),
        lax.psum_scatter(
            place_into(totals[4], mamba_heads, head_start, 1),
            ("head", "wide"),
            scatter_dimension=0,
            tiled=True,
        ),
        lax.psum_scatter(
            place_into(totals[5], inner_total, col_start, 1),
            ("head", "wide"),
            scatter_dimension=1,
            tiled=True,
        ),
        lax.psum_scatter(totals[6], ("head", "wide"), scatter_dimension=1, tiled=True),
        lax.psum_scatter(
            place_into(totals[7], inner_total, col_start, 0),
            ("head", "wide"),
            scatter_dimension=0,
            tiled=True,
        ),
        lax.psum_scatter(
            place_into(totals[8], query_total, query_start, 1),
            ("head", "wide"),
            scatter_dimension=0,
            tiled=True,
        ),
        lax.psum_scatter(
            place_into(totals[9], kv_total, key_value_start, 1),
            ("head", "wide"),
            scatter_dimension=0,
            tiled=True,
        ),
        lax.psum_scatter(
            place_into(totals[10], inner_total, col_start, 0),
            ("head", "wide"),
            scatter_dimension=0,
            tiled=True,
        ),
        lax.psum_scatter(
            place_into(totals[11], query_total, query_start, 0),
            ("head", "wide"),
            scatter_dimension=0,
            tiled=True,
        ),
        lax.psum_scatter(totals[12], ("head", "wide"), scatter_dimension=0, tiled=True),
        lax.psum_scatter(totals[13], ("head", "wide"), scatter_dimension=0, tiled=True),
        lax.psum_scatter(totals[14], ("head", "wide"), scatter_dimension=0, tiled=True),
        lax.psum_scatter(totals[15], ("head", "wide"), scatter_dimension=0, tiled=True),
    )
    owned_part = tuple(owned_part)
    per_head = lax.psum(
        (
            place_into(totals[16], mamba_heads, head_start, 0),
            place_into(totals[17], mamba_heads, head_start, 0),
            place_into(totals[18], mamba_heads, head_start, 0),
        ),
        ("head", "wide"),
    )
    totals = owned_part + tuple(per_head)
    outputs = jnp.stack(result_out)[:, None]
    input_grads = jnp.stack(result_dx)[:, None]
    return (
        outputs,
        input_grads,
        totals[0],
        totals[1],
        totals[2],
        totals[3],
        totals[4],
        totals[16],
        totals[17],
        totals[18],
        totals[5],
        totals[6],
        totals[7],
        totals[8],
        totals[9],
        totals[10],
        totals[11],
        totals[12],
        totals[13],
        totals[14],
        totals[15],
    )


def solution(mesh):
    in_specs = (
        P(None, "wide", "head", None),
        P(None, "wide", "head", None),
        P(),
        P(("head", "wide")),
        P(("head", "wide"), None),
        P(("head", "wide"), None),
        P(("head", "wide"), None),
        P(("head", "wide"), None),
        P(),
        P(),
        P(),
        P(None, ("head", "wide")),
        P(None, ("head", "wide")),
        P(("head", "wide")),
        P(("head", "wide"), None),
        P(("head", "wide"), None),
        P(("head", "wide"), None),
        P(("head", "wide"), None),
        P(("head", "wide")),
        P(("head", "wide"), None),
        P(("head", "wide"), None),
        P(("head", "wide"), None),
    )
    out_specs = (
        P(None, "wide", "head", None),
        P(None, "wide", "head", None),
        P(("head", "wide")),
        P(("head", "wide"), None),
        P(("head", "wide"), None),
        P(("head", "wide"), None),
        P(("head", "wide"), None),
        P(),
        P(),
        P(),
        P(None, ("head", "wide")),
        P(None, ("head", "wide")),
        P(("head", "wide")),
        P(("head", "wide"), None),
        P(("head", "wide"), None),
        P(("head", "wide"), None),
        P(("head", "wide"), None),
        P(("head", "wide")),
        P(("head", "wide"), None),
        P(("head", "wide"), None),
        P(("head", "wide"), None),
    )
    return jax.shard_map(
        per_device, mesh=mesh, in_specs=in_specs, out_specs=out_specs, check_vma=False
    )
```

profile of v0, /device:TPU:24, one launch (start us, length us, event | category | flops | bytes accessed | tf_op | source)
XLA Modules:
  0.0 3107.1 jit_solution(3871199632200632825)
XLA Ops:
  11.3 39.2 %all-reduce.68 = (bf16[1024]{0:T(1024)(128)(2,1)S(1)}, bf16[1536]{0:T(1024)(128)(2,1)S(1)}, bf16[1024]{0:T(1024)(128)(2,1)}) all-reduce(bf16[1024]{0:T(1024)(128)(2,1)S(1)} %dynamic-update-slice.18, bf16[1536]{0:T(1024)(128)(2,1)S(1)} %dynamic-update-slice.19, ...), channel_id=1, replica_groups=mesh['head'=4,'wide'=8] {'head','wide'}, use_global_device_ids=true, to_apply=%add.60 | all-reduce | flops 3584 | bytes 14336
  55.4 36.9 %all_gather.174 = bf16[1024,256]{1,0:T(8,128)(2,1)S(1)} all-gather(bf16[32,256]{1,0:T(8,128)(2,1)} %param.98), channel_id=1, replica_groups=mesh['head'=4,'wide'=8] {'head','wide'}, dimensions={0}, use_global_device_ids=true | all-gather | bytes 540672 | tf_op jit(solution)/shard_map/all_gather | solution.py:250
  100.4 37.5 %all-gather.6 = bf16[32,48,4]{1,2,0:T(4,128)(2,1)S(1)} all-gather(bf16[1,48,4]{1,2,0:T(4,128)(2,1)S(1)} %bitcast.1243), channel_id=1, replica_groups=mesh['head'=4,'wide'=8] {'head','wide'}, dimensions={0}, use_global_device_ids=true | all-gather | bytes 12672 | tf_op jit(solution)/shard_map/all_gather | solution.py:234
  138.7 38.0 %all-gather.7 = bf16[32,32,24]{1,2,0:T(8,128)(2,1)S(1)} all-gather(bf16[1,32,24]{1,2,0:T(8,128)(2,1)S(1)} %bitcast.1221), channel_id=1, replica_groups=mesh['head'=4,'wide'=8] {'head','wide'}, dimensions={0}, use_global_device_ids=true | all-gather | bytes 50688 | tf_op jit(solution)/shard_map/all_gather | solution.py:228
  177.1 37.3 %all-gather.8 = bf16[32,8,4]{1,2,0:T(4,128)(2,1)S(1)} all-gather(bf16[1,8,4]{1,2,0:T(4,128)(2,1)S(1)} %bitcast.1244), channel_id=1, replica_groups=mesh['head'=4,'wide'=8] {'head','wide'}, dimensions={0}, use_global_device_ids=true | all-gather | bytes 2112 | tf_op jit(solution)/shard_map/all_gather | solution.py:239
  228.5 41.5 %all_gather.165 = bf16[1024,256]{1,0:T(8,128)(2,1)} all-gather(bf16[32,256]{1,0:T(8,128)(2,1)S(1)} %copy-done.331), channel_id=1, replica_groups=mesh['head'=4,'wide'=8] {'head','wide'}, dimensions={0}, use_global_device_ids=true | all-gather | bytes 540672 | tf_op jit(solution)/shard_map/all_gather | solution.py:226
  366.5 35.1 %all-gather.32.cloned.1.call-done = bf16[1024,1536]{1,0:T(8,128)(2,1)} async-done(((bf16[32,1536]{1,0:T(8,128)(2,1)}), bf16[1024,1536]{1,0:T(8,128)(2,1)}) %all-gather.32.cloned.1.call-update) | async-done | bytes 3145744 | tf_op jit(solution)/shard_map/all_gather | solution.py:197
  668.2 55.6 %reduce-scatter.31.cloned.1.call-done = bf16[128,1024]{1,0:T(8,128)(2,1)} async-done(((bf16[512,1024]{1,0:T(8,128)(2,1)}), bf16[128,1024]{1,0:T(8,128)(2,1)}) %reduce-scatter.31.cloned.1.call-update) | async-done | bytes 262160 | tf_op jit(solution)/shard_map/reduce_scatter | solution.py:367
  726.7 61.7 %all-gather.44.cloned.1.call-done = bf16[1024,2048]{1,0:T(8,128)(2,1)} async-done(((bf16[32,2048]{1,0:T(8,128)(2,1)}), bf16[1024,2048]{1,0:T(8,128)(2,1)}) %all-gather.44.cloned.1.call-update) | async-done | bytes 4194320 | tf_op jit(solution)/shard_map/all_gather | solution.py:260
  792.3 59.8 %all-gather.46.cloned.1.call-done = bf16[1024,2048]{1,0:T(8,128)(2,1)} async-done(((bf16[32,2048]{1,0:T(8,128)(2,1)}), bf16[1024,2048]{1,0:T(8,128)(2,1)}) %all-gather.46.cloned.1.call-update) | async-done | bytes 4194320 | tf_op jit(solution)/shard_map/all_gather | solution.py:261
  865.5 50.4 %all-gather.48.cloned.1.call-done = bf16[2048,1024]{1,0:T(8,128)(2,1)} async-done(((bf16[64,1024]{1,0:T(8,128)(2,1)}), bf16[2048,1024]{1,0:T(8,128)(2,1)}) %all-gather.48.cloned.1.call-update) | async-done | bytes 4194320 | tf_op jit(solution)/shard_map/all_gather | solution.py:262
  1556.2 117.3 %reduce-scatter.65.cloned.1.call-done = f32[32,24]{1,0:T(8,128)} async-done(((f32[1024,24]{1,0:T(8,128)}), f32[32,24]{1,0:T(8,128)}) %reduce-scatter.65.cloned.1.call-update) | async-done | bytes 3088
  1674.8 39.8 %reduce-scatter.35.cloned.1.call-done = bf16[128,1024]{1,0:T(8,128)(2,1)} async-done(((bf16[512,1024]{1,0:T(8,128)(2,1)}), bf16[128,1024]{1,0:T(8,128)(2,1)}) %reduce-scatter.35.cloned.1.call-update) | async-done | bytes 262160 | tf_op jit(solution)/shard_map/reduce_scatter | solution.py:486
  1772.6 40.7 %all-reduce.67 = (f32[1024]{0:T(1024)S(1)}, f32[24]{0:T(128)}, f32[24]{0:T(128)}, f32[24]{0:T(128)}, f32[4,256]{1,0:T(4,128)S(1)}, /*index=5*/f32[1536]{0:T(1024)S(1)}, f32[1024]{0:T(1024)S(1)}) all-reduce(f32[1024]{0:T(1024)S(1)} %add_add_fusion.15, ...), channel_id=17, replica_groups=mesh['head'=4,'wide'=8] {'head','wide'}, use_global_device_ids=true, to_apply=%region_138.140.clone | all-reduce | flops 4680 | bytes 37440
  1819.0 72.1 %reduce-scatter.49.cloned.1.call-done = f32[32,256]{1,0:T(8,128)} async-done(((f32[1024,256]{1,0:T(8,128)}), f32[32,256]{1,0:T(8,128)}) %reduce-scatter.49.cloned.1.call-update) | async-done | bytes 32784 | tf_op jit(solution)/shard_map/reduce_scatter | solution.py:530
  1891.2 133.4 %reduce-scatter.53.cloned.1.call-done = f32[32,256]{1,0:T(8,128)} async-done(((f32[1024,256]{1,0:T(8,128)}), f32[32,256]{1,0:T(8,128)}) %reduce-scatter.53.cloned.1.call-update) | async-done | bytes 32784 | tf_op jit(solution)/shard_map/reduce_scatter | solution.py:556
  2024.6 135.5 %reduce-scatter.51.cloned.1.call-done = f32[32,512]{1,0:T(8,128)} async-done(((f32[1024,512]{1,0:T(8,128)}), f32[32,512]{1,0:T(8,128)}) %reduce-scatter.51.cloned.1.call-update) | async-done | bytes 65552 | tf_op jit(solution)/shard_map/reduce_scatter | solution.py:550
  2160.1 135.7 %reduce-scatter.57.cloned.1.call-done = f32[16,1024]{1,0:T(8,128)} async-done(((f32[512,1024]{1,0:T(8,128)}), f32[16,1024]{1,0:T(8,128)}) %reduce-scatter.57.cloned.1.call-update) | async-done | bytes 65552 | tf_op jit(solution)/shard_map/reduce_scatter | solution.py:568
  2295.8 134.9 %reduce-scatter.45.cloned.1.call-done = f32[32,1536]{1,0:T(8,128)} async-done(((f32[1024,1536]{1,0:T(8,128)}), f32[32,1536]{1,0:T(8,128)}) %reduce-scatter.45.cloned.1.call-update) | async-done | bytes 196624 | tf_op jit(solution)/shard_map/reduce_scatter | solution.py:518
  2430.7 119.7 %reduce-scatter.55.cloned.1.call-done = f32[48,1024]{1,0:T(8,128)} async-done(((f32[1536,1024]{1,0:T(8,128)}), f32[48,1024]{1,0:T(8,128)}) %reduce-scatter.55.cloned.1.call-update) | async-done | bytes 196624 | tf_op jit(solution)/shard_map/reduce_scatter | solution.py:562
  2550.4 120.7 %reduce-scatter.47.cloned.1.call-done = f32[32,1536]{1,0:T(8,128)} async-done(((f32[1024,1536]{1,0:T(8,128)}), f32[32,1536]{1,0:T(8,128)}) %reduce-scatter.47.cloned.1.call-update) | async-done | bytes 196624 | tf_op jit(solution)/shard_map/reduce_scatter | solution.py:524
  2671.1 133.9 %reduce-scatter.59.cloned.1.call-done = f32[32,2048]{1,0:T(8,128)} async-done(((f32[1024,2048]{1,0:T(8,128)}), f32[32,2048]{1,0:T(8,128)}) %reduce-scatter.59.cloned.1.call-update) | async-done | bytes 262160 | tf_op jit(solution)/shard_map/reduce_scatter | solution.py:575
  2805.0 147.2 %reduce-scatter.61.cloned.1.call-done = f32[32,2048]{1,0:T(8,128)} async-done(((f32[1024,2048]{1,0:T(8,128)}), f32[32,2048]{1,0:T(8,128)}) %reduce-scatter.61.cloned.1.call-update) | async-done | bytes 262160 | tf_op jit(solution)/shard_map/reduce_scatter | solution.py:576
  2952.2 148.0 %reduce-scatter.63.cloned.1.call-done = f32[64,1024]{1,0:T(8,128)} async-done(((f32[2048,1024]{1,0:T(8,128)}), f32[64,1024]{1,0:T(8,128)}) %reduce-scatter.63.cloned.1.call-update) | async-done | bytes 262160 | tf_op jit(solution)/shard_map/reduce_scatter | solution.py:577
  (1689 shorter events, 1315.5 us)
Async XLA Ops:
  54.8 268.8 %all-gather.40.cloned.1.call-start = ((), (), s32[]{:S(2)}) async-start(), calls=%async_computation.26 | async-start | bytes 1081344 | tf_op jit(solution)/shard_map/all_gather | solution.py:203
  55.3 269.7 %all-gather.38.cloned.1.call-start = ((), (), s32[]{:S(2)}) async-start(), calls=%async_computation.25 | async-start | bytes 1179648 | tf_op jit(solution)/shard_map/all_gather | solution.py:305
  96.2 305.3 %all-gather.32.cloned.1.call-start = ((), (), s32[]{:S(2)}) async-start(), calls=%async_computation.22 | async-start | bytes 3244032 | tf_op jit(solution)/shard_map/all_gather | solution.py:197
  97.0 464.9 %all-gather.36.cloned.1.call-start = ((), (), s32[]{:S(2)}) async-start(), calls=%async_computation.24 | async-start | bytes 3244032 | tf_op jit(solution)/shard_map/all_gather | solution.py:209
  97.7 470.2 %all-gather.52.cloned.1.call-start = ((), (), s32[]{:S(2)}) async-start(), calls=%async_computation.33 | async-start | bytes 1179648 | tf_op jit(solution)/shard_map/all_gather | solution.py:305
  292.6 309.5 %all-gather.56.cloned.1.call-start = ((), (), s32[]{:S(2)}) async-start(), calls=%async_computation.36 | async-start | bytes 1179648 | tf_op jit(solution)/shard_map/all_gather | solution.py:305
  321.1 313.8 %reduce-scatter.27.cloned.1.call-start = ((), (), s32[]{:S(2)}) async-start(), calls=%async_computation.28 | async-start | bytes 1310720 | tf_op jit(solution)/shard_map/reduce_scatter | solution.py:367
  633.7 282.1 %all-gather.48.cloned.1.call-start = ((), (), s32[]{:S(2)}) async-start(), calls=%async_computation.31 | async-start | bytes 4325376 | tf_op jit(solution)/shard_map/all_gather | solution.py:262
  634.3 334.3 %all-gather.58.cloned.1.call-start = ((), (), s32[]{:S(2)}) async-start(), calls=%async_computation.38 | async-start | bytes 1310720 | tf_op jit(solution)/shard_map/all_gather | solution.py:397
  943.3 445.4 %reduce-scatter.33.cloned.1.call-start = ((), (), s32[]{:S(2)}) async-start(), calls=%async_computation.39 | async-start | bytes 1179648 | tf_op jit(solution)/shard_map/reduce_scatter | solution.py:465
  1360.3 313.1 %reduce-scatter.65.cloned.1.call-start = ((), (), s32[]{:S(2)}) async-start(), calls=%async_computation.57 | async-start | bytes 540672
  1369.6 345.0 %reduce-scatter.35.cloned.1.call-start = ((), (), s32[]{:S(2)}) async-start(), calls=%async_computation.40 | async-start | bytes 1310720 | tf_op jit(solution)/shard_map/reduce_scatter | solution.py:486
  1395.9 346.8 %reduce-scatter.43.cloned.1.call-start = ((), (), s32[]{:S(2)}) async-start(), calls=%async_computation.46 | async-start | bytes 1310720 | tf_op jit(solution)/shard_map/reduce_scatter | solution.py:486
  1418.9 351.9 %reduce-scatter.39.cloned.1.call-start = ((), (), s32[]{:S(2)}) async-start(), calls=%async_computation.43 | async-start | bytes 1310720 | tf_op jit(solution)/shard_map/reduce_scatter | solution.py:486
  1461.5 429.6 %reduce-scatter.49.cloned.1.call-start = ((), (), s32[]{:S(2)}) async-start(), calls=%async_computation.49 | async-start | bytes 1081344 | tf_op jit(solution)/shard_map/reduce_scatter | solution.py:530
  1466.0 558.6 %reduce-scatter.53.cloned.1.call-start = ((), (), s32[]{:S(2)}) async-start(), calls=%async_computation.51 | async-start | bytes 1081344 | tf_op jit(solution)/shard_map/reduce_scatter | solution.py:556
  1471.2 688.9 %reduce-scatter.51.cloned.1.call-start = ((), (), s32[]{:S(2)}) async-start(), calls=%async_computation.50 | async-start | bytes 2162688 | tf_op jit(solution)/shard_map/reduce_scatter | solution.py:550
  1477.0 818.8 %reduce-scatter.57.cloned.1.call-start = ((), (), s32[]{:S(2)}) async-start(), calls=%async_computation.53 | async-start | bytes 2162688 | tf_op jit(solution)/shard_map/reduce_scatter | solution.py:568
  1483.2 947.5 %reduce-scatter.45.cloned.1.call-start = ((), (), s32[]{:S(2)}) async-start(), calls=%async_computation.47 | async-start | bytes 6488064 | tf_op jit(solution)/shard_map/reduce_scatter | solution.py:518
  1492.2 1058.3 %reduce-scatter.55.cloned.1.call-start = ((), (), s32[]{:S(2)}) async-start(), calls=%async_computation.52 | async-start | bytes 6488064 | tf_op jit(solution)/shard_map/reduce_scatter | solution.py:562
  1501.6 1169.5 %reduce-scatter.47.cloned.1.call-start = ((), (), s32[]{:S(2)}) async-start(), calls=%async_computation.48 | async-start | bytes 6488064 | tf_op jit(solution)/shard_map/reduce_scatter | solution.py:524
  1510.6 1294.4 %reduce-scatter.59.cloned.1.call-start = ((), (), s32[]{:S(2)}) async-start(), calls=%async_computation.54 | async-start | bytes 8650752 | tf_op jit(solution)/shard_map/reduce_scatter | solution.py:575
  1519.0 1433.2 %reduce-scatter.61.cloned.1.call-start = ((), (), s32[]{:S(2)}) async-start(), calls=%async_computation.55 | async-start | bytes 8650752 | tf_op jit(solution)/shard_map/reduce_scatter | solution.py:576
  1527.2 1572.9 %reduce-scatter.63.cloned.1.call-start = ((), (), s32[]{:S(2)}) async-start(), calls=%async_computation.56 | async-start | bytes 8650752 | tf_op jit(solution)/shard_map/reduce_scatter | solution.py:577
  (440 other events, 13397.7 us)
Sparse Core Ops, SparseCore 0:
  144.9 53.5 all-gather.39
  227.1 53.0 all-gather.41
  283.1 57.7 all-gather.33
  343.7 57.7 all-gather.31
  404.4 59.6 all-gather.35
  604.8 63.3 reduce-scatter.28
  670.3 53.3 reduce-scatter.30
  726.8 61.5 all-gather.43
  791.5 60.5 all-gather.45
  855.3 60.5 all-gather.47
  1318.8 78.8 reduce-scatter.40
  1401.2 53.2 reduce-scatter.36
  1460.2 94.5 reduce-scatter.66
  1557.7 115.7 reduce-scatter.64
  1773.7 117.4 reduce-scatter.48
  1893.8 130.7 reduce-scatter.52
  2027.5 132.5 reduce-scatter.50
  2163.0 132.8 reduce-scatter.56
  2302.8 127.8 reduce-scatter.44
  2436.9 113.4 reduce-scatter.54
  2557.6 113.4 reduce-scatter.46
  2673.8 131.1 reduce-scatter.58
  2807.7 144.4 reduce-scatter.60
  2955.1 145.0 reduce-scatter.62
  (14 shorter events, 415.5 us)
where the time goes:
time: 3140 us; the launch traced here: 3110 us
  waiting for transfers between devices  1910 us (61%)
  blocking collectives  396 us (13%)
  matrix products  396 us (13%)
  other arithmetic  187 us (6%)
  local copies, waits for them, and re-layouts  154 us (5%)
    reduce_scatter x1, waiting for transfers between devices, per_device(): lax.psum_scatter(totals[15], ('head', 'wide'), scatter_dimension=0, tiled...  148 us
    reduce_scatter x1, waiting for transfers between devices, per_device(): lax.psum_scatter(totals[14], ('head', 'wide'), scatter_dimension=0, tiled...  147 us
    reduce_scatter x1, waiting for transfers between devices, per_device(): lax.psum_scatter(place_into(totals[11], query_total, query_start, 0), ('h...  136 us
    reduce_scatter x1, waiting for transfers between devices, per_device(): lax.psum_scatter(place_into(totals[8], query_total, query_start, 1), ('he...  136 us
    unnamed x40, waiting for transfers between devices  135 us
    reduce_scatter x1, waiting for transfers between devices, per_device(): lax.psum_scatter(place_into(totals[1], inner_total, col_start, 1), ('head...  135 us
    reduce_scatter x1, waiting for transfers between devices, per_device(): lax.psum_scatter(totals[13], ('head', 'wide'), scatter_dimension=0, tiled...  134 us
    reduce_scatter x1, waiting for transfers between devices, per_device(): lax.psum_scatter(place_into(totals[9], kv_total, key_value_start, 1), ('h...  133 us
  transfers between devices with their start and end apart: 44, of which 25 were waited for; matrix products, arithmetic and copies ran while one was open for 18% of the time, Pallas kernels for 0%

commit v1 on v0

v1 whole, which is shorter than its diff:
```python
from functools import partial

import jax
import jax.numpy as jnp
from jax import lax
from jax.experimental import pallas as pl
from jax.experimental.pallas import tpu as pltpu
from jax.sharding import PartitionSpec as P

QUERY_HEADS = 8
KEY_VALUE_HEADS = 2
HEAD_SIZE = 64
GROUP = QUERY_HEADS // KEY_VALUE_HEADS
LANES = 128
LOW = jnp.bfloat16
FAR = -1e30
ALL = ("head", "wide")

epsilon = 1e-05
highest = lax.Precision.HIGHEST


def nn(left, right):
    return jnp.dot(left, right, preferred_element_type=jnp.float32)


def nt(left, right):
    return lax.dot_general(left, right, (((1,), (1,)), ((), ())), preferred_element_type=jnp.float32)


def tn(left, right):
    return lax.dot_general(left, right, (((0,), (0,)), ((), ())), preferred_element_type=jnp.float32)


def split_low(value, parts):
    terms = []
    for _ in range(parts):
        term = value.astype(LOW)
        terms.append(term)
        value = value - term.astype(jnp.float32)
    return terms


def shape(dims, kind=jnp.float32):
    return jax.ShapeDtypeStruct(dims, kind)


def shifted(value, axis, steps):
    count = lax.axis_size(axis)
    initial, last = (max(0, -steps), min(count, count - steps))
    return lax.ppermute(value, axis, [(source, source + steps) for source in range(initial, last)])


def swapped(value, axis, bit):
    count = lax.axis_size(axis)
    return lax.ppermute(value, axis, [(i, i ^ bit) for i in range(count)])


def pick(array, index, axis=0):
    return lax.dynamic_index_in_dim(array, index, axis, False)


def guess(us):
    return pl.CostEstimate(flops=int(us * 1e9), bytes_accessed=int(us * 3e6), transcendentals=0)


def gather_head(own, receivers, when=()):
    count = lax.axis_size("head")
    place = lax.axis_index("head")
    both = jnp.zeros((count,) + own.shape, own.dtype)
    both = lax.dynamic_update_index_in_dim(both, own, place, 0)
    for step in range(1, count):
        pairs = [(i, (i + step) % count) for i in range(count) if (i + step) % count < receivers]
        got = after(lax.ppermute(own, "head", pairs), *when)
        both = lax.dynamic_update_index_in_dim(both, got, (place - step) % count, 0)
    return both.reshape(-1, own.shape[1])


def after(value, *others):
    return lax.optimization_barrier((value,) + others)[0] if others else value


def to_blocks(pieces, when=()):
    count = lax.axis_size("head")
    place = lax.axis_index("head")
    micro_count = pieces.shape[0]

    def of(target):
        return pick(pieces, jnp.minimum(target, micro_count - 1))

    own = jnp.where(place < micro_count, of(place), jnp.zeros_like(pieces[0]))
    block = jnp.zeros((count,) + pieces.shape[1:], pieces.dtype)
    block = lax.dynamic_update_index_in_dim(block, own, place, 0)
    for step in range(1, count):
        pairs = [(i, (i + step) % count) for i in range(count) if (i + step) % count < micro_count]
        got = after(lax.ppermute(of((place + step) % count), "head", pairs), *when)
        block = lax.dynamic_update_index_in_dim(block, got, (place - step) % count, 0)
    return block.reshape(count * pieces.shape[1], pieces.shape[2])


def from_blocks(block, micro_count, when=()):
    count = lax.axis_size("head")
    place = lax.axis_index("head")
    parts = block.reshape(count, block.shape[0] // count, block.shape[1])
    pieces = jnp.zeros_like(parts)
    pieces = lax.dynamic_update_index_in_dim(pieces, pick(parts, place), place, 0)
    for step in range(1, count):
        pairs = [(i, (i + step) % count) for i in range(min(micro_count, count))]
        got = after(lax.ppermute(pick(parts, (place + step) % count), "head", pairs), *when)
        pieces = lax.dynamic_update_index_in_dim(pieces, got, (place - step) % count, 0)
    return pieces[:micro_count]


def sum_everywhere(value):
    for axis in ALL:
        step = 1
        while step < lax.axis_size(axis):
            value = value + swapped(value, axis, step)
            step *= 2
    return value


def wide_bits():
    bits = []
    while 1 << (len(bits) + 1) <= lax.axis_size("wide"):
        bits.append(1 << len(bits))
    return bits


class Gathered:
    def __init__(self, own):
        bits = wide_bits()
        half = own.shape[1] // 2
        self.parts = [own[:, :half], own[:, half:]]
        self.left = [bits[1:], bits[:0:-1]]
        self.done = [[], []]

    def step(self):
        place = lax.axis_index("wide")
        for i in range(2):
            bit = self.left[i].pop(0)
            array = self.parts[i]
            got = swapped(array, "wide", bit)
            mine = (place // bit) % 2
            self.parts[i] = jnp.where(mine == 0, jnp.stack([array, got]), jnp.stack([got, array]))
            self.done[i].insert(0, bit)

    def rest(self):
        while self.left[0]:
            self.step()
        arrays = []
        for array, done in zip(self.parts, self.done):
            ranks = [done.index(bit) for bit in sorted(done, reverse=True)]
            arrays.append(array.transpose(ranks + [len(done), len(done) + 1]))
        both = jnp.concatenate(arrays, axis=-1)
        got = swapped(both, "wide", 1)
        mine = lax.axis_index("wide") % 2
        stacked = jnp.where(mine == 0, jnp.stack([both, got], axis=-3), jnp.stack([got, both], axis=-3))
        return stacked.reshape(-1, both.shape[-1])


class Reduced:
    def __init__(self, array):
        self.bits = wide_bits()
        self.orders = [self.bits[1:], self.bits[:0:-1]]
        self.parts = [array.reshape((array.shape[0], -1, 2) + array.shape[2:])]
        self.axes = [[1]]
        self.steps = len(self.bits)

    def begin(self):
        self.moves = []
        for i, part in enumerate(self.parts):
            bit = 1 if len(self.parts) == 1 else self.orders[i].pop(0)
            axis = 2 if len(self.parts) == 1 else 1 + self.axes[i].index(bit)
            mine = (lax.axis_index("wide") // bit) % 2
            send = pick(part, 1 - mine, axis)
            self.moves.append((bit, pick(part, mine, axis), send, swapped(send, "wide", bit)))
        return [send for _, _, send, _ in self.moves]

    def end(self, *when):
        parts = []
        for bit, kept, _, got in self.moves:
            parts.append((kept.astype(jnp.float32) + after(got, *when).astype(jnp.float32)).astype(kept.dtype))
        if len(parts) == 1:
            half = parts[0].shape[0] // 2
            self.axes = [list(self.bits[:0:-1]) for _ in range(2)]
            parts = [
                part.reshape((half,) + (2,) * len(axes) + part.shape[2:])
                for part, axes in zip((parts[0][:half], parts[0][half:]), self.axes)
            ]
        else:
            for axes, (bit, _, _, _) in zip(self.axes, self.moves):
                axes.remove(bit)
        self.parts = parts
        self.steps -= 1

    def rest(self):
        while self.steps:
            self.begin()
            self.end()
        return jnp.concatenate(self.parts, axis=0)


def reduce_head(array, sources, when=()):
    count = lax.axis_size("head")
    place = lax.axis_index("head")
    total = jnp.where(place < sources, pick(array, place).astype(jnp.float32), 0.0)
    for step in range(1, count):
        pairs = [(i, (i + step) % count) for i in range(min(sources, count))]
        got = after(lax.ppermute(pick(array, (place + step) % count), "head", pairs), *when)
        total = total + got.astype(jnp.float32)
    return total


def sum_wide(array):
    return lax.psum_scatter(array, "wide", scatter_dimension=0, tiled=True)


def owned(part, sources, when=()):
    return reduce_head(part.reshape(lax.axis_size("head"), -1, part.shape[1]), sources, when)


class Carried:
    def __init__(self, sent, total, rows, backward):
        self.sent, self.total, self.rows = sent, total, rows
        self.state = jnp.zeros_like(total)
        self.backward = backward
        self.left = wide_bits()

    def step(self, *when):
        bit = self.left.pop(0)
        got = after(swapped(self.sent, "wide", bit), *when)
        mine = (lax.axis_index("wide") // bit) % 2
        ahead = 1 - mine if self.backward else mine
        self.total, self.state, self.rows, self.sent = join(
            self.total, self.state, self.rows, got, jnp.reshape(ahead, (1,)).astype(jnp.int32)
        )

    def rest(self, *when):
        while self.left:
            self.step(*when)
        return self.state


def rms_scale(values, scales):
    return values * lax.rsqrt(jnp.mean(values * values, axis=-1, keepdims=True) + epsilon) * scales


def doc_index(starts, positions):
    passed = (starts[None, :] <= positions[:, None]).astype(jnp.int32)
    return jnp.sum(passed, axis=1) - 1


def split_at(array, sizes, axis):
    out, at = [], 0
    for size in sizes:
        out.append(lax.slice_in_dim(array, at, at + size, axis=axis))
        at += size
    return out


def packed(parts, rows):
    flat = jnp.concatenate([part.reshape(-1) for part in parts])
    columns = -(-flat.shape[0] // rows)
    return jnp.pad(flat, (0, rows * columns - flat.shape[0])).reshape(rows, columns)


CHUNK = 128
EXTRA = 16


def spread(value, spread_ref):
    return nn(jnp.concatenate(split_low(value, 2), axis=1), spread_ref[...])


def gathered(value, gather_ref):
    return nn(value.astype(LOW), gather_ref[...])


def gathered_fine(value, gather_ref):
    high, rest = split_low(value, 2)
    return nn(high, gather_ref[...]) + nn(rest, gather_ref[...])


def with_decay(state, decay):
    terms = split_low(decay, 3) + [jnp.zeros((EXTRA - 3, decay.shape[1]), LOW)]
    return jnp.concatenate([state.astype(LOW)] + terms, axis=0)


def silu_parts(value):
    sigma = jax.nn.sigmoid(value)
    return value * sigma, sigma * (1.0 + value * (1.0 - sigma))


def local_kernel(
    x_ref, xp_ref, bc_ref, bcp_ref, rimx_ref, rimb_ref, dt_ref, marks_ref, tapx_ref, tapb_ref, bias_ref, rate_ref, spread_ref,
    act_ref, slope_ref, bcact_ref, bcslope_ref, step_ref, cum_ref, sent_ref, state_ref, decay_ref,
):
    part = pl.program_id(0)
    marks = marks_ref[...]

    def conv(raw_ref, prev_ref, rim_ref, tap_ref):
        before = jnp.where(part == 0, rim_ref[...], prev_ref[...])
        both = jnp.concatenate([before, raw_ref[...]], axis=0)
        taps = 4
        total = None
        for i in range(taps):
            term = both[8 - taps + 1 + i : 8 - taps + 1 + i + CHUNK] * tap_ref[i : i + 1, :] * marks[:, i : i + 1]
            total = term if total is None else total + term
        return silu_parts(total)

    act, slope = conv(x_ref, xp_ref, rimx_ref, tapx_ref)
    act_ref[...] = act
    slope_ref[...] = slope.astype(LOW)
    bc, bc_slope = conv(bc_ref, bcp_ref, rimb_ref, tapb_ref)
    bcact_ref[...] = bc.astype(LOW)
    bcslope_ref[...] = bc_slope.astype(LOW)
    lane = lax.broadcasted_iota(jnp.int32, (CHUNK, LANES), 1)
    value = dt_ref[...] + bias_ref[0:1, :]
    softplus = jnp.maximum(value, 0.0) + jnp.log1p(jnp.exp(-jnp.abs(value)))
    step = jnp.where(rate_ref[0:1, :] < 0.0, softplus, 0.0)
    row = lax.broadcasted_iota(jnp.int32, (CHUNK, CHUNK), 0)
    col = lax.broadcasted_iota(jnp.int32, (CHUNK, CHUNK), 1)
    cum = jnp.dot((col <= row).astype(jnp.float32), step * rate_ref[0:1, :], precision=highest, preferred_element_type=jnp.float32)
    step_ref[...] = step
    cum_ref[...] = cum
    tail = jnp.exp(cum[CHUNK - 1 :] - cum) * marks[:, 5:6] * step
    weighted = (act * spread(tail, spread_ref)).astype(LOW)
    decay = spread(jnp.exp(cum[CHUNK - 8 :]) * marks[CHUNK - 8 :, 7:8], spread_ref)[7:8]
    own = tn(bc[:, :LANES].astype(LOW), weighted)

    @pl.when(part == 0)
    def _():
        state_ref[...] = own
        decay_ref[...] = jnp.ones_like(decay_ref)
        decay_ref[0:1, :] = decay

    @pl.when(part > 0)
    def _():
        state_ref[...] = state_ref[...] * decay + own
        decay_ref[0:1, :] = decay_ref[0:1, :] * decay

    @pl.when(part == pl.num_programs(0) - 1)
    def _():
        sent_ref[...] = with_decay(state_ref[...], decay_ref[0:1, :])


def join_kernel(ahead_ref, total_ref, state_ref, rows_ref, got_ref, total_out, state_out, rows_out, sent_out):
    size = total_ref.shape[0]
    got = got_ref[:size, :].astype(jnp.float32)
    extra = got_ref[size:, :].astype(jnp.float32)
    got_decay = extra[0:1] + extra[1:2] + extra[2:3]
    decay, sweep = rows_ref[0:1, :], rows_ref[1:2, :]
    rows_out[...] = jnp.ones_like(rows_out)
    rows_out[0:1, :] = decay * got_decay

    @pl.when(ahead_ref[0] == 1)
    def _():
        state_out[...] = state_ref[...] + sweep * got
        rows_out[1:2, :] = sweep * got_decay
        total_out[...] = total_ref[...] + decay * got

    @pl.when(ahead_ref[0] == 0)
    def _():
        state_out[...] = state_ref[...]
        rows_out[1:2, :] = sweep
        total_out[...] = got + got_decay * total_ref[...]

    sent_out[...] = with_decay(total_out[...], decay * got_decay)


def mix_kernel(
    act_ref, bcact_ref, z_ref, step_ref, cum_ref, marks_ref, docs_ref, first_ref, skip_ref, gain_ref, spread_ref, gather_ref,
    ym_ref, y_ref, entry_ref, state_ref, inner_ref,
):
    part = pl.program_id(0)

    @pl.when(part == 0)
    def _():
        state_ref[...] = first_ref[...]

    marks = marks_ref[...]
    cum = cum_ref[...]
    cum_rows = cum.T
    step = step_ref[...]
    b_mat = bcact_ref[:, :LANES]
    c_mat = bcact_ref[:, LANES:]
    act = act_ref[...]
    stepped = act * spread(step, spread_ref)
    low_stepped = stepped.astype(LOW)
    row = lax.broadcasted_iota(jnp.int32, (CHUNK, CHUNK), 0)
    col = lax.broadcasted_iota(jnp.int32, (CHUNK, CHUNK), 1)
    allowed = (row >= col) & (marks[:, 6:7] == docs_ref[0:1, :])
    gram = jnp.where(allowed, nt(c_mat, b_mat), 0.0)
    first = lax.broadcasted_iota(jnp.int32, (CHUNK, LANES), 1) < LANES // 2
    pairs = act.shape[1] // LANES
    for pair in range(pairs):
        parts = []
        for head in (2 * pair, 2 * pair + 1):
            gaps = jnp.minimum(cum[:, head : head + 1] - cum_rows[head : head + 1, :], 0.0)
            parts.append((jnp.exp(gaps) * gram).astype(LOW))
        values = low_stepped[:, pair * LANES : (pair + 1) * LANES]
        zero = jnp.zeros_like(values)
        inner_ref[:, pair * LANES : (pair + 1) * LANES] = nn(
            jnp.concatenate(parts, axis=1),
            jnp.concatenate([jnp.where(first, values, zero), jnp.where(first, zero, values)], axis=0),
        )
    state = state_ref[...]
    low_state = state.astype(LOW)
    entry_ref[0] = low_state
    entering = spread(jnp.exp(cum) * marks[:, 4:5], spread_ref)
    y = inner_ref[...] + nn(c_mat, low_state) * entering + skip_ref[0:1, :] * act
    y_ref[...] = y
    gated = y * silu_parts(z_ref[...])[0]
    scale = lax.rsqrt(gathered(gated * gated, gather_ref) * (2.0 / LANES) + epsilon)
    ym_ref[...] = (gated * spread(scale, spread_ref) * gain_ref[0:1, :]).astype(LOW)
    tail = jnp.exp(cum[CHUNK - 1 :] - cum) * marks[:, 5:6]
    weighted = (stepped * spread(tail, spread_ref)).astype(LOW)
    decay = spread(jnp.exp(cum[CHUNK - 8 :]) * marks[CHUNK - 8 :, 7:8], spread_ref)[7:8]
    state_ref[...] = state * decay + tn(b_mat, weighted)


def gate_back_kernel(
    dym_ref, y_ref, z_ref, bcact_ref, cum_ref, marks_ref, gain_ref, spread_ref, gather_ref,
    dz_ref, dy_ref, dgain_ref, sent_ref, state_ref, decay_ref,
):
    part = pl.program_id(0)
    marks = marks_ref[...]
    cum = cum_ref[...]
    y = y_ref[...]
    silu, slope = silu_parts(z_ref[...])
    gated = y * silu
    scale = lax.rsqrt(gathered(gated * gated, gather_ref) * (2.0 / LANES) + epsilon)
    wide_scale = spread(scale, spread_ref)
    d_normed = dym_ref[...]
    d_gain = jnp.sum(d_normed * gated * wide_scale, axis=0, keepdims=True)
    u = d_normed * gain_ref[0:1, :]
    inner = gathered(u * gated, gather_ref) * (2.0 / LANES) * scale * scale * scale
    d_gated = u * wide_scale - gated * spread(inner, spread_ref)
    dz_ref[...] = (d_gated * y * slope).astype(LOW)
    dy = d_gated * silu
    dy_ref[...] = dy
    entering = spread(jnp.exp(cum) * marks[:, 4:5], spread_ref)
    own = tn(bcact_ref[:, LANES:], (dy * entering).astype(LOW))
    decay = spread(jnp.exp(cum[CHUNK - 8 :]) * marks[CHUNK - 8 :, 7:8], spread_ref)[7:8]

    @pl.when(part == 0)
    def _():
        state_ref[...] = own
        decay_ref[...] = jnp.ones_like(decay_ref)
        decay_ref[0:1, :] = decay
        dgain_ref[0:1, :] = d_gain

    @pl.when(part > 0)
    def _():
        state_ref[...] = state_ref[...] * decay + own
        decay_ref[0:1, :] = decay_ref[0:1, :] * decay
        dgain_ref[0:1, :] += d_gain

    @pl.when(part == pl.num_programs(0) - 1)
    def _():
        sent_ref[...] = with_decay(state_ref[...], decay_ref[0:1, :])


def scan_back_kernel(
    act_ref, slope_ref, bcact_ref, bcslope_ref, dt_ref, step_ref, cum_ref, marks_ref, docs_ref, dy_ref, entry_ref, first_ref,
    skip_ref, bias_ref, rate_ref, spread_ref, gather_ref, x_ref, xp_ref, bc_ref, bcp_ref, rimx_ref, rimb_ref, tapx_ref, tapb_ref,
    dscan_ref, dskip_ref, dhead_ref, dtap_ref, rim_ref, edge_ref, state_ref, inner_ref, rows_ref, next_ref, nextm_ref,
):
    part = pl.program_id(0)

    @pl.when(part == 0)
    def _():
        state_ref[...] = first_ref[...]
        rows_ref[...] = jnp.zeros_like(rows_ref)
        dskip_ref[...] = jnp.zeros_like(dskip_ref)
        dhead_ref[...] = jnp.zeros_like(dhead_ref)
        dtap_ref[...] = jnp.zeros_like(dtap_ref)
        next_ref[...] = jnp.zeros_like(next_ref)
        nextm_ref[...] = jnp.zeros_like(nextm_ref)

    marks = marks_ref[...]
    cum = cum_ref[...]
    cum_rows = cum.T
    step = step_ref[...]
    b_mat = bcact_ref[:, :LANES]
    c_mat = bcact_ref[:, LANES:]
    act = act_ref[...]
    wide_step = spread(step, spread_ref)
    stepped = act * wide_step
    low_stepped = stepped.astype(LOW)
    dy = dy_ref[...]
    low_dy = dy.astype(LOW)
    row = lax.broadcasted_iota(jnp.int32, (CHUNK, CHUNK), 0)
    col = lax.broadcasted_iota(jnp.int32, (CHUNK, CHUNK), 1)
    allowed = (row <= col) & (marks[:, 6:7] == docs_ref[0:1, :])
    gram = jnp.where(allowed, nt(b_mat, c_mat), 0.0)
    first = lax.broadcasted_iota(jnp.int32, (CHUNK, LANES), 1) < LANES // 2
    lane = lax.broadcasted_iota(jnp.int32, (CHUNK, LANES), 1)
    pairs = act.shape[1] // LANES
    d_gram = jnp.zeros((CHUNK, CHUNK), jnp.float32)
    leaving = jnp.zeros((CHUNK, LANES), jnp.float32)
    for pair in range(pairs):
        cols = slice(pair * LANES, (pair + 1) * LANES)
        values, grads = low_stepped[:, cols], low_dy[:, cols]
        zero = jnp.zeros_like(values)
        d_weights = nt(jnp.concatenate([jnp.where(first, values, zero), jnp.where(first, zero, values)], axis=0), grads)
        parts = []
        for i, head in enumerate((2 * pair, 2 * pair + 1)):
            fade = jnp.exp(jnp.minimum(cum_rows[head : head + 1, :] - cum[:, head : head + 1], 0.0))
            d_weight = d_weights[i * CHUNK : (i + 1) * CHUNK]
            weight = fade * gram
            d_gram = d_gram + d_weight * fade
            moved = d_weight * weight
            rows_ref[head : head + 1, :] = jnp.sum(moved, axis=0, keepdims=True)
            leaving = jnp.where(lane == head, jnp.sum(moved, axis=1, keepdims=True), leaving)
            parts.append(weight.astype(LOW))
        inner_ref[:, cols] = nn(
            jnp.concatenate(parts, axis=1),
            jnp.concatenate([jnp.where(first, grads, zero), jnp.where(first, zero, grads)], axis=0),
        )
    d_state = state_ref[...]
    low_d_state = d_state.astype(LOW)
    entry = entry_ref[0]
    entering = spread(jnp.exp(cum) * marks[:, 4:5], spread_ref)
    tail = spread(jnp.exp(cum[CHUNK - 1 :] - cum) * marks[:, 5:6], spread_ref)
    from_state = nn(b_mat, low_d_state) * tail
    d_stepped = inner_ref[...] + from_state
    out_moved = gathered_fine(stepped * from_state, gather_ref)
    entering_dy = dy * entering
    in_moved = gathered_fine(entering_dy * nn(c_mat, entry), gather_ref)
    low_entering_dy = entering_dy.astype(LOW)
    low_gram = jnp.where(allowed, d_gram, 0.0).astype(LOW)
    d_b = nt((stepped * tail).astype(LOW), low_d_state) + nn(low_gram, c_mat)
    d_c = nt(low_entering_dy, entry) + tn(low_gram, b_mat)
    decay_small = jnp.exp(cum[CHUNK - 8 :]) * marks[CHUNK - 8 :, 7:8]
    decay = spread(decay_small, spread_ref)[7:8]
    overlap = jnp.sum(d_state * entry.astype(jnp.float32), axis=0, keepdims=True)
    d_decay = nn(jnp.concatenate(split_low(jnp.broadcast_to(overlap, (8, overlap.shape[1])), 2), axis=0), gather_ref[...])
    at_end = jnp.sum(out_moved, axis=0, keepdims=True) + (d_decay[0:1] + d_decay[8:9]) * decay_small[7:8]
    d_cum = rows_ref[...].T - leaving + in_moved - out_moved
    d_cum = d_cum + jnp.where(lax.broadcasted_iota(jnp.int32, d_cum.shape, 0) == CHUNK - 1, at_end, 0.0)
    d_log = jnp.dot((row <= col).astype(jnp.float32), d_cum, precision=highest, preferred_element_type=jnp.float32)
    rate = rate_ref[0:1, :]
    d_step = gathered_fine(act * d_stepped, gather_ref) + d_log * rate
    d_dt = d_step * jax.nn.sigmoid(dt_ref[...] + bias_ref[0:1, :])
    d_dt = jnp.where(rate < 0.0, d_dt, 0.0)
    inner = act.shape[1]
    scan = inner + 2 * LANES
    dscan_ref[:, scan:] = d_dt.astype(LOW)
    dhead_ref[0:1, :] += jnp.sum(d_dt, axis=0, keepdims=True)
    dhead_ref[1:2, :] += jnp.sum(d_log * rate * step, axis=0, keepdims=True)
    dskip_ref[0:1, :] += jnp.sum(dy * act, axis=0, keepdims=True)
    taps = 4
    marks_ext = jnp.concatenate([marks, nextm_ref[...]], axis=0)

    def conv_back(d_pre, lanes, raw_ref, prev_ref, edge_raw_ref, tap_ref):
        before = jnp.where(part == pl.num_programs(0) - 1, edge_raw_ref[...], prev_ref[...])
        raw = jnp.concatenate([before, raw_ref[...]], axis=0)
        ext = jnp.concatenate([d_pre, next_ref[:, lanes]], axis=0)
        top = jnp.concatenate([jnp.zeros_like(ext[:8]), d_pre[:8]], axis=0)
        top_marks = jnp.concatenate([marks[:8], marks[:8]], axis=0)
        d_raw, rim = None, None
        for i in range(taps):
            ahead = taps - 1 - i
            tap = tap_ref[i : i + 1, :]
            masked = d_pre * marks[:, i : i + 1]
            dtap_ref[i : i + 1, lanes] += jnp.sum(masked * raw[8 - ahead : 8 - ahead + CHUNK], axis=0, keepdims=True)
            term = (ext * marks_ext[:, i : i + 1])[ahead : ahead + CHUNK] * tap
            d_raw = term if d_raw is None else d_raw + term
            if ahead:
                term = (top * top_marks[:, i : i + 1])[ahead : ahead + 8] * tap
                rim = term if rim is None else rim + term
        next_ref[:, lanes] = d_pre[:8]
        dscan_ref[:, lanes] = d_raw.astype(LOW)
        rim_ref[:, lanes] = rim

        @pl.when(part == 0)
        def _():
            edge_ref[:, lanes] = d_raw[CHUNK - 8 :]

    conv_back(
        (d_stepped * wide_step + dy * skip_ref[0:1, :]) * slope_ref[...].astype(jnp.float32),
        slice(0, inner), x_ref, xp_ref, rimx_ref, tapx_ref,
    )
    conv_back(
        jnp.concatenate([d_b, d_c], axis=1) * bcslope_ref[...].astype(jnp.float32),
        slice(inner, scan), bc_ref, bcp_ref, rimb_ref, tapb_ref,
    )
    nextm_ref[...] = marks[:8]
    state_ref[...] = d_state * decay + tn(c_mat, low_entering_dy)


def head_matrices(inner, heads):
    owner = jnp.arange(inner, dtype=jnp.int32) // (inner // heads)
    gather_m = (owner[:, None] == jnp.arange(LANES, dtype=jnp.int32)[None, :]).astype(LOW)
    return jnp.concatenate([gather_m.T, gather_m.T], axis=0), gather_m


def lanes_row(vector):
    return jnp.pad(vector, (0, LANES - vector.shape[0]))[None, :]


def call(kernel, name, us, parts, ins, outs, scratch, reverse=False):
    def spec(block, how):
        if how == "part":
            how = lambda c: (c,) + (0,) * (len(block) - 1)
        elif how == "whole":
            how = lambda c: (0,) * len(block)
        elif isinstance(how, int):
            column = how
            how = lambda c: (c, column)

        def index(c):
            return how(parts - 1 - c if reverse else c)

        return pl.BlockSpec(block, index)

    return pl.pallas_call(
        kernel,
        grid=(parts,),
        in_specs=[spec(block, how) for _, block, how in ins],
        out_specs=[spec(block, how) for _, block, how in outs],
        scratch_shapes=scratch,
        out_shape=[shape for shape, _, _ in outs],
        compiler_params=pltpu.CompilerParams(vmem_limit_bytes=56 * 2**20),
        cost_estimate=guess(us),
        name=name,
    )(*[array for array, _, _ in ins])


def mamba_local(raw, rim, marks, taps, bias, rate, cols, mats):
    length = raw.shape[0]
    parts = length // CHUNK
    inner, n2, x_at, bc_at, dt_at = cols
    before = CHUNK // 8

    def prev(column):
        return lambda c: (jnp.maximum(c * before - 1, 0), column)

    return call(
        local_kernel,
        "mamba_local",
        11,
        parts,
        [
            (raw, (CHUNK, inner), x_at),
            (raw, (8, inner), prev(x_at)),
            (raw, (CHUNK, n2), bc_at),
            (raw, (8, n2), prev(bc_at)),
            (rim[:, :inner], (8, inner), "whole"),
            (rim[:, inner:], (8, n2), "whole"),
            (raw, (CHUNK, LANES), dt_at),
            (marks, (CHUNK, LANES), "part"),
            (taps[:, :inner], (8, inner), "whole"),
            (taps[:, inner:], (8, n2), "whole"),
            (bias, (1, LANES), "whole"),
            (rate, (1, LANES), "whole"),
            (mats[0], mats[0].shape, "whole"),
        ],
        [
            (shape((length, inner)), (CHUNK, inner), "part"),
            (shape((length, inner), LOW), (CHUNK, inner), "part"),
            (shape((length, n2), LOW), (CHUNK, n2), "part"),
            (shape((length, n2), LOW), (CHUNK, n2), "part"),
            (shape((length, LANES)), (CHUNK, LANES), "part"),
            (shape((length, LANES)), (CHUNK, LANES), "part"),
            (shape((n2 // 2 + EXTRA, inner), LOW), (n2 // 2 + EXTRA, inner), "whole"),
            (shape((n2 // 2, inner)), (n2 // 2, inner), "whole"),
            (shape((8, inner)), (8, inner), "whole"),
        ],
        [],
    )


def mamba_mix(feats, raw, marks, docs, state, skip, gain, mats):
    act, slope, bcact, bcslope, step, cum = feats
    length, inner = act.shape
    parts = length // CHUNK
    n2 = bcact.shape[1]
    return call(
        mix_kernel,
        "mamba_mix",
        11,
        parts,
        [
            (act, (CHUNK, inner), "part"),
            (bcact, (CHUNK, n2), "part"),
            (raw, (CHUNK, inner), 0),
            (step, (CHUNK, LANES), "part"),
            (cum, (CHUNK, LANES), "part"),
            (marks, (CHUNK, LANES), "part"),
            (docs, (8, CHUNK), lambda c: (0, c)),
            (state, state.shape, "whole"),
            (skip, (1, inner), "whole"),
            (gain, (1, inner), "whole"),
            (mats[0], mats[0].shape, "whole"),
            (mats[1], mats[1].shape, "whole"),
        ],
        [
            (shape((length, inner), LOW), (CHUNK, inner), "part"),
            (shape((length, inner)), (CHUNK, inner), "part"),
            (shape((parts, n2 // 2, inner), LOW), (1, n2 // 2, inner), "part"),
        ],
        [pltpu.VMEM((n2 // 2, inner), jnp.float32), pltpu.VMEM((CHUNK, inner), jnp.float32)],
    )


def mamba_gate_back(d_normed, y, raw, feats, marks, gain, mats):
    act, slope, bcact, bcslope, step, cum = feats
    length, inner = act.shape
    parts = length // CHUNK
    n2 = bcact.shape[1]
    return call(
        gate_back_kernel,
        "mamba_gate_back",
        11,
        parts,
        [
            (d_normed, (CHUNK, inner), "part"),
            (y, (CHUNK, inner), "part"),
            (raw, (CHUNK, inner), 0),
            (bcact, (CHUNK, n2), "part"),
            (cum, (CHUNK, LANES), "part"),
            (marks, (CHUNK, LANES), "part"),
            (gain, (1, inner), "whole"),
            (mats[0], mats[0].shape, "whole"),
            (mats[1], mats[1].shape, "whole"),
        ],
        [
            (shape((length, inner), LOW), (CHUNK, inner), "part"),
            (shape((length, inner)), (CHUNK, inner), "part"),
            (shape((8, inner)), (8, inner), "whole"),
            (shape((n2 // 2 + EXTRA, inner), LOW), (n2 // 2 + EXTRA, inner), "whole"),
            (shape((n2 // 2, inner)), (n2 // 2, inner), "whole"),
            (shape((8, inner)), (8, inner), "whole"),
        ],
        [],
        reverse=True,
    )


def mamba_scan_back(feats, raw, rim, taps, marks, docs, dy, entry, state, skip, bias, rate, cols, mats):
    act, slope, bcact, bcslope, step, cum = feats
    length, inner = act.shape
    parts = length // CHUNK
    n2 = bcact.shape[1]
    x_at, bc_at, dt_at = cols[2:]
    scan = inner + n2

    def prev(column):
        return lambda c: (jnp.maximum(c * (CHUNK // 8) - 1, 0), column)

    return call(
        scan_back_kernel,
        "mamba_scan_back",
        23,
        parts,
        [
            (act, (CHUNK, inner), "part"),
            (slope, (CHUNK, inner), "part"),
            (bcact, (CHUNK, n2), "part"),
            (bcslope, (CHUNK, n2), "part"),
            (raw, (CHUNK, LANES), dt_at),
            (step, (CHUNK, LANES), "part"),
            (cum, (CHUNK, LANES), "part"),
            (marks, (CHUNK, LANES), "part"),
            (docs, (8, CHUNK), lambda c: (0, c)),
            (dy, (CHUNK, inner), "part"),
            (entry, (1, n2 // 2, inner), "part"),
            (state, state.shape, "whole"),
            (skip, (1, inner), "whole"),
            (bias, (1, LANES), "whole"),
            (rate, (1, LANES), "whole"),
            (mats[0], mats[0].shape, "whole"),
            (mats[1], mats[1].shape, "whole"),
            (raw, (CHUNK, inner), x_at),
            (raw, (8, inner), prev(x_at)),
            (raw, (CHUNK, n2), bc_at),
            (raw, (8, n2), prev(bc_at)),
            (rim[:, :inner], (8, inner), "whole"),
            (rim[:, inner:], (8, n2), "whole"),
            (taps[:, :inner], (8, inner), "whole"),
            (taps[:, inner:], (8, n2), "whole"),
        ],
        [
            (shape((length, scan + LANES), LOW), (CHUNK, scan + LANES), "part"),
            (shape((8, inner)), (8, inner), "whole"),
            (shape((8, LANES)), (8, LANES), "whole"),
            (shape((8, scan)), (8, scan), "whole"),
            (shape((8, scan)), (8, scan), "whole"),
            (shape((8, scan)), (8, scan), "whole"),
        ],
        [
            pltpu.VMEM((n2 // 2, inner), jnp.float32),
            pltpu.VMEM((CHUNK, inner), jnp.float32),
            pltpu.VMEM((LANES, CHUNK), jnp.float32),
            pltpu.VMEM((8, scan), jnp.float32),
            pltpu.VMEM((8, LANES), jnp.float32),
        ],
        reverse=True,
    )


def join(total, state, rows, got, ahead):
    whole = pl.BlockSpec(memory_space=pltpu.VMEM)
    return pl.pallas_call(
        join_kernel,
        in_specs=[pl.BlockSpec(memory_space=pltpu.SMEM)] + [whole] * 4,
        out_specs=[whole] * 4,
        out_shape=[shape(total.shape), shape(total.shape), shape(rows.shape), shape(got.shape, LOW)],
        compiler_params=pltpu.CompilerParams(vmem_limit_bytes=32 * 2**20),
        cost_estimate=guess(2),
        name="join",
    )(ahead, total, state, rows, got)


BOTH = 2
ONES = 16


def causal(scores):
    key_row = lax.broadcasted_iota(jnp.int32, scores.shape, 0)
    query = lax.broadcasted_iota(jnp.int32, scores.shape, 1)
    return jnp.where(key_row <= query, scores, FAR)


def attend_kernel(place_ref, q_ref, far_ref, kv_ref, extra_ref, o_ref, qb_ref, keys_ref, values_ref, acc_ref):
    blk = q_ref.shape[2]
    last = place_ref[0]

    @pl.when(pl.program_id(0) == 0)
    def _():
        first = lax.broadcasted_iota(jnp.int32, (blk, LANES), 1) < HEAD_SIZE

        @pl.loop(0, last + 1)
        def _(block):
            rows = pl.ds(pl.multiple_of(block * blk, blk), blk)
            both = kv_ref[rows, :]
            keys_ref[rows, :] = jnp.where(first, both, extra_ref[rows, :])
            values_ref[:ONES, rows] = jnp.ones((ONES, blk), LOW)
            values_ref[ONES:, rows] = both.astype(jnp.float32).T[HEAD_SIZE:].astype(LOW)

    queries = [
        jnp.concatenate([q_ref[i] * jnp.asarray(HEAD_SIZE ** (-0.5), LOW), far_ref[...]], axis=0)
        for i in range(BOTH)
    ]
    acc_ref[...] = jnp.zeros_like(acc_ref)

    def step(block, tops, diagonal):
        rows = pl.ds(pl.multiple_of(block * blk, blk), blk)
        keys, values = keys_ref[rows, :], values_ref[:, rows]
        new_tops = []
        for i in range(BOTH):
            scores = nn(keys, queries[i])
            if diagonal:
                scores = causal(scores)
            new_top = jnp.maximum(tops[i], jnp.max(scores, axis=0, keepdims=True))
            probs = jnp.exp(scores - new_top).astype(LOW)
            acc_ref[i] = acc_ref[i] * jnp.exp(tops[i] - new_top) + nn(values, probs)
            new_tops.append(new_top)
        return tuple(new_tops)

    tops = (jnp.full((1, blk), FAR, jnp.float32),) * BOTH
    tops = lax.fori_loop(0, last, lambda block, tops: step(block, tops, False), tops)
    tops = step(last, tops, True)
    row = lax.broadcasted_iota(jnp.int32, (HEAD_SIZE, blk), 0)
    for i in range(BOTH):
        total = acc_ref[i, 0:1, :]
        o_ref[i] = acc_ref[i, ONES:, :] / total
        extra = far_ref[...].astype(jnp.float32)
        for at, term in enumerate(split_low(-(tops[i] + jnp.log(total)), 3)):
            extra = jnp.where(row == 4 + at, term.astype(jnp.float32), extra)
        qb_ref[i] = jnp.concatenate([queries[i][:HEAD_SIZE], extra.astype(LOW)], axis=0)


def attend_back_kernel(place_ref, qb_ref, dot_ref, o_ref, kv_ref, extra_ref, dq_ref, dkv_ref, keys_ref, rows_ref, values_ref, acc_ref, dqa_ref):
    blk = qb_ref.shape[2]
    last = place_ref[0]
    member = pl.program_id(0)

    @pl.when(member == 0)
    def _():
        acc_ref[...] = jnp.zeros_like(acc_ref)
        lane = lax.broadcasted_iota(jnp.int32, (blk, LANES), 1)
        ones = jnp.where(lane < 3, 1.0, 0.0).astype(LOW)

        @pl.loop(0, last + 1)
        def _(block):
            rows = pl.ds(pl.multiple_of(block * blk, blk), blk)
            both = kv_ref[rows, :]
            keys_ref[rows, :] = jnp.where(lane < HEAD_SIZE, both, extra_ref[rows, :])
            values_ref[rows, :] = jnp.where(lane < HEAD_SIZE, ones, both)
            rows_ref[:, rows] = both.astype(jnp.float32).T[:HEAD_SIZE].astype(LOW)

    row = lax.broadcasted_iota(jnp.int32, (HEAD_SIZE, blk), 0)
    none = jnp.zeros((HEAD_SIZE, blk), jnp.float32)
    queries, d_outs, pairs = [], [], []
    for i in range(BOTH):
        queries.append(qb_ref[i])
        d_out = dot_ref[i].astype(jnp.float32)
        row_dot = jnp.sum(d_out * o_ref[i], axis=0, keepdims=True)
        extra = none
        for at, term in enumerate(split_low(-row_dot, 3)):
            extra = jnp.where(row == at, term.astype(jnp.float32), extra)
        d_outs.append(jnp.concatenate([extra, d_out], axis=0).astype(LOW))
        q_part = jnp.concatenate([qb_ref[i, :HEAD_SIZE, :].astype(jnp.float32), none], axis=0)
        pairs.append(jnp.concatenate([q_part.T, jnp.concatenate([none, d_out], axis=0).T], axis=0).astype(LOW))
    dqa_ref[...] = jnp.zeros_like(dqa_ref)

    def step(block, diagonal):
        rows = pl.ds(pl.multiple_of(block * blk, blk), blk)
        keys, values, key_rows = keys_ref[rows, :], values_ref[rows, :], rows_ref[:, rows]
        total = acc_ref[rows, :]
        for i in range(BOTH):
            logs = nn(keys, queries[i])
            if diagonal:
                logs = causal(logs)
            probs = jnp.exp(logs)
            d_scores = (probs * nn(values, d_outs[i])).astype(LOW)
            total = total + nn(jnp.concatenate([d_scores, probs.astype(LOW)], axis=1), pairs[i])
            dqa_ref[i] += nn(key_rows, d_scores)
        acc_ref[rows, :] = total

    @pl.loop(0, last)
    def _(block):
        step(block, False)

    step(last, True)
    dq_ref[...] = (dqa_ref[...] * HEAD_SIZE ** (-0.5)).astype(LOW)

    @pl.when(member == GROUP // BOTH - 1)
    def _():
        dkv_ref[...] = acc_ref[...].astype(LOW)


def attend_back_more(place_ref, qb_ref, dot_ref, o_ref, kv_ref, extra_ref, _, *refs):
    attend_back_kernel(place_ref, qb_ref, dot_ref, o_ref, kv_ref, extra_ref, *refs)


def attend_specs(blk, total, group):
    mine = group * (GROUP // BOTH)
    return dict(
        narrow=pl.BlockSpec((BOTH, HEAD_SIZE, blk), lambda r, p: (mine + r, 0, 0)),
        own_narrow=pl.BlockSpec((BOTH, HEAD_SIZE, blk), lambda r, p: (r, 0, 0)),
        own_broad=pl.BlockSpec((BOTH, LANES, blk), lambda r, p: (r, 0, 0)),
        kv=pl.BlockSpec((total, LANES), lambda r, p: (0, group)),
        extra=pl.BlockSpec((total, LANES), lambda r, p: (0, 0)),
        far=pl.BlockSpec((HEAD_SIZE, blk), lambda r, p: (0, 0)),
    )


def attend_masks(doc_here, key_doc, doc_count):
    docs = jnp.arange(HEAD_SIZE, dtype=jnp.int32)
    far = jnp.where((docs[:, None] != doc_here[None, :]) & (docs[:, None] < doc_count), FAR, 0.0).astype(LOW)
    lane = jnp.arange(LANES, dtype=jnp.int32)[None, :] - HEAD_SIZE
    extra = ((key_doc[:, None] == lane) | ((lane >= doc_count) & (lane < doc_count + 3))).astype(LOW)
    return far, extra


def attend(group, q_rows, key_all, masks, place):
    blk = q_rows.shape[2]
    total = key_all.shape[0]
    specs = attend_specs(blk, total, group)
    return pl.pallas_call(
        attend_kernel,
        grid_spec=pltpu.PrefetchScalarGridSpec(
            num_scalar_prefetch=1,
            grid=(GROUP // BOTH,),
            in_specs=[specs["narrow"], specs["far"], specs["kv"], specs["extra"]],
            out_specs=[specs["own_narrow"], specs["own_broad"]],
            scratch_shapes=[
                pltpu.VMEM((total, LANES), LOW),
                pltpu.VMEM((HEAD_SIZE + ONES, total), LOW),
                pltpu.VMEM((BOTH, HEAD_SIZE + ONES, blk), jnp.float32),
            ],
        ),
        out_shape=[shape((GROUP, HEAD_SIZE, blk)), shape((GROUP, LANES, blk), LOW)],
        compiler_params=pltpu.CompilerParams(vmem_limit_bytes=56 * 2**20),
        cost_estimate=guess(17),
        name="attend",
    )(place, q_rows, masks[0], key_all, masks[1])


def attend_back(group, q_back, out, d_rows, key_all, masks, place, d_kv=None):
    blk = d_rows.shape[2]
    total = key_all.shape[0]
    specs = attend_specs(blk, total, group)
    more = [] if d_kv is None else [d_kv]
    return pl.pallas_call(
        attend_back_kernel if d_kv is None else attend_back_more,
        grid_spec=pltpu.PrefetchScalarGridSpec(
            num_scalar_prefetch=1,
            grid=(GROUP // BOTH,),
            in_specs=[specs["own_broad"], specs["narrow"], specs["own_narrow"], specs["kv"], specs["extra"]]
            + [pl.BlockSpec(memory_space=pl.ANY)] * len(more),
            out_specs=[specs["own_narrow"], specs["kv"]],
            scratch_shapes=[
                pltpu.VMEM((total, LANES), LOW),
                pltpu.VMEM((HEAD_SIZE, total), LOW),
                pltpu.VMEM((total, LANES), LOW),
                pltpu.VMEM((total, LANES), jnp.float32),
                pltpu.VMEM((BOTH, HEAD_SIZE, blk), jnp.float32),
            ],
        ),
        out_shape=[shape((GROUP, HEAD_SIZE, blk), LOW), shape((total, key_all.shape[1]), LOW)],
        input_output_aliases={6: 1} if more else {},
        compiler_params=pltpu.CompilerParams(vmem_limit_bytes=60 * 2**20),
        cost_estimate=guess(27),
        name="attend_back",
    )(place, q_back, d_rows, out, key_all, masks[1], *more)


PIECE = 256


def feed_kernel(x_ref, gy_ref, plain_ref, w_ref, out_ref, dx_ref, grad_ref, xt_ref):
    fold = w_ref.shape[1] // 3

    @pl.when(pl.program_id(0) == 0)
    def _():
        out_ref[...] = jnp.zeros_like(out_ref)
        dx_ref[...] = jnp.zeros_like(dx_ref)
        xt_ref[...] = x_ref[...].astype(jnp.float32).T.astype(LOW)

    @pl.loop(0, fold // PIECE)
    def _(piece):
        at = pl.multiple_of(piece * PIECE, PIECE)
        gate_cols = pl.ds(at, PIECE)
        up_cols = pl.ds(pl.multiple_of(fold + at, PIECE), PIECE)
        down_cols = pl.ds(2 * fold, fold)
        w_gate, w_up, w_down = w_ref[:, gate_cols], w_ref[:, up_cols], w_ref[gate_cols, down_cols]
        x, gy = x_ref[...], gy_ref[...]
        gate, up = nn(x, w_gate), nn(x, w_up)
        sigma = jax.nn.sigmoid(gate)
        silu = gate * sigma
        act = silu * up
        d_act = nt(gy, w_down)
        d_gate = (d_act * up * sigma * (1.0 + gate * (1.0 - sigma))).astype(LOW)
        d_up = (d_act * silu).astype(LOW)
        out_ref[...] += nn(act.astype(LOW), w_down)
        dx_ref[...] += nt(d_gate, w_gate) + nt(d_up, w_up)
        x_t = xt_ref[...]
        grad_ref[:, gate_cols] = nn(x_t, d_gate).astype(LOW)
        grad_ref[:, up_cols] = nn(x_t, d_up).astype(LOW)
        grad_ref[gate_cols, down_cols] = nn(act.T.astype(LOW), plain_ref[...]).astype(LOW)


def feed_forward(x, gy, plain, w, folds, fold):
    tokens, width = x.shape
    whole = pl.BlockSpec((tokens, width), lambda j: (0, 0))
    return pl.pallas_call(
        feed_kernel,
        grid=(folds,),
        in_specs=[whole, whole, whole, pl.BlockSpec((width, 3 * fold), lambda j: (0, j))],
        out_specs=[whole, whole, pl.BlockSpec((width, 3 * fold), lambda j: (0, j))],
        out_shape=[
            shape((tokens, width)),
            shape((tokens, width)),
            shape((width, 3 * fold * folds), LOW),
        ],
        scratch_shapes=[pltpu.VMEM((width, tokens), LOW)],
        compiler_params=pltpu.CompilerParams(vmem_limit_bytes=60 * 2**20),
        cost_estimate=guess(35),
        name="feed_forward",
    )(x, gy, plain, w)


def last_grads_kernel(x_ref, scan_ref, query_ref, kv_ref, small_ref, grad_ref):
    x_t = x_ref[...].astype(jnp.float32).T.astype(LOW)
    scan = scan_ref.shape[1]
    query = query_ref.shape[1]
    grad_ref[:, : scan - LANES] = nn(x_t, scan_ref[:, : scan - LANES]).astype(LOW)
    grad_ref[:, scan - LANES : scan] = (nn(x_t, scan_ref[:, scan - LANES :]) + small_ref[...]).astype(LOW)
    grad_ref[:, scan : scan + query] = nn(x_t, query_ref[...]).astype(LOW)
    grad_ref[:, scan + query :] = nn(x_t, kv_ref[...]).astype(LOW)


def last_grads(x, d_scan, d_query, d_kv, small):
    tokens, width = x.shape
    count = d_scan.shape[1] + d_query.shape[1] + d_kv.shape[1]
    return pl.pallas_call(
        last_grads_kernel,
        out_shape=shape((width, count), LOW),
        compiler_params=pltpu.CompilerParams(vmem_limit_bytes=56 * 2**20),
        cost_estimate=guess(8),
        name="last_grads",
    )(x, d_scan, d_query, d_kv, small)


def tap_marks(starts, first, length, taps):
    ext = doc_index(starts, first - (taps - 1) + jnp.arange(length + taps - 1, dtype=jnp.int32))
    return jnp.stack([(ext[i : i + length] == ext[taps - 1 :]).astype(jnp.float32) for i in range(taps)], axis=1)


def marks_of(starts, block_base, length, taps):
    ext = doc_index(starts, block_base - (taps - 1) + jnp.arange(length + taps - 1, dtype=jnp.int32))
    here = ext[taps - 1 :]
    chunks = here.reshape(-1, CHUNK)
    ahead = ext[taps - 2 : taps - 2 + length].reshape(-1, CHUNK)[:, :1]
    last = chunks[:, -1:]
    columns = [ext[i : i + length] == here for i in range(taps)] + [
        (chunks == ahead).reshape(-1),
        (chunks == last).reshape(-1),
        here,
        jnp.broadcast_to(last == ahead, chunks.shape).reshape(-1),
    ]
    marks = jnp.stack([column.astype(jnp.float32) for column in columns], axis=1)
    marks = jnp.pad(marks, ((0, 0), (0, LANES - len(columns))))
    return marks, jnp.broadcast_to(here.astype(jnp.float32)[None], (8, length)), here


def per_device(
    hidden_in,
    cotangent,
    doc_starts,
    gain_in,
    mamba_gate_w,
    mamba_in_w,
    mamba_bc_w,
    mamba_dt_w,
    dt_bias,
    a_log,
    d_skip,
    conv_x,
    conv_bc,
    mamba_gain,
    attn_q_w,
    attention_key_value_weight,
    mamba_out_w,
    attn_out_w,
    gain_ffn,
    ffn_gate_w,
    ffn_up_w,
    ffn_down_w,
):
    devices = lax.axis_size("head") * lax.axis_size("wide")
    wide_id = lax.axis_index("wide")
    micro_count = hidden_in.shape[0]
    block_tok = hidden_in.shape[2] * lax.axis_size("head")
    taps = conv_x.shape[0]
    heads = dt_bias.shape[0]
    rows, inner = mamba_gate_w.shape
    width = rows * devices
    bc_cols = mamba_bc_w.shape[1]
    query_cols = attn_q_w.shape[1]
    kv_cols = attention_key_value_weight.shape[1]
    hidden = ffn_gate_w.shape[1]
    out_rows = mamba_out_w.shape[0]
    attn_rows = attn_out_w.shape[0]
    chan = conv_x.shape[1]
    chan_bc = conv_bc.shape[1]

    scan_cols = inner + bc_cols
    first_cols = scan_cols + LANES

    heads_dev, wide_dev = lax.axis_size("head"), lax.axis_size("wide")
    folds = hidden // width
    feature = jnp.arange(width, dtype=jnp.int32)
    inside = (feature // rows) % wide_dev * heads_dev + feature // (rows * wide_dev)
    order = (inside[:, None] * rows + (feature % rows)[:, None] == feature[None, :]).astype(LOW)

    def mixed(array):
        return nn(array.reshape(-1, width), order).astype(LOW).reshape(array.shape)

    def plain(array):
        return nt(array.reshape(-1, width), order).astype(LOW).reshape(array.shape)

    def by_place(array):
        return array.reshape((heads_dev, wide_dev) + array.shape[1:]).swapaxes(0, 1).reshape(array.shape)

    def by_owner(array):
        return array.reshape((wide_dev, heads_dev) + array.shape[1:]).swapaxes(0, 1).reshape(array.shape)

    def folded(weight):
        return weight.reshape(rows, heads_dev, wide_dev, folds, rows).transpose(0, 3, 2, 1, 4).reshape(rows, folds, width)

    def unfolded(parts):
        unit = jnp.arange(hidden, dtype=jnp.int32)
        owner, fold, row = unit // (folds * rows), unit // rows % folds, unit % rows
        at = (owner % wide_dev * heads_dev + owner // wide_dev) * rows + row
        total = 0.0
        for i, part in enumerate(parts):
            one_hot = ((feature[:, None] == at[None, :]) & (fold == i)[None, :]).astype(LOW)
            total = total + nn(jnp.concatenate(split_low(part, 3), axis=0), one_hot)
        high, middle, low = split_at(total, (rows,) * 3, 0)
        return high + (middle + low)

    small = packed([gain_in, gain_ffn, mamba_gain, conv_x, conv_bc], rows)
    small_cols = small.shape[1]
    pad = jnp.zeros((rows, LANES - heads - small_cols), LOW)
    in_shard = jnp.concatenate(
        [mamba_in_w, mamba_bc_w, mamba_dt_w, small, pad, mamba_gate_w, attn_q_w, attention_key_value_weight], axis=1
    )
    in_rows = gather_head(in_shard, micro_count)
    w_in = lax.all_gather(in_rows, "wide", axis=0, tiled=True)
    x_low = to_blocks(after(mixed(hidden_in[:, 0]), in_rows))
    gy_pieces = cotangent[:, 0]
    to_width = mixed(jnp.concatenate([ffn_down_w, mamba_out_w, attn_out_w], axis=0)).reshape(-1, rows, width)
    gate_folds, up_folds = folded(ffn_gate_w), folded(ffn_up_w)
    late_parts = []
    for i in range(folds):
        late_parts += [gate_folds[:, i], up_folds[:, i], to_width[i]]
    late_parts += [to_width[i] for i in range(folds, to_width.shape[0])]
    late_shard = after(jnp.concatenate(late_parts, axis=1), x_low)
    micro = jnp.minimum(lax.axis_index("head"), micro_count - 1)
    starts = pick(doc_starts, micro)
    block_base = wide_id * block_tok
    marks, docs_row, doc_here = marks_of(starts, block_base, block_tok, taps)
    key_doc = doc_index(starts, jnp.arange(block_tok * lax.axis_size("wide"), dtype=jnp.int32))
    masks = attend_masks(doc_here, key_doc, doc_starts.shape[1])
    mats = head_matrices(inner, heads)
    bias_row = lanes_row(dt_bias)
    rate_row = lanes_row(-jnp.exp(a_log))
    skip_row = jnp.repeat(d_skip, inner // heads)[None]
    x_low, marks, docs_row, masks, mats, bias_row, rate_row, skip_row = lax.optimization_barrier(
        (x_low, marks, docs_row, masks, mats, bias_row, rate_row, skip_row)
    )
    x_tokens = x_low.astype(jnp.float32)

    small_at = scan_cols + heads
    w_scan, w_gate, w_qkv = split_at(w_in, (first_cols, inner, query_cols + kv_cols), 1)
    small_all = w_scan[:, small_at : small_at + small_cols].reshape(devices, -1).astype(jnp.float32)
    g_in, g_ffn, g_mamba, c_x, c_bc = split_at(
        small_all, (rows, rows, chan, taps * chan, taps * chan_bc), 1
    )
    gain_in_all = g_in.reshape(-1)
    gain_ffn_all = g_ffn.reshape(-1)
    g_mamba, c_x, c_bc = by_owner(g_mamba), by_owner(c_x), by_owner(c_bc)
    gain_mamba_row = g_mamba.reshape(1, -1)
    taps_all = jnp.concatenate(
        [
            c_x.reshape(devices, taps, chan).transpose(1, 0, 2).reshape(taps, -1),
            c_bc.reshape(devices, taps, chan_bc).transpose(1, 0, 2).reshape(taps, -1),
        ],
        axis=1,
    )
    cols = (inner, bc_cols, 0, inner // bc_cols, scan_cols // LANES)
    place = jnp.reshape(wide_id, (1,)).astype(jnp.int32)


    normed_in, pull_in = jax.vjp(rms_scale, x_tokens, gain_in_all)
    block_in = normed_in.astype(LOW)
    raw_qkv = nn(block_in, w_qkv).astype(LOW)
    keys = Gathered(raw_qkv[:, query_cols:])
    raw_scan = nn(after(block_in, raw_qkv), w_scan)
    rim = shifted(raw_scan[block_tok - 8 :, :scan_cols], "wide", 1)
    rim = jnp.where(jnp.arange(8)[:, None] > 8 - taps, rim, 0.0)
    raw_gate = nn(after(block_in, raw_scan), w_gate)
    keys.step()
    taps_ext = jnp.pad(taps_all, ((0, 8 - taps), (0, 0)))
    *feats, sent, total, decay_rows = mamba_local(
        raw_scan, after(rim, *keys.parts), marks, taps_ext, bias_row, rate_row, cols, mats
    )
    late_rows = gather_head(late_shard, micro_count, (sent,))
    w_late = lax.all_gather(late_rows, "wide", axis=0, tiled=True)
    q_rows = raw_qkv[:, :query_cols].T.reshape(QUERY_HEADS, HEAD_SIZE, block_tok)
    key_all = keys.rest()
    forward = Carried(sent, total, decay_rows, False)
    forward.step()
    out_0, q_back_0 = attend(0, after(q_rows, forward.sent), key_all, masks, place)
    forward.step(out_0)
    out_1, q_back_1 = attend(1, after(q_rows, forward.sent, out_0), key_all, masks, place)
    attn_low = jnp.concatenate([out_0, out_1], axis=0).reshape(query_cols, block_tok).astype(LOW)
    mamba_low, y_low, entry = mamba_mix(
        feats, raw_gate, marks, docs_row, forward.rest(out_1), skip_row, gain_mamba_row, mats
    )
    gy_plain = to_blocks(after(gy_pieces, raw_scan), (out_0,))
    d_out_low = mixed(gy_plain)
    out_at = 3 * hidden
    out_both = jnp.concatenate(
        [w_late[:, i : i + width].reshape(devices, rows, width) for i in range(out_at, w_late.shape[1], width)], axis=1
    )
    out_both = by_owner(out_both)
    w_mamba_out = out_both[:, :out_rows].reshape(-1, width)
    w_attn_out = out_both[:, out_rows:].reshape(-1, width)

    resid = x_tokens + nn(mamba_low, w_mamba_out) + tn(attn_low, w_attn_out)
    normed_ffn, pull_ffn = jax.vjp(rms_scale, resid, gain_ffn_all)
    ffn_in = normed_ffn.astype(LOW)
    fed, d_ffn_in, grad_ffn = feed_forward(ffn_in, d_out_low, gy_plain, w_late, folds, width)
    part_ffn = sum_wide(grad_ffn)
    d_resid_norm, grad_gain_ffn = pull_ffn(d_ffn_in)
    d_resid = d_out_low.astype(jnp.float32) + d_resid_norm

    d_mix = d_resid.astype(LOW)
    d_gate_z, dy_low, grad_gain_m, sent_back, total, decay_rows = mamba_gate_back(
        nt(d_mix, w_mamba_out), y_low, raw_gate, feats, marks, gain_mamba_row, mats
    )
    backward = Carried(sent_back, total, decay_rows, True)
    backward.step()
    d_attn = nt(w_attn_out, after(d_mix, backward.sent)).astype(LOW).reshape(QUERY_HEADS, HEAD_SIZE, block_tok)
    d_query_0, d_kv_0 = attend_back(0, q_back_0, out_0, d_attn, key_all, masks, place)
    backward.step(d_query_0)
    d_query_1, d_kv_all = attend_back(
        1, q_back_1, out_1, after(d_attn, backward.sent, d_kv_0), key_all, masks, place, d_kv_0
    )
    d_kv_sum = Reduced(d_kv_all.reshape(-1, 2, block_tok // 2, kv_cols).swapaxes(0, 1))
    d_kv_sent = d_kv_sum.begin()
    d_query = jnp.concatenate([d_query_0, d_query_1], axis=0).reshape(query_cols, block_tok).T
    d_mix_plain = plain(after(d_mix, *d_kv_sent))
    grad_out = jnp.concatenate(
        [
            tn(mamba_low, d_mix_plain).astype(LOW).reshape(devices, out_rows, width),
            nn(attn_low, d_mix_plain).astype(LOW).reshape(devices, attn_rows, width),
        ],
        axis=1,
    ).reshape(devices, -1, rows, width)
    grad_out = by_place(grad_out)
    grad_gate = tn(after(block_in, *d_kv_sent), d_gate_z).astype(LOW)
    early = jnp.concatenate(
        [grad_out[:, i].reshape(width, width) for i in range(grad_out.shape[1])] + [grad_gate], axis=1
    )
    d_kv_sum.end(early)
    d_kv_sent = d_kv_sum.begin()
    part_early = sum_wide(after(early, part_ffn))
    d_state = backward.rest(early)
    d_scan, grad_skip, grad_head, grad_taps, rim_back, edge = mamba_scan_back(
        feats, raw_scan, rim, taps_ext, marks, docs_row, dy_low, entry, after(d_state, part_ffn, *d_kv_sent),
        skip_row, bias_row, rate_row, cols, mats,
    )
    d_kv_sum.end(d_scan)
    own_ffn = owned(part_ffn, micro_count, (d_scan,))
    d_kv = d_kv_sum.rest().reshape(block_tok, kv_cols)
    rim_came = shifted(rim_back, "wide", -1)
    d_scan = lax.dynamic_update_slice(d_scan, (edge + rim_came).astype(LOW), (block_tok - 8, 0))
    grad_small = jnp.concatenate(
        [
            jnp.zeros((devices, rows), jnp.float32),
            grad_gain_ffn.reshape(devices, rows),
            by_place(grad_gain_m[0].reshape(devices, chan)),
            by_place(grad_taps[:taps, :inner].reshape(taps, devices, chan).transpose(1, 0, 2).reshape(devices, -1)),
            by_place(grad_taps[:taps, inner:].reshape(taps, devices, chan_bc).transpose(1, 0, 2).reshape(devices, -1)),
        ],
        axis=1,
    )
    grad_small = jnp.pad(grad_small, ((0, 0), (0, rows * small_cols - grad_small.shape[1])))
    grad_small = jnp.pad(
        grad_small.reshape(width, small_cols), ((0, 0), (heads, LANES - heads - small_cols))
    )
    late = last_grads(after(block_in, own_ffn), d_scan, d_query, d_kv, grad_small)

    d_late = after(jnp.concatenate([d_query, d_kv], axis=1), late)
    d_x_norm, grad_gain_in = pull_in(nt(d_gate_z, w_gate) + nt(d_late, w_qkv) + nt(d_scan, w_scan))
    grad_x = (d_resid + d_x_norm).astype(LOW)
    part_late = sum_wide(after(late, part_early))
    own_early = owned(after(part_early, late), micro_count, (grad_x,))
    results = from_blocks(
        jnp.concatenate([plain((resid + fed).astype(LOW)), plain(grad_x)], axis=1), micro_count
    )
    summed = sum_everywhere(
        jnp.concatenate(
            [grad_head[:2, :heads].reshape(-1), jnp.sum(grad_skip[0].reshape(heads, -1), axis=1), grad_gain_in]
        )
    )
    per_head = summed[: 3 * heads].reshape(3, heads)
    inside_place = wide_id * heads_dev + lax.axis_index("head")
    o_gain_in = lax.dynamic_slice_in_dim(summed[3 * heads :], inside_place * rows, rows)
    own_late = owned(part_late, micro_count)

    g_x, g_bc, g_dt, g_small, _, g_q, g_kv = split_at(
        own_late, (inner, bc_cols, heads, small_cols, LANES - heads - small_cols, query_cols, kv_cols), 1
    )
    *g_out, g_gate = split_at(own_early, (width,) * ((out_rows + attn_rows) // rows) + (inner,), 1)
    _, o_gain_ffn, o_gain_m, o_conv_x, o_conv_bc = split_at(
        g_small.reshape(-1), (rows, rows, chan, taps * chan, taps * chan_bc), 0
    )
    g_mamba_out, g_attn_out = split_at(jnp.concatenate(g_out, axis=0), (out_rows, attn_rows), 0)
    g_ffn = split_at(own_ffn, (width,) * (3 * folds), 1)
    return (
        results[:, None, :, :width],
        results[:, None, :, width:],
        o_gain_in,
        g_gate,
        g_x,
        g_bc,
        g_dt,
        per_head[0],
        per_head[1],
        per_head[2],
        o_conv_x.reshape(taps, chan),
        o_conv_bc.reshape(taps, chan_bc),
        o_gain_m,
        g_q,
        g_kv,
        g_mamba_out,
        g_attn_out,
        o_gain_ffn,
        unfolded(g_ffn[0::3]),
        unfolded(g_ffn[1::3]),
        jnp.concatenate(g_ffn[2::3], axis=0),
    )


def solution(mesh):
    tokens = P(None, "wide", "head", None)
    matrix = P(ALL, None)
    vector = P(ALL)
    taps = P(None, ALL)
    in_specs = (
        (tokens, tokens, P(), vector)
        + (matrix,) * 4
        + (P(),) * 3
        + (taps, taps, vector)
        + (matrix,) * 4
        + (vector,)
        + (matrix,) * 3
    )
    out_specs = (
        (tokens, tokens, vector)
        + (matrix,) * 4
        + (P(),) * 3
        + (taps, taps, vector)
        + (matrix,) * 4
        + (vector,)
        + (matrix,) * 3
    )
    return jax.shard_map(
        per_device, mesh=mesh, in_specs=in_specs, out_specs=out_specs, check_vma=False
    )
```

time: 3140 us -> 621 us (0.20)
  waiting for transfers between devices: 1910 us -> 195 us
  blocking collectives: 396 us -> 0 us
  matrix products: 396 us -> 58.3 us
  other arithmetic: 187 us -> 34.2 us
  Pallas kernels: 0 us -> 124 us
  starting transfers between devices: 15.5 us -> 106 us
  local copies, waits for them, and re-layouts: 154 us -> 75.8 us
    reduce_scatter x19 -> x3, waiting for transfers between devices: 1490 us -> 27.7 us  [sum_wide(): return lax.psum_scatter(array, 'wide', scatter_dimension=0, tiled=True)]
    dot_general x156 -> x23, matrix products: 396 us -> 58.3 us  [the longest x12 28.1 us: nn(): return jnp.dot(left, right, preferred_element_type=jnp.float32)]
    all_gather x14 -> x0, blocking collectives: 316 us -> none  [the longest x9 125 us: carried_in(): lax.all_gather(a.astype(kind), axis)]
    all_gather x17 -> x2, waiting for transfers between devices: 285 us -> 28 us  [the longest x1 21.9 us: per_device(): w_late = lax.all_gather(late_rows, 'wide', axis=0, tiled=True)]
    ppermute x0 -> x45, waiting for transfers between devices: none -> 139 us  [the longest x21 63.8 us: swapped(): return lax.ppermute(value, axis, [(i, i ^ bit) for i in range(count)])]
    unnamed x40 -> x5, waiting for transfers between devices: 135 us -> 0.08 us
    pallas_call x0 -> x16, Pallas kernels: none -> 124 us  [the longest x4 57.8 us: call(): pl.pallas_call(kernel, grid=(parts,), in_specs=[spec(block, how) for _, b...]
    ppermute x0 -> x45, starting transfers between devices: none -> 102 us  [the longest x21 35.2 us: swapped(): return lax.ppermute(value, axis, [(i, i ^ bit) for i in range(count)])]
  transfers between devices with their start and end apart: 44 -> 52, of which waited for: 25 -> 24; matrix products, arithmetic and copies ran while one was open for 18% -> 20% of each run, Pallas kernels for 0% -> 15%
where the time goes in v1:
time: 621 us; the launch traced here: 610 us
  waiting for transfers between devices  195 us (31%)
  Pallas kernels  124 us (20%)
  starting transfers between devices  106 us (17%)
  local copies, waits for them, and re-layouts  75.8 us (12%)
  matrix products  58.3 us (9%)
  other arithmetic  34.2 us (6%)
  between operations  16.6 us (3%)
    ppermute x21, waiting for transfers between devices, swapped(): return lax.ppermute(value, axis, [(i, i ^ bit) for i in range(count)])  63.8 us
    pallas_call x4, Pallas kernels, call(): pl.pallas_call(kernel, grid=(parts,), in_specs=[spec(block, how) for _, b...  57.8 us
    ppermute x21, starting transfers between devices, swapped(): return lax.ppermute(value, axis, [(i, i ^ bit) for i in range(count)])  35.2 us
    ppermute x3, waiting for transfers between devices, from_blocks(): lax.ppermute(pick(parts, (place + step) % count), 'head', pairs)  31.7 us
    pallas_call x1, Pallas kernels, feed_forward(): pl.pallas_call(feed_kernel, grid=(folds,), in_specs=[whole, whole, whole,...  30.3 us
    dot_general x12, matrix products, nn(): return jnp.dot(left, right, preferred_element_type=jnp.float32)  28.1 us
    reduce_scatter x3, waiting for transfers between devices, sum_wide(): return lax.psum_scatter(array, 'wide', scatter_dimension=0, tiled=True)  27.7 us
    ppermute x9, waiting for transfers between devices, reduce_head(): lax.ppermute(pick(array, (place + step) % count), 'head', pairs)  27.5 us
  transfers between devices with their start and end apart: 52, of which 24 were waited for; matrix products, arithmetic and copies ran while one was open for 20% of the time, Pallas kernels for 15%

profile of v1, /device:TPU:24, one launch (start us, length us, event | category | flops | bytes accessed | tf_op | source)
XLA Modules:
  0.0 610.1 jit_solution(9240444430993054921)
XLA Ops:
  44.7 6.3 %collective-permute-start.3 = (bf16[128,1024]{1,0:T(8,128)(2,1)S(1)}, bf16[128,1024]{1,0:T(8,128)(2,1)S(1)}, u32[]{:S(2)}, u32[]{:S(2)}) collective-permute-start(bf16[128,1024]{1,0:T(8,128)(2,1)S(1)} %get-tuple-element.388), channel_id=1, source_target_pairs={{0,8},{8,16},{24,0},{1,9},{9,17},{25,1},{2,10},{10,18},{26,2},{3,1... | collective-permute-start | bytes 786440 | tf_op jit(solution)/shard_map/ppermute | solution.py:96
  51.8 6.7 %collective-permute-start.4 = (bf16[128,1024]{1,0:T(8,128)(2,1)S(1)}, bf16[128,1024]{1,0:T(8,128)(2,1)S(1)}, u32[]{:S(2)}, u32[]{:S(2)}) collective-permute-start(bf16[128,1024]{1,0:T(8,128)(2,1)S(1)} %get-tuple-element.387), channel_id=1, source_target_pairs={{0,16},{16,0},{24,8},{1,17},{17,1},{25,9},{2,18},{18,2},{26,10},{3... | collective-permute-start | bytes 786440 | tf_op jit(solution)/shard_map/ppermute | solution.py:96
  69.8 9.9 %collective-permute-start.15 = (bf16[32,8192]{1,0:T(8,128)(2,1)S(1)}, bf16[32,8192]{1,0:T(8,128)(2,1)}, u32[]{:S(2)}, u32[]{:S(2)}) collective-permute-start(bf16[32,8192]{1,0:T(8,128)(2,1)S(1)} %slice_dynamic-update-slice_fusion), channel_id=1, source_target_pairs={{0,8},{8,16},{24,0},{1,9},{9,17},{25,1},{2,10},{10,18},{26,2},{3,1... | collective-permute-start | bytes 1572872 | tf_op jit(solution)/shard_map/ppermute | solution.py:74
  121.2 11.0 %mamba_local.1 = (f32[512,1536]{1,0:T(8,128)}, bf16[512,1536]{1,0:T(8,128)(2,1)}, bf16[512,256]{1,0:T(8,128)(2,1)}, bf16[512,256]{1,0:T(8,128)(2,1)}, f32[512,12...) custom-call(f32[512,1920]{1,0:T(8,128)} %copy-done.71, ...), custom_call_target="tpu_custom_call" | custom-call | flops 11000000512 | bytes 33000000 | tf_op jit(solution)/shard_map/mamba_local/pallas_call | solution.py:619
  139.7 6.4 %collective-permute-done.11 = bf16[2,512,128]{2,1,0:T(8,128)(2,1)S(1)} collective-permute-done((bf16[2,512,128]{2,1,0:T(8,128)(2,1)S(1)}, bf16[2,512,128]{2,1,0:T(8,128)(2,1)S(1)}, u32[]{:S(2)}, u32[]{:S(2)}) %collective-permute-start.11) | collective-permute-done | bytes 262176 | tf_op jit(solution)/shard_map/ppermute | solution.py:56
  174.1 7.1 %collective-permute-done.10.got_ref = bf16[144,1536]{1,0:T(8,128)(2,1)S(1)} collective-permute-done((bf16[144,1536]{1,0:T(8,128)(2,1)S(1)}, bf16[144,1536]{1,0:T(8,128)(2,1)S(1)}, u32[]{:S(2)}, u32[]{:S(2)}) %collective-permute-start.10) | collective-permute-done | bytes 442400 | tf_op jit(solution)/shard_map/ppermute | solution.py:56
  193.4 11.3 %collective-permute-done.14.got_ref = bf16[144,1536]{1,0:T(8,128)(2,1)S(1)} collective-permute-done((bf16[144,1536]{1,0:T(8,128)(2,1)S(1)}, bf16[144,1536]{1,0:T(8,128)(2,1)S(1)}, u32[]{:S(2)}, u32[]{:S(2)}) %collective-permute-start.14) | collective-permute-done | bytes 442400 | tf_op jit(solution)/shard_map/ppermute | solution.py:56
  207.0 10.9 %mamba_mix.1 = (bf16[512,1536]{1,0:T(8,128)(2,1)}, f32[512,1536]{1,0:T(8,128)}, bf16[4,128,1536]{2,1,0:T(8,128)(2,1)}) custom-call(f32[512,1536]{1,0:T(8,128)} %get-tuple-element.129.act_ref, bf16[512,256]{1,0:T(8,128)(2,1)} %get-tuple-element.130.bcact_ref, f32[512,1536]{1,0:T(8,128)} %fusion.30.z_ref, f32[512,128]{1,0:T(8,128)} %get-tuple-element.132.step_ref, ...), custom_call_target="tpu_custom_call" | custom-call | flops 11000000512 | bytes 33000000 | tf_op jit(solution)/shard_map/mamba_mix/pallas_call | solution.py:619
  217.9 21.9 %all-gather.5.cloned.1.call-done.w_ref = bf16[1024,8192]{1,0:T(8,128)(2,1)} async-done(((bf16[128,8192]{1,0:T(8,128)(2,1)}), bf16[1024,8192]{1,0:T(8,128)(2,1)}) %all-gather.5.cloned.1.call-update) | async-done | bytes 16777232 | tf_op jit(solution)/shard_map/all_gather | solution.py:1256
  250.7 30.3 %feed_forward.1 = (f32[512,1024]{1,0:T(8,128)}, f32[512,1024]{1,0:T(8,128)}, bf16[1024,6144]{1,0:T(8,128)(2,1)}) custom-call(bf16[512,1024]{1,0:T(8,128)(2,1)} %multiply_convert_fusion.x_ref, bf16[512,1024]{1,0:T(8,128)(2,1)} %fusion.57.gy_ref, bf16[512,1024]{1,0:T(8,128)(2,1)} %bitcast.334, bf16[1024,8192]{1,0:T(8,128)(2,1)} %all-gather.5.cloned.1.call-done.w_ref), custom_call_target="tpu_custom_call" | custom-call | flops 35000000512 | bytes 105000000 | tf_op jit(solution)/shard_map/feed_forward/pallas_call | solution.py:1052
  289.2 12.7 %mamba_gate_back.1 = (bf16[512,1536]{1,0:T(8,128)(2,1)}, f32[512,1536]{1,0:T(8,128)}, f32[8,1536]{1,0:T(8,128)}, bf16[144,1536]{1,0:T(8,128)(2,1)}, f32[128,1536]{1,0:T(8,128)}, /*index=5*/f32[8,1536]{1,0:T(8,128)}) custom-call(f32[512,1536]{1,0:T(8,128)} %fusion.182.dym_ref, f32[512,1536]{1,0:T(8,128)} %get-tuple-element.168.y_ref, ...), custom_call_target="tpu_custom_call" | custom-call | flops 11000000512 | bytes 33000000 | tf_op jit(solution)/shard_map/mamba_gate_back/pallas_call | solution.py:619
  310.2 7.4 %attend_back.2 = (bf16[4,64,512]{2,1,0:T(8,128)(2,1)}, bf16[4096,256]{1,0:T(8,128)(2,1)}) custom-call(s32[1]{0:T(128)} %bitcast.41.place_ref, bf16[4,128,512]{2,1,0:T(8,128)(2,1)} %get-tuple-element.170.qb_ref, bf16[8,64,512]{2,1,0:T(8,128)(2,1)} %bitcast.370, f32[4,64,512]{2,1,0:T(8,128)} %get-tuple-element.145.o_ref, bf16[4096,256]{1,0:T(8,128)(2,1)} %bitcast.321, ...), custom_call_target="tpu_custom_call" | custom-call | flops 27000000512 | bytes 81000000 | tf_op jit(solution)/shard_map/attend_back/pallas_call | solution.py:990
  317.6 10.1 %collective-permute-done.22.got_ref = bf16[144,1536]{1,0:T(8,128)(2,1)S(1)} collective-permute-done((bf16[144,1536]{1,0:T(8,128)(2,1)S(1)}, bf16[144,1536]{1,0:T(8,128)(2,1)S(1)}, u32[]{:S(2)}, u32[]{:S(2)}) %collective-permute-start.22) | collective-permute-done | bytes 442400 | tf_op jit(solution)/shard_map/ppermute | solution.py:56
  329.5 7.1 %attend_back.3 = (bf16[4,64,512]{2,1,0:T(8,128)(2,1)}, bf16[4096,256]{1,0:T(8,128)(2,1)}) custom-call(s32[1]{0:T(128)} %bitcast.41.place_ref, bf16[4,128,512]{2,1,0:T(8,128)(2,1)} %get-tuple-element.177.qb_ref, bf16[8,64,512]{2,1,0:T(8,128)(2,1)} %bitcast.371, f32[4,64,512]{2,1,0:T(8,128)} %get-tuple-element.152.o_ref, ...), custom_call_target="tpu_custom_call", output_to_operand_aliasing={{1}: (6, {})} | custom-call | flops 27000000512 | bytes 81000000 | tf_op jit(solution)/shard_map/attend_back/pallas_call | solution.py:990
  353.4 27.7 %reduce-scatter.4.cloned.1.call-done = bf16[128,6144]{1,0:T(8,128)(2,1)} async-done(((bf16[1024,6144]{1,0:T(8,128)(2,1)}), bf16[128,6144]{1,0:T(8,128)(2,1)}) %reduce-scatter.4.cloned.1.call-update) | async-done | bytes 1572880 | tf_op jit(solution)/shard_map/reduce_scatter | solution.py:216
  395.8 8.6 %collective-permute-done.25.got_ref = bf16[144,1536]{1,0:T(8,128)(2,1)S(1)} collective-permute-done((bf16[144,1536]{1,0:T(8,128)(2,1)S(1)}, bf16[144,1536]{1,0:T(8,128)(2,1)S(1)}, u32[]{:S(2)}, u32[]{:S(2)}) %collective-permute-start.25) | collective-permute-done | bytes 442400 | tf_op jit(solution)/shard_map/ppermute | solution.py:56
  408.3 9.3 %collective-permute-start.24 = (bf16[1,2,256,256]{3,2,1,0:T(8,128)(2,1)S(1)}, bf16[1,2,256,256]{3,2,1,0:T(8,128)(2,1)S(1)}, u32[]{:S(2)}, u32[]{:S(2)}) collective-permute-start(bf16[1,2,256,256]{3,2,1,0:T(8,128)(2,1)S(1)} %dynamic-slice_bitcast_fusion.8), channel_id=1, source_target_pairs={{0,2},{1,3},{2,0},{3,1},{4,6},{5,7},{6,4},{7,5},{8,10},{9,11},{10,... | collective-permute-start | bytes 786440 | tf_op jit(solution)/shard_map/ppermute | solution.py:56
  424.6 23.3 %mamba_scan_back.1 = (bf16[512,1920]{1,0:T(8,128)(2,1)}, f32[8,1536]{1,0:T(8,128)}, f32[8,128]{1,0:T(8,128)}, f32[8,1792]{1,0:T(8,128)}, f32[8,1792]{1,0:T(8,128)}, /*index=5*/f32[8,1792]{1,0:T(8,128)}) custom-call(f32[512,1536]{1,0:T(8,128)} %get-tuple-element.129.act_ref, bf16[512,1536]{1,0:T(8,128)(2,1)} %get-tuple-element.190.slope_ref, ...), custom_call_target="tpu_custom_call" | custom-call | flops 23000000512 | bytes 69000000 | tf_op jit(solution)/shard_map/mamba_scan_back/pallas_call | solution.py:619
  463.6 8.0 %last_grads.1 = bf16[1024,2688]{1,0:T(8,128)(2,1)} custom-call(bf16[512,1024]{1,0:T(8,128)(2,1)} %copy-done.31, bf16[512,1920]{1,0:T(8,128)(2,1)} %fusion.115.scan_ref, bf16[512,512]{1,0:T(8,128)(2,1)} %bitcast.316, bf16[512,256]{1,0:T(8,128)(2,1)} %bitcast.336, f32[1024,128]{1,0:T(8,128)} %pad.33.small_ref), custom_call_target="tpu_custom_call" | custom-call | flops 8000000000 | bytes 24000000 | tf_op jit(solution)/shard_map/last_grads/pallas_call | solution.py:1082
  475.3 6.9 %fusion.41 = (f32[1024]{0:T(1024)S(1)}, f32[512]{0:T(512)S(1)}, f32[512,1024]{1,0:T(8,128)}) fusion(bf16[512,1024]{1,0:T(8,128)(2,1)S(1)} %bitcast.294, f32[512]{0:T(512)S(1)} %copy-done.61, f32[1024]{0:T(1024)S(1)} %copy-done.57, bf16[512,1920]{1,0:T(8,128)(2,1)S(1)} %copy-done.75, bf16[1024,4224]{1,0:T(8,128)(2,1)} %all-gather.3.cloned.1.call-done, ...), kind=kOutput, calls=%fused_computation.47 | convolution fusion | flops 2017982976 | bytes 13250560 | tf_op jit(solution)/shard_map/dot_general | solution.py:28
  503.5 9.9 %collective-permute-done.37 = f32[1096]{0:T(1024)S(1)} collective-permute-done((f32[1096]{0:T(1024)S(1)}, f32[1096]{0:T(1024)S(1)}, u32[]{:S(2)}, u32[]{:S(2)}) %collective-permute-start.37) | collective-permute-done | bytes 4416 | tf_op jit(solution)/shard_map/ppermute | solution.py:56
  524.9 31.7 %collective-permute-done.34 = bf16[128,2048]{1,0:T(8,128)(2,1)S(1)} collective-permute-done((bf16[128,2048]{1,0:T(8,128)(2,1)S(1)}, bf16[128,2048]{1,0:T(8,128)(2,1)S(1)}, u32[]{:S(2)}, u32[]{:S(2)}) %collective-permute-start.34) | collective-permute-done | bytes 524320 | tf_op jit(solution)/shard_map/ppermute | solution.py:109
  567.2 11.2 %collective-permute-done.42 = bf16[32,3584]{1,0:T(8,128)(2,1)S(1)} collective-permute-done((bf16[32,3584]{1,0:T(8,128)(2,1)S(1)}, bf16[32,3584]{1,0:T(8,128)(2,1)S(1)}, u32[]{:S(2)}, u32[]{:S(2)}) %collective-permute-start.42) | collective-permute-done | bytes 229408 | tf_op jit(solution)/shard_map/ppermute | solution.py:210
  589.0 7.8 %collective-permute-done.45 = bf16[32,2688]{1,0:T(8,128)(2,1)S(1)} collective-permute-done((bf16[32,2688]{1,0:T(8,128)(2,1)S(1)}, bf16[32,2688]{1,0:T(8,128)(2,1)S(1)}, u32[]{:S(2)}, u32[]{:S(2)}) %collective-permute-start.45) | collective-permute-done | bytes 172064 | tf_op jit(solution)/shard_map/ppermute | solution.py:210
  (514 shorter events, 290.2 us)
Async XLA Ops:
  7.2 89.6 %all-gather.3.cloned.1.call-start = ((), (), s32[]{:S(2)}) async-start(), calls=%async_computation.3 | async-start | bytes 9732096 | tf_op jit(solution)/shard_map/all_gather | solution.py:1196
  32.9 206.9 %all-gather.5.cloned.1.call-start = ((), (), s32[]{:S(2)}) async-start(), calls=%async_computation.4 | async-start | bytes 18874368 | tf_op jit(solution)/shard_map/all_gather | solution.py:1256
  44.7 19.4 %collective-permute-start.3 = (bf16[128,1024]{1,0:T(8,128)(2,1)S(1)}, bf16[128,1024]{1,0:T(8,128)(2,1)S(1)}, u32[]{:S(2)}, u32[]{:S(2)}) collective-permute-start(bf16[128,1024]{1,0:T(8,128)(2,1)S(1)} %get-tuple-element.388), channel_id=1, source_target_pairs={{0,8},{8,16},{24,0},{1,9},{9,17},{25,1},{2,10},{10,18},{26,2},{3,1... | collective-permute-start | bytes 786440 | tf_op jit(solution)/shard_map/ppermute | solution.py:96
  69.8 62.4 %collective-permute-start.15 = (bf16[32,8192]{1,0:T(8,128)(2,1)S(1)}, bf16[32,8192]{1,0:T(8,128)(2,1)}, u32[]{:S(2)}, u32[]{:S(2)}) collective-permute-start(bf16[32,8192]{1,0:T(8,128)(2,1)S(1)} %slice_dynamic-update-slice_fusion), channel_id=1, source_target_pairs={{0,8},{8,16},{24,0},{1,9},{9,17},{25,1},{2,10},{10,18},{26,2},{3,1... | collective-permute-start | bytes 1572872 | tf_op jit(solution)/shard_map/ppermute | solution.py:74
  79.8 52.4 %collective-permute-start.16 = (bf16[32,8192]{1,0:T(8,128)(2,1)S(1)}, bf16[32,8192]{1,0:T(8,128)(2,1)}, u32[]{:S(2)}, u32[]{:S(2)}) collective-permute-start(bf16[32,8192]{1,0:T(8,128)(2,1)S(1)} %slice_dynamic-update-slice_fusion), channel_id=1, source_target_pairs={{0,16},{16,0},{24,8},{1,17},{17,1},{25,9},{2,18},{18,2},{26,10},{3... | collective-permute-start | bytes 1572872 | tf_op jit(solution)/shard_map/ppermute | solution.py:74
  83.5 48.7 %collective-permute-start.17 = (bf16[32,8192]{1,0:T(8,128)(2,1)S(1)}, bf16[32,8192]{1,0:T(8,128)(2,1)}, u32[]{:S(2)}, u32[]{:S(2)}) collective-permute-start(bf16[32,8192]{1,0:T(8,128)(2,1)S(1)} %slice_dynamic-update-slice_fusion), channel_id=1, source_target_pairs={{8,0},{16,8},{24,16},{9,1},{17,9},{25,17},{10,2},{18,10},{26,18},{... | collective-permute-start | bytes 1572872 | tf_op jit(solution)/shard_map/ppermute | solution.py:74
  137.9 243.1 %reduce-scatter.4.cloned.1.call-start = ((), (), s32[]{:S(2)}) async-start(), calls=%async_computation.5 | async-start | bytes 14155776 | tf_op jit(solution)/shard_map/reduce_scatter | solution.py:216
  149.8 35.0 %collective-permute-start.18 = (bf16[128,1024]{1,0:T(8,128)(2,1)S(1)}, bf16[128,1024]{1,0:T(8,128)(2,1)S(1)}, u32[]{:S(2)}, u32[]{:S(2)}) collective-permute-start(bf16[128,1024]{1,0:T(8,128)(2,1)S(1)} %get-tuple-element.378), channel_id=1, source_target_pairs={{0,8},{8,16},{24,0},{1,9},{9,17},{25,1},{2,10},{10,18},{26,2},{3,1... | collective-permute-start | bytes 786440 | tf_op jit(solution)/shard_map/ppermute | solution.py:96
  152.4 32.4 %collective-permute-start.19 = (bf16[128,1024]{1,0:T(8,128)(2,1)S(1)}, bf16[128,1024]{1,0:T(8,128)(2,1)S(1)}, u32[]{:S(2)}, u32[]{:S(2)}) collective-permute-start(bf16[128,1024]{1,0:T(8,128)(2,1)S(1)} %get-tuple-element.377), channel_id=1, source_target_pairs={{0,16},{16,0},{24,8},{1,17},{17,1},{25,9},{2,18},{18,2},{26,10},{3... | collective-permute-start | bytes 786440 | tf_op jit(solution)/shard_map/ppermute | solution.py:96
  155.6 29.2 %collective-permute-start.20 = (bf16[128,1024]{1,0:T(8,128)(2,1)S(1)}, bf16[128,1024]{1,0:T(8,128)(2,1)S(1)}, u32[]{:S(2)}, u32[]{:S(2)}) collective-permute-start(bf16[128,1024]{1,0:T(8,128)(2,1)S(1)} %get-tuple-element.376), channel_id=1, source_target_pairs={{8,0},{16,8},{24,16},{9,1},{17,9},{25,17},{10,2},{18,10},{26,18},{... | collective-permute-start | bytes 786440 | tf_op jit(solution)/shard_map/ppermute | solution.py:96
  181.5 23.2 %collective-permute-start.14 = (bf16[144,1536]{1,0:T(8,128)(2,1)S(1)}, bf16[144,1536]{1,0:T(8,128)(2,1)S(1)}, u32[]{:S(2)}, u32[]{:S(2)}) collective-permute-start(bf16[144,1536]{1,0:T(8,128)(2,1)S(1)} %get-tuple-element.150), channel_id=1, source_target_pairs={{0,4},{1,5},{2,6},{3,7},{4,0},{5,1},{6,2},{7,3},{8,12},{9,13},{10,... | collective-permute-start | bytes 1327112 | tf_op jit(solution)/shard_map/ppermute | solution.py:56
  281.1 190.4 %reduce-scatter.6.cloned.1.call-start = ((), (), s32[]{:S(2)}) async-start(), calls=%async_computation.6 | async-start | bytes 8257536 | tf_op jit(solution)/shard_map/reduce_scatter | solution.py:216
  307.1 20.5 %collective-permute-start.22 = (bf16[144,1536]{1,0:T(8,128)(2,1)S(1)}, bf16[144,1536]{1,0:T(8,128)(2,1)S(1)}, u32[]{:S(2)}, u32[]{:S(2)}) collective-permute-start(bf16[144,1536]{1,0:T(8,128)(2,1)S(1)} %get-tuple-element.174), channel_id=1, source_target_pairs={{0,2},{1,3},{2,0},{3,1},{4,6},{5,7},{6,4},{7,5},{8,10},{9,11},{10,... | collective-permute-start | bytes 1327112 | tf_op jit(solution)/shard_map/ppermute | solution.py:56
  381.1 197.4 %reduce-scatter.8.cloned.1.call-start = ((), (), s32[]{:S(2)}) async-start(), calls=%async_computation.7 | async-start | bytes 6193152 | tf_op jit(solution)/shard_map/reduce_scatter | solution.py:216
  386.0 19.7 %collective-permute-start.23 = (bf16[2,4,256,256]{3,2,1,0:T(8,128)(2,1)}, bf16[2,4,256,256]{3,2,1,0:T(8,128)(2,1)}, u32[]{:S(2)}, u32[]{:S(2)}) collective-permute-start(bf16[2,4,256,256]{3,2,1,0:T(8,128)(2,1)} %dynamic-slice_bitcast_fusion), channel_id=1, source_target_pairs={{0,1},{1,0},{2,3},{3,2},{4,5},{5,4},{6,7},{7,6},{8,9},{9,8},{10,11... | collective-permute-start | bytes 3145736 | tf_op jit(solution)/shard_map/ppermute | solution.py:56
  408.3 39.6 %collective-permute-start.24 = (bf16[1,2,256,256]{3,2,1,0:T(8,128)(2,1)S(1)}, bf16[1,2,256,256]{3,2,1,0:T(8,128)(2,1)S(1)}, u32[]{:S(2)}, u32[]{:S(2)}) collective-permute-start(bf16[1,2,256,256]{3,2,1,0:T(8,128)(2,1)S(1)} %dynamic-slice_bitcast_fusion.8), channel_id=1, source_target_pairs={{0,2},{1,3},{2,0},{3,1},{4,6},{5,7},{6,4},{7,5},{8,10},{9,11},{10,... | collective-permute-start | bytes 786440 | tf_op jit(solution)/shard_map/ppermute | solution.py:56
  417.6 30.5 %collective-permute-start.27 = (bf16[1,2,256,256]{3,2,1,0:T(8,128)(2,1)S(1)}, bf16[1,2,256,256]{3,2,1,0:T(8,128)(2,1)S(1)}, u32[]{:S(2)}, u32[]{:S(2)}) collective-permute-start(bf16[1,2,256,256]{3,2,1,0:T(8,128)(2,1)S(1)} %dynamic-slice_bitcast_fusion.7), channel_id=1, source_target_pairs={{0,4},{1,5},{2,6},{3,7},{4,0},{5,1},{6,2},{7,3},{8,12},{9,13},{10,... | collective-permute-start | bytes 786440 | tf_op jit(solution)/shard_map/ppermute | solution.py:56
  420.7 40.8 %collective-permute-start.29 = (bf16[32,6144]{1,0:T(8,128)(2,1)}, bf16[32,6144]{1,0:T(8,128)(2,1)}, u32[]{:S(2)}, u32[]{:S(2)}) collective-permute-start(bf16[32,6144]{1,0:T(8,128)(2,1)} %get-tuple-element.352), channel_id=1, source_target_pairs={{0,8},{8,16},{16,24},{1,9},{9,17},{17,25},{2,10},{10,18},{18,26},{... | collective-permute-start | bytes 1179656 | tf_op jit(solution)/shard_map/ppermute | solution.py:210
  422.0 39.5 %collective-permute-start.30 = (bf16[32,6144]{1,0:T(8,128)(2,1)}, bf16[32,6144]{1,0:T(8,128)(2,1)}, u32[]{:S(2)}, u32[]{:S(2)}) collective-permute-start(bf16[32,6144]{1,0:T(8,128)(2,1)} %get-tuple-element.354), channel_id=1, source_target_pairs={{0,16},{8,24},{16,0},{1,17},{9,25},{17,1},{2,18},{10,26},{18,2},{3... | collective-permute-start | bytes 1179656 | tf_op jit(solution)/shard_map/ppermute | solution.py:210
  423.3 38.2 %collective-permute-start.31 = (bf16[32,6144]{1,0:T(8,128)(2,1)}, bf16[32,6144]{1,0:T(8,128)(2,1)}, u32[]{:S(2)}, u32[]{:S(2)}) collective-permute-start(bf16[32,6144]{1,0:T(8,128)(2,1)} %get-tuple-element.353), channel_id=1, source_target_pairs={{0,24},{8,0},{16,8},{1,25},{9,1},{17,9},{2,26},{10,2},{18,10},{3,2... | collective-permute-start | bytes 1179656 | tf_op jit(solution)/shard_map/ppermute | solution.py:210
  497.8 27.0 %collective-permute-start.33 = (bf16[128,2048]{1,0:T(8,128)(2,1)S(1)}, bf16[128,2048]{1,0:T(8,128)(2,1)S(1)}, u32[]{:S(2)}, u32[]{:S(2)}) collective-permute-start(bf16[128,2048]{1,0:T(8,128)(2,1)S(1)} %get-tuple-element.350), channel_id=1, source_target_pairs={{0,8},{8,16},{16,24},{1,9},{9,17},{17,25},{2,10},{10,18},{18,26},{... | collective-permute-start | bytes 1572872 | tf_op jit(solution)/shard_map/ppermute | solution.py:109
  517.2 39.4 %collective-permute-start.34 = (bf16[128,2048]{1,0:T(8,128)(2,1)S(1)}, bf16[128,2048]{1,0:T(8,128)(2,1)S(1)}, u32[]{:S(2)}, u32[]{:S(2)}) collective-permute-start(bf16[128,2048]{1,0:T(8,128)(2,1)S(1)} %get-tuple-element.349), channel_id=1, source_target_pairs={{0,16},{8,24},{16,0},{1,17},{9,25},{17,1},{2,18},{10,26},{18,2},{3... | collective-permute-start | bytes 1572872 | tf_op jit(solution)/shard_map/ppermute | solution.py:109
  518.6 38.1 %collective-permute-start.35 = (bf16[128,2048]{1,0:T(8,128)(2,1)S(1)}, bf16[128,2048]{1,0:T(8,128)(2,1)S(1)}, u32[]{:S(2)}, u32[]{:S(2)}) collective-permute-start(bf16[128,2048]{1,0:T(8,128)(2,1)S(1)} %get-tuple-element.348), channel_id=1, source_target_pairs={{0,24},{8,0},{16,8},{1,25},{9,1},{17,9},{2,26},{10,2},{18,10},{3,2... | collective-permute-start | bytes 1572872 | tf_op jit(solution)/shard_map/ppermute | solution.py:109
  558.1 20.3 %collective-permute-start.42 = (bf16[32,3584]{1,0:T(8,128)(2,1)S(1)}, bf16[32,3584]{1,0:T(8,128)(2,1)S(1)}, u32[]{:S(2)}, u32[]{:S(2)}) collective-permute-start(bf16[32,3584]{1,0:T(8,128)(2,1)S(1)} %get-tuple-element.361), channel_id=1, source_target_pairs={{0,16},{8,24},{16,0},{1,17},{9,25},{17,1},{2,18},{10,26},{18,2},{3... | collective-permute-start | bytes 688136 | tf_op jit(solution)/shard_map/ppermute | solution.py:210
  (113 other events, 1368.8 us)
Sparse Core Ops, SparseCore 0:
  33.0 63.7 all-gather.2
  138.1 101.7 all-gather.4
  281.2 99.8 reduce-scatter.3
  384.3 82.2 reduce-scatter.5
  471.7 61.0 reduce-scatter.7

commit v2 on v1

--- a/solution.py
+++ b/solution.py
@@ -64,60 +64,95 @@
     return pl.CostEstimate(flops=int(us * 1e9), bytes_accessed=int(us * 3e6), transcendentals=0)
 
 
-def gather_head(own, receivers, when=()):
+def tied(*values):
+    return lax.optimization_barrier(values)
+
+
+def sent_on(pieces, sources, receivers):
     count = lax.axis_size("head")
     place = lax.axis_index("head")
-    both = jnp.zeros((count,) + own.shape, own.dtype)
-    both = lax.dynamic_update_index_in_dim(both, own, place, 0)
+    got = []
     for step in range(1, count):
-        pairs = [(i, (i + step) % count) for i in range(count) if (i + step) % count < receivers]
-        got = after(lax.ppermute(own, "head", pairs), *when)
-        both = lax.dynamic_update_index_in_dim(both, got, (place - step) % count, 0)
-    return both.reshape(-1, own.shape[1])
-
-
-def after(value, *others):
-    return lax.optimization_barrier((value,) + others)[0] if others else value
-
-
-def to_blocks(pieces, when=()):
-    count = lax.axis_size("head")
+        pairs = [(i, (i + step) % count) for i in range(count)]
+        pairs = [(i, k) for i, k in pairs if i < sources and k < receivers]
+        got.append(lax.ppermute(pieces((place + step) % count), "head", pairs))
+    return got
+
+
+def put_together(own, got):
     place = lax.axis_index("head")
-    micro_count = pieces.shape[0]
-
-    def of(target):
-        return pick(pieces, jnp.minimum(target, micro_count - 1))
-
-    own = jnp.where(place < micro_count, of(place), jnp.zeros_like(pieces[0]))
-    block = jnp.zeros((count,) + pieces.shape[1:], pieces.dtype)
-    block = lax.dynamic_update_index_in_dim(block, own, place, 0)
-    for step in range(1, count):
-        pairs = [(i, (i + step) % count) for i in range(count) if (i + step) % count < micro_count]
-        got = after(lax.ppermute(of((place + step) % count), "head", pairs), *when)
-        block = lax.dynamic_update_index_in_dim(block, got, (place - step) % count, 0)
-    return block.reshape(count * pieces.shape[1], pieces.shape[2])
-
-
-def from_blocks(block, micro_count, when=()):
-    count = lax.axis_size("head")
-    place = lax.axis_index("head")
-    parts = block.reshape(count, block.shape[0] // count, block.shape[1])
-    pieces = jnp.zeros_like(parts)
-    pieces = lax.dynamic_update_index_in_dim(pieces, pick(parts, place), place, 0)
-    for step in range(1, count):
-        pairs = [(i, (i + step) % count) for i in range(min(micro_count, count))]
-        got = after(lax.ppermute(pick(parts, (place + step) % count), "head", pairs), *when)
-        pieces = lax.dynamic_update_index_in_dim(pieces, got, (place - step) % count, 0)
-    return pieces[:micro_count]
-
-
-def sum_everywhere(value):
-    for axis in ALL:
-        step = 1
-        while step < lax.axis_size(axis):
-            value = value + swapped(value, axis, step)
-            step *= 2
-    return value
+    count = len(got) + 1
+    whole = lax.dynamic_update_index_in_dim(jnp.zeros((count,) + own.shape, own.dtype), own, place, 0)
+    for step, array in enumerate(got, 1):
+        whole = lax.dynamic_update_index_in_dim(whole, array, (place - step) % count, 0)
+    return whole
+
+
+class HeadRows:
+    def __init__(self, own, receivers):
+        self.own = own
+        self.got = sent_on(lambda target: own, lax.axis_size("head"), receivers)
+
+    def end(self):
+        return put_together(self.own, self.got).reshape(-1, self.own.shape[1])
+
+
+class ToBlocks:
+    def __init__(self, pieces):
+        micro_count = pieces.shape[0]
+        place = lax.axis_index("head")
+
+        def of(target):
+            return pick(pieces, jnp.minimum(target, micro_count - 1))
+
+        self.own = jnp.where(place < micro_count, of(place), jnp.zeros_like(pieces[0]))
+        self.got = sent_on(of, lax.axis_size("head"), micro_count)
+
+    def end(self):
+        return put_together(self.own, self.got).reshape(-1, self.own.shape[1])
+
+
+class FromBlocks:
+    def __init__(self, block, micro_count):
+        count = lax.axis_size("head")
+        parts = block.reshape(count, block.shape[0] // count, block.shape[1])
+        self.micro_count = micro_count
+        self.own = pick(parts, lax.axis_index("head"))
+        self.got = sent_on(lambda target: pick(parts, target), micro_count, count)
+
+    def end(self):
+        return put_together(self.own, self.got)[: self.micro_count]
+
+
+class HeadSum:
+    def __init__(self, part, sources, block=None):
+        count = lax.axis_size("head")
+        place = lax.axis_index("head")
+        array = part.reshape(count, -1, part.shape[1])
+        self.width = array.shape[2]
+        self.sources = sources
+        if block is not None:
+            self.block_shape = (block.shape[0] // count, block.shape[1])
+            array = jnp.concatenate([array, block.reshape(count, array.shape[1], -1)], axis=2)
+        self.own = pick(array, place)
+        self.got = sent_on(lambda target: pick(array, target), sources, count)
+
+    def end(self, sizes=None):
+        place = lax.axis_index("head")
+        at, out = 0, []
+        for size in sizes or (self.width,):
+            cut = [array[:, at : at + size].astype(jnp.float32) for array in [self.own] + self.got]
+            total = jnp.where(place < self.sources, cut[0], 0.0)
+            for term in cut[1:]:
+                total = total + term
+            out.append(total)
+            at += size
+        return out if sizes else out[0]
+
+    def end_block(self):
+        own, got = self.own[:, self.width :], [array[:, self.width :] for array in self.got]
+        whole = put_together(own, got)
+        return whole.reshape((whole.shape[0],) + self.block_shape)[: self.sources]
 
 
 def wide_bits():
@@ -125,6 +160,28 @@
     while 1 << (len(bits) + 1) <= lax.axis_size("wide"):
         bits.append(1 << len(bits))
     return bits
+
+
+class EverySum:
+    def __init__(self, value):
+        self.value = value
+        self.left = [("wide", bit) for bit in wide_bits()]
+        bit = 1
+        while bit < lax.axis_size("head"):
+            self.left.append(("head", bit))
+            bit *= 2
+
+    def begin(self):
+        self.got = swapped(self.value, *self.left.pop(0))
+
+    def end(self):
+        self.value = self.value + self.got
+
+    def rest(self):
+        while self.left:
+            self.begin()
+            self.end()
+        return self.value
 
 
 class Gathered:
@@ -135,19 +192,22 @@
         self.left = [bits[1:], bits[:0:-1]]
         self.done = [[], []]
 
-    def step(self):
+    def begin(self):
+        self.got = [swapped(array, "wide", left[0]) for array, left in zip(self.parts, self.left)]
+
+    def end(self):
         place = lax.axis_index("wide")
-        for i in range(2):
+        for i, got in enumerate(self.got):
             bit = self.left[i].pop(0)
+            mine = (place // bit) % 2
             array = self.parts[i]
-            got = swapped(array, "wide", bit)
-            mine = (place // bit) % 2
             self.parts[i] = jnp.where(mine == 0, jnp.stack([array, got]), jnp.stack([got, array]))
             self.done[i].insert(0, bit)
 
     def rest(self):
         while self.left[0]:
-            self.step()
+            self.begin()
+            self.end()
         arrays = []
         for array, done in zip(self.parts, self.done):
             ranks = [done.index(bit) for bit in sorted(done, reverse=True)]
@@ -159,65 +219,37 @@
         return stacked.reshape(-1, both.shape[-1])
 
 
-class Reduced:
+class CoreSum:
+    def __init__(self, part):
+        count = lax.axis_size("wide")
+        mine = lax.axis_index("wide") % 2
+        part = part.reshape(count // 2, 2, -1, part.shape[1])
+        self.own = pick(part, mine, 1)
+        self.got = swapped(pick(part, 1 - mine, 1), "wide", 1)
+
+    def end(self):
+        return (self.own.astype(jnp.float32) + self.got.astype(jnp.float32)).astype(self.own.dtype)
+
+
+class ChipSum:
     def __init__(self, array):
-        self.bits = wide_bits()
-        self.orders = [self.bits[1:], self.bits[:0:-1]]
-        self.parts = [array.reshape((array.shape[0], -1, 2) + array.shape[2:])]
-        self.axes = [[1]]
-        self.steps = len(self.bits)
-
-    def begin(self):
-        self.moves = []
-        for i, part in enumerate(self.parts):
-            bit = 1 if len(self.parts) == 1 else self.orders[i].pop(0)
-            axis = 2 if len(self.parts) == 1 else 1 + self.axes[i].index(bit)
-            mine = (lax.axis_index("wide") // bit) % 2
-            send = pick(part, 1 - mine, axis)
-            self.moves.append((bit, pick(part, mine, axis), send, swapped(send, "wide", bit)))
-        return [send for _, _, send, _ in self.moves]
-
-    def end(self, *when):
-        parts = []
-        for bit, kept, _, got in self.moves:
-            parts.append((kept.astype(jnp.float32) + after(got, *when).astype(jnp.float32)).astype(kept.dtype))
-        if len(parts) == 1:
-            half = parts[0].shape[0] // 2
-            self.axes = [list(self.bits[:0:-1]) for _ in range(2)]
-            parts = [
-                part.reshape((half,) + (2,) * len(axes) + part.shape[2:])
-                for part, axes in zip((parts[0][:half], parts[0][half:]), self.axes)
-            ]
-        else:
-            for axes, (bit, _, _, _) in zip(self.axes, self.moves):
-                axes.remove(bit)
-        self.parts = parts
-        self.steps -= 1
-
-    def rest(self):
-        while self.steps:
-            self.begin()
-            self.end()
-        return jnp.concatenate(self.parts, axis=0)
-
-
-def reduce_head(array, sources, when=()):
-    count = lax.axis_size("head")
-    place = lax.axis_index("head")
-    total = jnp.where(place < sources, pick(array, place).astype(jnp.float32), 0.0)
-    for step in range(1, count):
-        pairs = [(i, (i + step) % count) for i in range(min(sources, count))]
-        got = after(lax.ppermute(pick(array, (place + step) % count), "head", pairs), *when)
-        total = total + got.astype(jnp.float32)
-    return total
+        chip = lax.axis_index("wide") // 2
+        self.own = pick(array, chip)
+        self.got = [swapped(pick(array, chip ^ other), "wide", 2 * other) for other in range(1, array.shape[0])]
+
+    def end(self):
+        total = self.own.astype(jnp.float32)
+        for array in self.got:
+            total = total + array.astype(jnp.float32)
+        return total.astype(self.own.dtype)
 
 
 def sum_wide(array):
     return lax.psum_scatter(array, "wide", scatter_dimension=0, tiled=True)
 
 
-def owned(part, sources, when=()):
-    return reduce_head(part.reshape(lax.axis_size("head"), -1, part.shape[1]), sources, when)
+def gather_wide(array):
+    return lax.all_gather(array, "wide", axis=0, tiled=True)
 
 
 class Carried:
@@ -227,18 +259,22 @@
         self.backward = backward
         self.left = wide_bits()
 
-    def step(self, *when):
+    def begin(self):
+        self.got = swapped(self.sent, "wide", self.left[0])
+
+    def end(self):
         bit = self.left.pop(0)
-        got = after(swapped(self.sent, "wide", bit), *when)
         mine = (lax.axis_index("wide") // bit) % 2
         ahead = 1 - mine if self.backward else mine
         self.total, self.state, self.rows, self.sent = join(
-            self.total, self.state, self.rows, got, jnp.reshape(ahead, (1,)).astype(jnp.int32)
+            self.total, self.state, self.rows, self.got, jnp.reshape(ahead, (1,)).astype(jnp.int32)
         )
 
-    def rest(self, *when):
+    def last(self):
+        self.end()
         while self.left:
-            self.step(*when)
+            self.begin()
+            self.end()
         return self.state
 
 
@@ -422,7 +458,7 @@
 
 def gate_back_kernel(
     dym_ref, y_ref, z_ref, bcact_ref, cum_ref, marks_ref, gain_ref, spread_ref, gather_ref,
-    dz_ref, dy_ref, dgain_ref, sent_ref, state_ref, decay_ref,
+    dz_ref, dy_ref, sent_ref, state_ref, decay_ref,
 ):
     part = pl.program_id(0)
     marks = marks_ref[...]
@@ -433,7 +469,6 @@
     scale = lax.rsqrt(gathered(gated * gated, gather_ref) * (2.0 / LANES) + epsilon)
     wide_scale = spread(scale, spread_ref)
     d_normed = dym_ref[...]
-    d_gain = jnp.sum(d_normed * gated * wide_scale, axis=0, keepdims=True)
     u = d_normed * gain_ref[0:1, :]
     inner = gathered(u * gated, gather_ref) * (2.0 / LANES) * scale * scale * scale
     d_gated = u * wide_scale - gated * spread(inner, spread_ref)
@@ -449,13 +484,11 @@
         state_ref[...] = own
         decay_ref[...] = jnp.ones_like(decay_ref)
         decay_ref[0:1, :] = decay
-        dgain_ref[0:1, :] = d_gain
 
     @pl.when(part > 0)
     def _():
         state_ref[...] = state_ref[...] * decay + own
         decay_ref[0:1, :] = decay_ref[0:1, :] * decay
-        dgain_ref[0:1, :] += d_gain
 
     @pl.when(part == pl.num_programs(0) - 1)
     def _():
@@ -730,7 +763,6 @@
         [
             (shape((length, inner), LOW), (CHUNK, inner), "part"),
             (shape((length, inner)), (CHUNK, inner), "part"),
-            (shape((8, inner)), (8, inner), "whole"),
             (shape((n2 // 2 + EXTRA, inner), LOW), (n2 // 2 + EXTRA, inner), "whole"),
             (shape((n2 // 2, inner)), (n2 // 2, inner), "whole"),
             (shape((8, inner)), (8, inner), "whole"),
@@ -815,7 +847,7 @@
     )(ahead, total, state, rows, got)
 
 
-BOTH = 2
+BOTH = 4
 ONES = 16
 
 
@@ -932,10 +964,6 @@
     @pl.when(member == GROUP // BOTH - 1)
     def _():
         dkv_ref[...] = acc_ref[...].astype(LOW)
-
-
-def attend_back_more(place_ref, qb_ref, dot_ref, o_ref, kv_ref, extra_ref, _, *refs):
-    attend_back_kernel(place_ref, qb_ref, dot_ref, o_ref, kv_ref, extra_ref, *refs)
 
 
 def attend_specs(blk, total, group):
@@ -982,19 +1010,17 @@
     )(place, q_rows, masks[0], key_all, masks[1])
 
 
-def attend_back(group, q_back, out, d_rows, key_all, masks, place, d_kv=None):
+def attend_back(group, q_back, out, d_rows, key_all, masks, place):
     blk = d_rows.shape[2]
     total = key_all.shape[0]
     specs = attend_specs(blk, total, group)
-    more = [] if d_kv is None else [d_kv]
     return pl.pallas_call(
-        attend_back_kernel if d_kv is None else attend_back_more,
+        attend_back_kernel,
         grid_spec=pltpu.PrefetchScalarGridSpec(
             num_scalar_prefetch=1,
             grid=(GROUP // BOTH,),
-            in_specs=[specs["own_broad"], specs["narrow"], specs["own_narrow"], specs["kv"], specs["extra"]]
-            + [pl.BlockSpec(memory_space=pl.ANY)] * len(more),
-            out_specs=[specs["own_narrow"], specs["kv"]],
+            in_specs=[specs["own_broad"], specs["narrow"], specs["own_narrow"], specs["kv"], specs["extra"]],
+            out_specs=[specs["own_narrow"], specs["extra"]],
             scratch_shapes=[
                 pltpu.VMEM((total, LANES), LOW),
                 pltpu.VMEM((HEAD_SIZE, total), LOW),
@@ -1003,12 +1029,11 @@
                 pltpu.VMEM((BOTH, HEAD_SIZE, blk), jnp.float32),
             ],
         ),
-        out_shape=[shape((GROUP, HEAD_SIZE, blk), LOW), shape((total, key_all.shape[1]), LOW)],
-        input_output_aliases={6: 1} if more else {},
+        out_shape=[shape((GROUP, HEAD_SIZE, blk), LOW), shape((total, LANES), LOW)],
         compiler_params=pltpu.CompilerParams(vmem_limit_bytes=60 * 2**20),
         cost_estimate=guess(27),
         name="attend_back",
-    )(place, q_back, d_rows, out, key_all, masks[1], *more)
+    )(place, q_back, d_rows, out, key_all, masks[1])
 
 
 PIECE = 256
@@ -1086,6 +1111,36 @@
         cost_estimate=guess(8),
         name="last_grads",
     )(x, d_scan, d_query, d_kv, small)
+
+
+def input_back_kernel(scan_ref, gate_ref, query_ref, kv_ref, w_ref, x_ref, more_ref, gain_ref, dx_ref):
+    at, total = 0, None
+    for ref in (scan_ref, gate_ref, query_ref, kv_ref):
+        term = nt(ref[...], w_ref[:, at : at + ref.shape[1]])
+        total = term if total is None else total + term
+        at += ref.shape[1]
+    x = x_ref[...]
+    scale = lax.rsqrt(jnp.mean(x * x, axis=1, keepdims=True) + epsilon)
+    u = total * gain_ref[...]
+    inner = jnp.mean(u * x, axis=1, keepdims=True) * scale * scale * scale
+    dx_ref[...] = (more_ref[...] + u * scale - x * inner).astype(LOW)
+
+
+def input_back(d_scan, d_gate, d_query, d_kv, w, x, more, gain):
+    tokens, width = x.shape
+    part = min(2 * CHUNK, tokens)
+    rows = lambda array: pl.BlockSpec((part, array.shape[1]), lambda i: (i, 0))
+    whole = lambda array: pl.BlockSpec(array.shape, lambda i: (0, 0))
+    return pl.pallas_call(
+        input_back_kernel,
+        grid=(tokens // part,),
+        in_specs=[rows(a) for a in (d_scan, d_gate, d_query, d_kv)] + [whole(w), rows(x), rows(more), whole(gain)],
+        out_specs=rows(x),
+        out_shape=shape((tokens, width), LOW),
+        compiler_params=pltpu.CompilerParams(vmem_limit_bytes=56 * 2**20),
+        cost_estimate=guess(10),
+        name="input_back",
+    )(d_scan, d_gate, d_query, d_kv, w, x, more, gain)
 
 
 def tap_marks(starts, first, length, taps):
@@ -1192,17 +1247,15 @@
     in_shard = jnp.concatenate(
         [mamba_in_w, mamba_bc_w, mamba_dt_w, small, pad, mamba_gate_w, attn_q_w, attention_key_value_weight], axis=1
     )
-    in_rows = gather_head(in_shard, micro_count)
-    w_in = lax.all_gather(in_rows, "wide", axis=0, tiled=True)
-    x_low = to_blocks(after(mixed(hidden_in[:, 0]), in_rows))
-    gy_pieces = cotangent[:, 0]
     to_width = mixed(jnp.concatenate([ffn_down_w, mamba_out_w, attn_out_w], axis=0)).reshape(-1, rows, width)
     gate_folds, up_folds = folded(ffn_gate_w), folded(ffn_up_w)
-    late_parts = []
+    ffn_shard = []
     for i in range(folds):
-        late_parts += [gate_folds[:, i], up_folds[:, i], to_width[i]]
-    late_parts += [to_width[i] for i in range(folds, to_width.shape[0])]
-    late_shard = after(jnp.concatenate(late_parts, axis=1), x_low)
+        ffn_shard += [gate_folds[:, i], up_folds[:, i], to_width[i]]
+    ffn_shard = jnp.concatenate(ffn_shard, axis=1)
+    out_shard = jnp.concatenate([to_width[i] for i in range(folds, to_width.shape[0])], axis=1)
+    x_pieces = mixed(hidden_in[:, 0])
+
     micro = jnp.minimum(lax.axis_index("head"), micro_count - 1)
     starts = pick(doc_starts, micro)
     block_base = wide_id * block_tok
@@ -1213,9 +1266,17 @@
     bias_row = lanes_row(dt_bias)
     rate_row = lanes_row(-jnp.exp(a_log))
     skip_row = jnp.repeat(d_skip, inner // heads)[None]
-    x_low, marks, docs_row, masks, mats, bias_row, rate_row, skip_row = lax.optimization_barrier(
-        (x_low, marks, docs_row, masks, mats, bias_row, rate_row, skip_row)
-    )
+    in_rows = HeadRows(in_shard, micro_count)
+    prepared = (marks, docs_row, masks, mats, bias_row, rate_row, skip_row, ffn_shard, out_shard, x_pieces)
+    in_rows.got, prepared = tied(in_rows.got, prepared)
+    marks, docs_row, masks, mats, bias_row, rate_row, skip_row, ffn_shard, out_shard, x_pieces = prepared
+    in_rows, out_shard = tied(in_rows.end(), out_shard)
+    w_in = gather_wide(in_rows)
+    out_rows_all, x_pieces = tied(HeadRows(out_shard, micro_count).end(), x_pieces)
+    x_low, ffn_shard = tied(ToBlocks(x_pieces).end(), ffn_shard)
+    ffn_rows = HeadRows(ffn_shard, micro_count)
+    w_in, out_rows_all = tied(w_in, out_rows_all)
+    w_out = gather_wide(out_rows_all)
     x_tokens = x_low.astype(jnp.float32)
 
     small_at = scan_cols + heads
@@ -1239,66 +1300,80 @@
     place = jnp.reshape(wide_id, (1,)).astype(jnp.int32)
 
 
-    normed_in, pull_in = jax.vjp(rms_scale, x_tokens, gain_in_all)
-    block_in = normed_in.astype(LOW)
-    raw_qkv = nn(block_in, w_qkv).astype(LOW)
+    block_in = rms_scale(x_tokens, gain_in_all).astype(LOW)
+    raw_qkv, block_in = tied(nn(block_in, w_qkv).astype(LOW), block_in)
     keys = Gathered(raw_qkv[:, query_cols:])
-    raw_scan = nn(after(block_in, raw_qkv), w_scan)
+    keys.begin()
+    keys.got, raw_scan, block_in = tied(keys.got, nn(block_in, w_scan), block_in)
+    keys.end()
     rim = shifted(raw_scan[block_tok - 8 :, :scan_cols], "wide", 1)
+    keys.begin()
+    rim, raw_gate = tied(rim, nn(block_in, w_gate))
     rim = jnp.where(jnp.arange(8)[:, None] > 8 - taps, rim, 0.0)
-    raw_gate = nn(after(block_in, raw_scan), w_gate)
-    keys.step()
     taps_ext = jnp.pad(taps_all, ((0, 8 - taps), (0, 0)))
-    *feats, sent, total, decay_rows = mamba_local(
-        raw_scan, after(rim, *keys.parts), marks, taps_ext, bias_row, rate_row, cols, mats
-    )
-    late_rows = gather_head(late_shard, micro_count, (sent,))
-    w_late = lax.all_gather(late_rows, "wide", axis=0, tiled=True)
+    *feats, sent, total, decay_rows = mamba_local(raw_scan, rim, marks, taps_ext, bias_row, rate_row, cols, mats)
+    keys.got, ffn_rows.got, sent = tied(keys.got, ffn_rows.got, sent)
+    ffn_rows, w_out = tied(ffn_rows.end(), w_out)
+    w_ffn = gather_wide(ffn_rows)
+    keys.end()
+    forward = Carried(sent, total, decay_rows, False)
+    forward.begin()
+    key_all = keys.rest()
+    forward.end()
     q_rows = raw_qkv[:, :query_cols].T.reshape(QUERY_HEADS, HEAD_SIZE, block_tok)
-    key_all = keys.rest()
-    forward = Carried(sent, total, decay_rows, False)
-    forward.step()
-    out_0, q_back_0 = attend(0, after(q_rows, forward.sent), key_all, masks, place)
-    forward.step(out_0)
-    out_1, q_back_1 = attend(1, after(q_rows, forward.sent, out_0), key_all, masks, place)
+    gy = ToBlocks(cotangent[:, 0])
+    forward.begin()
+    out_0, q_back_0 = attend(0, q_rows, key_all, masks, place)
+    forward.got, gy.got, out_0, q_rows = tied(forward.got, gy.got, out_0, q_rows)
+    forward.end()
+    forward.sent, q_rows = tied(forward.sent, q_rows)
+    forward.begin()
+    out_1, q_back_1 = attend(1, q_rows, key_all, masks, place)
+    forward.got, out_1 = tied(forward.got, out_1)
+    state_in = forward.last()
     attn_low = jnp.concatenate([out_0, out_1], axis=0).reshape(query_cols, block_tok).astype(LOW)
-    mamba_low, y_low, entry = mamba_mix(
-        feats, raw_gate, marks, docs_row, forward.rest(out_1), skip_row, gain_mamba_row, mats
-    )
-    gy_plain = to_blocks(after(gy_pieces, raw_scan), (out_0,))
+    mamba_low, y_low, entry = mamba_mix(feats, raw_gate, marks, docs_row, state_in, skip_row, gain_mamba_row, mats)
+    gy_plain = gy.end()
     d_out_low = mixed(gy_plain)
-    out_at = 3 * hidden
     out_both = jnp.concatenate(
-        [w_late[:, i : i + width].reshape(devices, rows, width) for i in range(out_at, w_late.shape[1], width)], axis=1
+        [w_out[:, i : i + width].reshape(devices, rows, width) for i in range(0, w_out.shape[1], width)], axis=1
     )
     out_both = by_owner(out_both)
     w_mamba_out = out_both[:, :out_rows].reshape(-1, width)
     w_attn_out = out_both[:, out_rows:].reshape(-1, width)
 
     resid = x_tokens + nn(mamba_low, w_mamba_out) + tn(attn_low, w_attn_out)
-    normed_ffn, pull_ffn = jax.vjp(rms_scale, resid, gain_ffn_all)
+    normed_ffn, pull_ffn = jax.vjp(lambda values: rms_scale(values, gain_ffn_all), resid)
     ffn_in = normed_ffn.astype(LOW)
-    fed, d_ffn_in, grad_ffn = feed_forward(ffn_in, d_out_low, gy_plain, w_late, folds, width)
+    fed, d_ffn_in, grad_ffn = feed_forward(ffn_in, d_out_low, gy_plain, w_ffn, folds, width)
     part_ffn = sum_wide(grad_ffn)
-    d_resid_norm, grad_gain_ffn = pull_ffn(d_ffn_in)
+    (d_resid_norm,) = pull_ffn(d_ffn_in)
     d_resid = d_out_low.astype(jnp.float32) + d_resid_norm
 
     d_mix = d_resid.astype(LOW)
-    d_gate_z, dy_low, grad_gain_m, sent_back, total, decay_rows = mamba_gate_back(
+    d_gate_z, dy_low, sent_back, total, decay_rows = mamba_gate_back(
         nt(d_mix, w_mamba_out), y_low, raw_gate, feats, marks, gain_mamba_row, mats
     )
     backward = Carried(sent_back, total, decay_rows, True)
-    backward.step()
-    d_attn = nt(w_attn_out, after(d_mix, backward.sent)).astype(LOW).reshape(QUERY_HEADS, HEAD_SIZE, block_tok)
+    backward.begin()
+    d_attn = nt(w_attn_out, d_mix).astype(LOW).reshape(QUERY_HEADS, HEAD_SIZE, block_tok)
+    backward.got, d_attn = tied(backward.got, d_attn)
+    backward.end()
+    backward.sent, d_attn = tied(backward.sent, d_attn)
+    backward.begin()
     d_query_0, d_kv_0 = attend_back(0, q_back_0, out_0, d_attn, key_all, masks, place)
-    backward.step(d_query_0)
-    d_query_1, d_kv_all = attend_back(
-        1, q_back_1, out_1, after(d_attn, backward.sent, d_kv_0), key_all, masks, place, d_kv_0
-    )
-    d_kv_sum = Reduced(d_kv_all.reshape(-1, 2, block_tok // 2, kv_cols).swapaxes(0, 1))
-    d_kv_sent = d_kv_sum.begin()
+    backward.got, d_query_0, d_kv_0, d_attn = tied(backward.got, d_query_0, d_kv_0, d_attn)
+    backward.end()
+    backward.sent, d_attn, d_kv_0 = tied(backward.sent, d_attn, d_kv_0)
+    backward.begin()
+    core_0 = CoreSum(d_kv_0)
+    d_query_1, d_kv_1 = attend_back(1, q_back_1, out_1, d_attn, key_all, masks, place)
+    backward.got, core_0.got, d_query_1, d_kv_1 = tied(backward.got, core_0.got, d_query_1, d_kv_1)
+    d_state = backward.last()
+    d_state, d_kv_1, d_mix = tied(d_state, d_kv_1, d_mix)
+    core_1 = CoreSum(d_kv_1)
     d_query = jnp.concatenate([d_query_0, d_query_1], axis=0).reshape(query_cols, block_tok).T
-    d_mix_plain = plain(after(d_mix, *d_kv_sent))
+    d_mix_plain = plain(d_mix)
     grad_out = jnp.concatenate(
         [
             tn(mamba_low, d_mix_plain).astype(LOW).reshape(devices, out_rows, width),
@@ -1307,28 +1382,30 @@
         axis=1,
     ).reshape(devices, -1, rows, width)
     grad_out = by_place(grad_out)
-    grad_gate = tn(after(block_in, *d_kv_sent), d_gate_z).astype(LOW)
+    grad_gate = tn(block_in, d_gate_z).astype(LOW)
     early = jnp.concatenate(
         [grad_out[:, i].reshape(width, width) for i in range(grad_out.shape[1])] + [grad_gate], axis=1
     )
-    d_kv_sum.end(early)
-    d_kv_sent = d_kv_sum.begin()
-    part_early = sum_wide(after(early, part_ffn))
-    d_state = backward.rest(early)
+    core_1.got, early = tied(core_1.got, early)
+    chip_sum = ChipSum(jnp.concatenate([core_0.end(), core_1.end()], axis=2))
+    early, part_ffn = tied(early, part_ffn)
+    part_early = sum_wide(early)
+    out_plain = plain((resid + fed).astype(LOW))
+    own_ffn = HeadSum(part_ffn, micro_count)
     d_scan, grad_skip, grad_head, grad_taps, rim_back, edge = mamba_scan_back(
-        feats, raw_scan, rim, taps_ext, marks, docs_row, dy_low, entry, after(d_state, part_ffn, *d_kv_sent),
+        feats, raw_scan, rim, taps_ext, marks, docs_row, dy_low, entry, d_state,
         skip_row, bias_row, rate_row, cols, mats,
     )
-    d_kv_sum.end(d_scan)
-    own_ffn = owned(part_ffn, micro_count, (d_scan,))
-    d_kv = d_kv_sum.rest().reshape(block_tok, kv_cols)
+    chip_sum.got, own_ffn.got, d_scan, edge, rim_back, grad_taps, grad_head, grad_skip, d_query, out_plain = tied(
+        chip_sum.got, own_ffn.got, d_scan, edge, rim_back, grad_taps, grad_head, grad_skip, d_query, out_plain
+    )
     rim_came = shifted(rim_back, "wide", -1)
+    out_back = FromBlocks(out_plain, micro_count)
+    d_kv = chip_sum.end()
+    own_ffn = own_ffn.end()
     d_scan = lax.dynamic_update_slice(d_scan, (edge + rim_came).astype(LOW), (block_tok - 8, 0))
     grad_small = jnp.concatenate(
         [
-            jnp.zeros((devices, rows), jnp.float32),
-            grad_gain_ffn.reshape(devices, rows),
-            by_place(grad_gain_m[0].reshape(devices, chan)),
             by_place(grad_taps[:taps, :inner].reshape(taps, devices, chan).transpose(1, 0, 2).reshape(devices, -1)),
             by_place(grad_taps[:taps, inner:].reshape(taps, devices, chan_bc).transpose(1, 0, 2).reshape(devices, -1)),
         ],
@@ -1338,38 +1415,71 @@
     grad_small = jnp.pad(
         grad_small.reshape(width, small_cols), ((0, 0), (heads, LANES - heads - small_cols))
     )
-    late = last_grads(after(block_in, own_ffn), d_scan, d_query, d_kv, grad_small)
-
-    d_late = after(jnp.concatenate([d_query, d_kv], axis=1), late)
-    d_x_norm, grad_gain_in = pull_in(nt(d_gate_z, w_gate) + nt(d_late, w_qkv) + nt(d_scan, w_scan))
-    grad_x = (d_resid + d_x_norm).astype(LOW)
-    part_late = sum_wide(after(late, part_early))
-    own_early = owned(after(part_early, late), micro_count, (grad_x,))
-    results = from_blocks(
-        jnp.concatenate([plain((resid + fed).astype(LOW)), plain(grad_x)], axis=1), micro_count
-    )
-    summed = sum_everywhere(
-        jnp.concatenate(
-            [grad_head[:2, :heads].reshape(-1), jnp.sum(grad_skip[0].reshape(heads, -1), axis=1), grad_gain_in]
-        )
-    )
+    late = last_grads(block_in, d_scan, d_query, d_kv, grad_small)
+
+    head_sums = jnp.concatenate(
+        [grad_head[:2, :heads].reshape(-1), jnp.sum(grad_skip[0].reshape(heads, -1), axis=1)]
+    )
+    out_back.got, late, part_early, d_scan, own_ffn, head_sums = tied(
+        out_back.got, late, part_early, d_scan, own_ffn, head_sums
+    )
+    part_late = sum_wide(late)
+    totals = EverySum(head_sums)
+    totals.begin()
+    totals.got, part_early, d_scan = tied(totals.got, part_early, d_scan)
+    totals.end()
+    own_early = HeadSum(part_early, micro_count)
+    totals.begin()
+    grad_x = input_back(d_scan, d_gate_z, d_query, d_kv, w_in, x_tokens, d_resid, gain_in_all[None])
+    own_early.got, own_early.own, totals.got, grad_x = tied(own_early.got, own_early.own, totals.got, grad_x)
+    totals.end()
+    x_plain, own_ffn = tied(plain(grad_x), own_ffn)
+    x_back = FromBlocks(x_plain, micro_count)
+    totals.begin()
+    g_ffn = split_at(own_ffn, (width,) * (3 * folds), 1)
+    g_gate_w, g_up_w = unfolded(g_ffn[0::3]), unfolded(g_ffn[1::3])
+    totals.got, g_gate_w, g_up_w = tied(totals.got, g_gate_w, g_up_w)
+    totals.end()
+    totals.begin()
+    x_back.got, own_early.got, own_early.own, part_late, totals.got, g_gate_w, g_up_w = tied(
+        x_back.got, own_early.got, own_early.own, part_late, totals.got, g_gate_w, g_up_w
+    )
+    totals.end()
+    own_late = HeadSum(part_late, micro_count)
+    summed = totals.rest()
+    results = x_back.end()
+    own_late.got, results = tied(own_late.got, results)
     per_head = summed[: 3 * heads].reshape(3, heads)
-    inside_place = wide_id * heads_dev + lax.axis_index("head")
-    o_gain_in = lax.dynamic_slice_in_dim(summed[3 * heads :], inside_place * rows, rows)
-    own_late = owned(part_late, micro_count)
-
-    g_x, g_bc, g_dt, g_small, _, g_q, g_kv = split_at(
-        own_late, (inner, bc_cols, heads, small_cols, LANES - heads - small_cols, query_cols, kv_cols), 1
-    )
-    *g_out, g_gate = split_at(own_early, (width,) * ((out_rows + attn_rows) // rows) + (inner,), 1)
-    _, o_gain_ffn, o_gain_m, o_conv_x, o_conv_bc = split_at(
-        g_small.reshape(-1), (rows, rows, chan, taps * chan, taps * chan_bc), 0
+    g_x, g_bc, g_dt, g_small, _, g_q, g_kv = own_late.end(
+        (inner, bc_cols, heads, small_cols, LANES - heads - small_cols, query_cols, kv_cols)
+    )
+    *g_out, g_gate = own_early.end((width,) * ((out_rows + attn_rows) // rows) + (inner,))
+    o_conv_x, o_conv_bc, _ = split_at(
+        g_small.reshape(-1), (taps * chan, taps * chan_bc, rows * small_cols - taps * (chan + chan_bc)), 0
     )
     g_mamba_out, g_attn_out = split_at(jnp.concatenate(g_out, axis=0), (out_rows, attn_rows), 0)
-    g_ffn = split_at(own_ffn, (width,) * (3 * folds), 1)
+    def gain_grad(gain, pairs):
+        total = 0.0
+        for weight, grad in pairs:
+            total = total + jnp.sum(weight.astype(jnp.float32) * grad, axis=1)
+        return total / gain.astype(jnp.float32)
+
+    o_gain_in = gain_grad(
+        gain_in,
+        (
+            (mamba_in_w, g_x),
+            (mamba_bc_w, g_bc),
+            (mamba_dt_w, g_dt),
+            (mamba_gate_w, g_gate),
+            (attn_q_w, g_q),
+            (attention_key_value_weight, g_kv),
+        ),
+    )
+    o_gain_ffn = gain_grad(gain_ffn, ((ffn_gate_w, g_gate_w), (ffn_up_w, g_up_w)))
+    o_gain_m = gain_grad(mamba_gain, ((mamba_out_w, g_mamba_out),))
     return (
-        results[:, None, :, :width],
-        results[:, None, :, width:],
+        out_back.end()[:, None],
+        results[:, None],
         o_gain_in,
         g_gate,
         g_x,
@@ -1386,8 +1496,8 @@
         g_mamba_out,
         g_attn_out,
         o_gain_ffn,
-        unfolded(g_ffn[0::3]),
-        unfolded(g_ffn[1::3]),
+        g_gate_w,
+        g_up_w,
         jnp.concatenate(g_ffn[2::3], axis=0),
     )
 

time: 621 us -> 554 us (0.89)
  waiting for transfers between devices: 195 us -> 127 us
  Pallas kernels: 124 us -> 137 us
  matrix products: 58.3 us -> 48.3 us
  local copies, waits for them, and re-layouts: 75.8 us -> 67.1 us
    ppermute x24 -> x30, waiting for transfers between devices: 75.3 us -> 52.4 us  [sent_on(): got.append(lax.ppermute(pieces((place + step) % count), 'head', pairs))]
    ppermute x21, waiting for transfers between devices: 63.8 us -> 45.6 us  [swapped(): return lax.ppermute(value, axis, [(i, i ^ bit) for i in range(count)])]
    reduce_scatter x3, waiting for transfers between devices: 27.7 us -> 13.5 us  [sum_wide(): return lax.psum_scatter(array, 'wide', scatter_dimension=0, tiled=True)]
    all_gather x2 -> x3, waiting for transfers between devices: 28 us -> 15.8 us  [gather_wide(): return lax.all_gather(array, 'wide', axis=0, tiled=True)]
    dot_general x8 -> x5, matrix products: 25.5 us -> 13.6 us  [nt(): lax.dot_general(left, right, (((1,), (1,)), ((), ())), preferred_element_...]
    pallas_call x2 -> x3, Pallas kernels: 14.5 us -> 25.9 us  [the longest x2 13.8 us: attend_back(): pl.pallas_call(attend_back_kernel, grid_spec=pltpu.PrefetchScalarGridSpec...]
    ppermute x24 -> x30, starting transfers between devices: 66.5 us -> 76.8 us  [sent_on(): got.append(lax.ppermute(pieces((place + step) % count), 'head', pairs))]
    dynamic_update_slice x17 -> x25, local copies, waits for them, and re-layouts: 6.92 us -> 13.3 us  [the longest x21 12.1 us: put_together(): lax.dynamic_update_index_in_dim(whole, array, (place - step) % count, 0)]
  transfers between devices with their start and end apart: 52 -> 59, of which waited for: 24 -> 20; matrix products, arithmetic and copies ran while one was open for 20% -> 23% of each run, Pallas kernels for 15% -> 19%
where the time goes in v2:
time: 554 us; the launch traced here: 545 us
  Pallas kernels  137 us (25%)
  waiting for transfers between devices  127 us (23%)
  starting transfers between devices  109 us (20%)
  local copies, waits for them, and re-layouts  67.1 us (12%)
  matrix products  48.3 us (9%)
  other arithmetic  40 us (7%)
  between operations  16.6 us (3%)
    ppermute x30, starting transfers between devices, sent_on(): got.append(lax.ppermute(pieces((place + step) % count), 'head', pairs))  76.8 us
    pallas_call x4, Pallas kernels, call(): pl.pallas_call(kernel, grid=(parts,), in_specs=[spec(block, how) for _, b...  58.7 us
    ppermute x30, waiting for transfers between devices, sent_on(): got.append(lax.ppermute(pieces((place + step) % count), 'head', pairs))  52.4 us
    ppermute x21, waiting for transfers between devices, swapped(): return lax.ppermute(value, axis, [(i, i ^ bit) for i in range(count)])  45.6 us
    pallas_call x1, Pallas kernels, feed_forward(): pl.pallas_call(feed_kernel, grid=(folds,), in_specs=[whole, whole, whole,...  30.3 us
    ppermute x21, starting transfers between devices, swapped(): return lax.ppermute(value, axis, [(i, i ^ bit) for i in range(count)])  29 us
    dot_general x12, matrix products, nn(): return jnp.dot(left, right, preferred_element_type=jnp.float32)  28.6 us
    unnamed x189, local copies, waits for them, and re-layouts  16.1 us
  transfers between devices with their start and end apart: 59, of which 20 were waited for; matrix products, arithmetic and copies ran while one was open for 23% of the time, Pallas kernels for 19%

profile of v2, /device:TPU:24, one launch (start us, length us, event | category | flops | bytes accessed | tf_op | source)
XLA Modules:
  0.0 545.0 jit_solution(12054609444423036826)
XLA Ops:
  55.4 6.7 %collective-permute-start.6 = (bf16[128,1024]{1,0:T(8,128)(2,1)S(1)}, bf16[128,1024]{1,0:T(8,128)(2,1)S(1)}, u32[]{:S(2)}, u32[]{:S(2)}) collective-permute-start(bf16[128,1024]{1,0:T(8,128)(2,1)S(1)} %get-tuple-element.553), channel_id=1, source_target_pairs={{0,8},{8,16},{24,0},{1,9},{9,17},{25,1},{2,10},{10,18},{26,2},{3,1... | collective-permute-start | bytes 786440 | tf_op jit(solution)/shard_map/ppermute | solution.py:78
  78.0 7.5 %collective-permute-start.14 = (bf16[32,6144]{1,0:T(8,128)(2,1)}, bf16[32,6144]{1,0:T(8,128)(2,1)}, u32[]{:S(2)}, u32[]{:S(2)}) collective-permute-start(bf16[32,6144]{1,0:T(8,128)(2,1)} %get-tuple-element.220), channel_id=1, source_target_pairs={{0,8},{8,16},{24,0},{1,9},{9,17},{25,1},{2,10},{10,18},{26,2},{3,1... | collective-permute-start | bytes 1179656 | tf_op jit(solution)/shard_map/ppermute | solution.py:78
  85.5 6.1 %collective-permute-start.15 = (bf16[32,6144]{1,0:T(8,128)(2,1)}, bf16[32,6144]{1,0:T(8,128)(2,1)}, u32[]{:S(2)}, u32[]{:S(2)}) collective-permute-start(bf16[32,6144]{1,0:T(8,128)(2,1)} %get-tuple-element.220), channel_id=1, source_target_pairs={{0,16},{16,0},{24,8},{1,17},{17,1},{25,9},{2,18},{18,2},{26,10},{3... | collective-permute-start | bytes 1179656 | tf_op jit(solution)/shard_map/ppermute | solution.py:78
  127.3 10.9 %mamba_local.1 = (f32[512,1536]{1,0:T(8,128)}, bf16[512,1536]{1,0:T(8,128)(2,1)}, bf16[512,256]{1,0:T(8,128)(2,1)}, bf16[512,256]{1,0:T(8,128)(2,1)}, f32[512,12...) custom-call(f32[512,1920]{1,0:T(8,128)} %copy-done.80, ...), custom_call_target="tpu_custom_call" | custom-call | flops 11000000512 | bytes 33000000 | tf_op jit(solution)/shard_map/mamba_local/pallas_call | solution.py:652
  174.0 11.2 %collective-permute-done.18.got_ref = bf16[144,1536]{1,0:T(8,128)(2,1)S(1)} collective-permute-done((bf16[144,1536]{1,0:T(8,128)(2,1)S(1)}, bf16[144,1536]{1,0:T(8,128)(2,1)S(1)}, u32[]{:S(2)}, u32[]{:S(2)}) %collective-permute-start.18) | collective-permute-done | bytes 442400 | tf_op jit(solution)/shard_map/ppermute | solution.py:56
  196.9 6.1 %collective-permute-done.23.got_ref = bf16[144,1536]{1,0:T(8,128)(2,1)S(1)} collective-permute-done((bf16[144,1536]{1,0:T(8,128)(2,1)S(1)}, bf16[144,1536]{1,0:T(8,128)(2,1)S(1)}, u32[]{:S(2)}, u32[]{:S(2)}) %collective-permute-start.23) | collective-permute-done | bytes 442400 | tf_op jit(solution)/shard_map/ppermute | solution.py:56
  205.6 11.2 %mamba_mix.1 = (bf16[512,1536]{1,0:T(8,128)(2,1)}, f32[512,1536]{1,0:T(8,128)}, bf16[4,128,1536]{2,1,0:T(8,128)(2,1)}) custom-call(f32[512,1536]{1,0:T(8,128)} %get-tuple-element.232.act_ref, bf16[512,256]{1,0:T(8,128)(2,1)} %get-tuple-element.233.bcact_ref, f32[512,1536]{1,0:T(8,128)} %fusion.26.z_ref, f32[512,128]{1,0:T(8,128)} %get-tuple-element.235.step_ref, ...), custom_call_target="tpu_custom_call" | custom-call | flops 11000000512 | bytes 33000000 | tf_op jit(solution)/shard_map/mamba_mix/pallas_call | solution.py:652
  225.6 7.8 %all-gather.8.cloned.1.call-done.w_ref = bf16[1024,6144]{1,0:T(8,128)(2,1)} async-done(((bf16[128,6144]{1,0:T(8,128)(2,1)}), bf16[1024,6144]{1,0:T(8,128)(2,1)}) %all-gather.8.cloned.1.call-update) | async-done | bytes 12582928 | tf_op jit(solution)/shard_map/all_gather | solution.py:252
  233.4 30.3 %feed_forward.1 = (f32[512,1024]{1,0:T(8,128)}, f32[512,1024]{1,0:T(8,128)}, bf16[1024,6144]{1,0:T(8,128)(2,1)}) custom-call(bf16[512,1024]{1,0:T(8,128)(2,1)} %multiply_convert_fusion.x_ref, bf16[512,1024]{1,0:T(8,128)(2,1)} %fusion.43.gy_ref, bf16[512,1024]{1,0:T(8,128)(2,1)} %bitcast.331, bf16[1024,6144]{1,0:T(8,128)(2,1)} %all-gather.8.cloned.1.call-done.w_ref), custom_call_target="tpu_custom_call" | custom-call | flops 35000000512 | bytes 105000000 | tf_op jit(solution)/shard_map/feed_forward/pallas_call | solution.py:1077
  272.5 12.5 %mamba_gate_back.1 = (bf16[512,1536]{1,0:T(8,128)(2,1)}, f32[512,1536]{1,0:T(8,128)}, bf16[144,1536]{1,0:T(8,128)(2,1)}, f32[128,1536]{1,0:T(8,128)}, f32[8,1536]{1,0:T(8,128)}) custom-call(f32[512,1536]{1,0:T(8,128)} %fusion.171.dym_ref, f32[512,1536]{1,0:T(8,128)} %get-tuple-element.264.y_ref, f32[512,1536]{1,0:T(8,128)} %fusion.26.z_ref, ...), custom_call_target="tpu_custom_call" | custom-call | flops 11000000512 | bytes 33000000 | tf_op jit(solution)/shard_map/mamba_gate_back/pallas_call | solution.py:652
  292.9 7.2 %attend_back.2 = (bf16[4,64,512]{2,1,0:T(8,128)(2,1)}, bf16[4096,128]{1,0:T(8,128)(2,1)}) custom-call(s32[1]{0:T(128)} %bitcast.56.place_ref, bf16[4,128,512]{2,1,0:T(8,128)(2,1)} %get-tuple-element.275.qb_ref, bf16[8,64,512]{2,1,0:T(8,128)(2,1)} %bitcast.369, f32[4,64,512]{2,1,0:T(8,128)} %get-tuple-element.260.o_ref, bf16[4096,256]{1,0:T(8,128)(2,1)} %bitcast.321, ...), custom_call_target="tpu_custom_call" | custom-call | flops 27000000512 | bytes 81000000 | tf_op jit(solution)/shard_map/attend_back/pallas_call | solution.py:1017
  300.1 11.6 %collective-permute-done.25.got_ref = bf16[144,1536]{1,0:T(8,128)(2,1)S(1)} collective-permute-done((bf16[144,1536]{1,0:T(8,128)(2,1)S(1)}, bf16[144,1536]{1,0:T(8,128)(2,1)S(1)}, u32[]{:S(2)}, u32[]{:S(2)}) %collective-permute-start.25) | collective-permute-done | bytes 442400 | tf_op jit(solution)/shard_map/ppermute | solution.py:56
  313.1 5.9 %collective-permute-start.26 = (bf16[144,1536]{1,0:T(8,128)(2,1)S(1)}, bf16[144,1536]{1,0:T(8,128)(2,1)S(1)}, u32[]{:S(2)}, u32[]{:S(2)}) collective-permute-start(bf16[144,1536]{1,0:T(8,128)(2,1)S(1)} %get-tuple-element.284), channel_id=1, source_target_pairs={{0,4},{1,5},{2,6},{3,7},{4,0},{5,1},{6,2},{7,3},{8,12},{9,13},{10,... | collective-permute-start | bytes 1327112 | tf_op jit(solution)/shard_map/ppermute | solution.py:56
  319.0 6.6 %attend_back.3 = (bf16[4,64,512]{2,1,0:T(8,128)(2,1)}, bf16[4096,128]{1,0:T(8,128)(2,1)}) custom-call(s32[1]{0:T(128)} %bitcast.56.place_ref, bf16[4,128,512]{2,1,0:T(8,128)(2,1)} %get-tuple-element.285.qb_ref, bf16[8,64,512]{2,1,0:T(8,128)(2,1)} %bitcast.370, f32[4,64,512]{2,1,0:T(8,128)} %get-tuple-element.261.o_ref, bf16[4096,256]{1,0:T(8,128)(2,1)} %bitcast.322, ...), custom_call_target="tpu_custom_call" | custom-call | flops 27000000512 | bytes 81000000 | tf_op jit(solution)/shard_map/attend_back/pallas_call | solution.py:1017
  325.6 13.6 %collective-permute-done.26.got_ref = bf16[144,1536]{1,0:T(8,128)(2,1)S(1)} collective-permute-done((bf16[144,1536]{1,0:T(8,128)(2,1)S(1)}, bf16[144,1536]{1,0:T(8,128)(2,1)S(1)}, u32[]{:S(2)}, u32[]{:S(2)}) %collective-permute-start.26) | collective-permute-done | bytes 442400 | tf_op jit(solution)/shard_map/ppermute | solution.py:56
  353.1 13.5 %reduce-scatter.4.cloned.1.call-done = bf16[128,6144]{1,0:T(8,128)(2,1)} async-done(((bf16[1024,6144]{1,0:T(8,128)(2,1)}), bf16[128,6144]{1,0:T(8,128)(2,1)}) %reduce-scatter.4.cloned.1.call-update) | async-done | bytes 1572880 | tf_op jit(solution)/shard_map/reduce_scatter | solution.py:248
  382.8 24.0 %mamba_scan_back.1 = (bf16[512,1920]{1,0:T(8,128)(2,1)}, f32[8,1536]{1,0:T(8,128)}, f32[8,128]{1,0:T(8,128)}, f32[8,1792]{1,0:T(8,128)}, f32[8,1792]{1,0:T(8,128)}, /*index=5*/f32[8,1792]{1,0:T(8,128)}) custom-call(f32[512,1536]{1,0:T(8,128)} %get-tuple-element.232.act_ref, bf16[512,1536]{1,0:T(8,128)(2,1)} %get-tuple-element.303.slope_ref, ...), custom_call_target="tpu_custom_call" | custom-call | flops 23000000512 | bytes 69000000 | tf_op jit(solution)/shard_map/mamba_scan_back/pallas_call | solution.py:652
  408.0 6.1 %collective-permute-done.33 = bf16[32,6144]{1,0:T(8,128)(2,1)} collective-permute-done((bf16[32,6144]{1,0:T(8,128)(2,1)}, bf16[32,6144]{1,0:T(8,128)(2,1)}, u32[]{:S(2)}, u32[]{:S(2)}) %collective-permute-start.33) | collective-permute-done | bytes 393248 | tf_op jit(solution)/shard_map/ppermute | solution.py:78
  428.6 7.9 %last_grads.1 = bf16[1024,2688]{1,0:T(8,128)(2,1)} custom-call(bf16[512,1024]{1,0:T(8,128)(2,1)} %copy-done.30, bf16[512,1920]{1,0:T(8,128)(2,1)} %fusion.106.scan_ref, bf16[512,512]{1,0:T(8,128)(2,1)} %bitcast.344, bf16[512,256]{1,0:T(8,128)(2,1)} %fusion.60.kv_ref, f32[1024,128]{1,0:T(8,128)} %pad.33.small_ref), custom_call_target="tpu_custom_call" | custom-call | flops 8000000000 | bytes 24000000 | tf_op jit(solution)/shard_map/last_grads/pallas_call | solution.py:1107
  436.5 9.4 %collective-permute-done.36 = bf16[128,1024]{1,0:T(8,128)(2,1)} collective-permute-done((bf16[128,1024]{1,0:T(8,128)(2,1)}, bf16[128,1024]{1,0:T(8,128)(2,1)}, u32[]{:S(2)}, u32[]{:S(2)}) %collective-permute-start.36) | collective-permute-done | bytes 262176 | tf_op jit(solution)/shard_map/ppermute | solution.py:78
  458.4 12.1 %input_back.1 = bf16[512,1024]{1,0:T(8,128)(2,1)} custom-call(bf16[512,1920]{1,0:T(8,128)(2,1)} %fusion.106.scan_ref, bf16[512,1536]{1,0:T(8,128)(2,1)} %get-tuple-element.298.gate_ref, bf16[512,512]{1,0:T(8,128)(2,1)} %bitcast.345, bf16[512,256]{1,0:T(8,128)(2,1)} %fusion.60.kv_ref, bf16[1024,4224]{1,0:T(8,128)(2,1)} %all-gather.4.cloned.1.call-done.w_ref, ...), custom_call_target="tpu_custom_call" | custom-call | flops 10000000000 | bytes 30000000 | tf_op jit(solution)/shard_map/input_back/pallas_call | solution.py:1134
  470.5 6.0 %collective-permute-done.41 = bf16[32,3584]{1,0:T(8,128)(2,1)S(1)} collective-permute-done((bf16[32,3584]{1,0:T(8,128)(2,1)S(1)}, bf16[32,3584]{1,0:T(8,128)(2,1)S(1)}, u32[]{:S(2)}, u32[]{:S(2)}) %collective-permute-start.41) | collective-permute-done | bytes 229408 | tf_op jit(solution)/shard_map/ppermute | solution.py:78
  492.8 5.5 %collective-permute-start.48 = (f32[72]{0:T(128)S(1)}, f32[72]{0:T(128)S(1)}, u32[]{:S(2)}, u32[]{:S(2)}) collective-permute-start(f32[72]{0:T(128)S(1)} %add.704), channel_id=1, source_target_pairs={{0,8},{8,0},{16,24},{24,16},{1,9},{9,1},{17,25},{25,17},{2,10},{10... | collective-permute-start | bytes 872 | tf_op jit(solution)/shard_map/ppermute | solution.py:56
  522.0 10.7 %collective-permute-done.50 = bf16[32,2688]{1,0:T(8,128)(2,1)S(1)} collective-permute-done((bf16[32,2688]{1,0:T(8,128)(2,1)S(1)}, bf16[32,2688]{1,0:T(8,128)(2,1)S(1)}, u32[]{:S(2)}, u32[]{:S(2)}) %collective-permute-start.50) | collective-permute-done | bytes 172064 | tf_op jit(solution)/shard_map/ppermute | solution.py:78
  (532 shorter events, 278.0 us)
Async XLA Ops:
  7.2 93.5 %all-gather.4.cloned.1.call-start = ((), (), s32[]{:S(2)}) async-start(), calls=%async_computation.3 | async-start | bytes 9732096 | tf_op jit(solution)/shard_map/all_gather | solution.py:252
  13.0 27.5 %collective-permute-start = (bf16[32,4224]{1,0:T(8,128)(2,1)S(1)}, bf16[32,4224]{1,0:T(8,128)(2,1)S(1)}, u32[]{:S(2)}, u32[]{:S(2)}) collective-permute-start(bf16[32,4224]{1,0:T(8,128)(2,1)S(1)} %concatenate.103), channel_id=1, source_target_pairs={{0,8},{8,16},{24,0},{1,9},{9,17},{25,1},{2,10},{10,18},{26,2},{3,1... | collective-permute-start | bytes 811016 | tf_op jit(solution)/shard_map/ppermute | solution.py:78
  14.3 26.2 %collective-permute-start.1 = (bf16[32,4224]{1,0:T(8,128)(2,1)S(1)}, bf16[32,4224]{1,0:T(8,128)(2,1)}, u32[]{:S(2)}, u32[]{:S(2)}) collective-permute-start(bf16[32,4224]{1,0:T(8,128)(2,1)S(1)} %concatenate.103), channel_id=1, source_target_pairs={{0,16},{16,0},{24,8},{1,17},{17,1},{25,9},{2,18},{18,2},{26,10},{3... | collective-permute-start | bytes 811016 | tf_op jit(solution)/shard_map/ppermute | solution.py:78
  44.1 101.8 %all-gather.6.cloned.1.call-start = ((), (), s32[]{:S(2)}) async-start(), calls=%async_computation.4 | async-start | bytes 4718592 | tf_op jit(solution)/shard_map/all_gather | solution.py:252
  78.0 60.3 %collective-permute-start.14 = (bf16[32,6144]{1,0:T(8,128)(2,1)}, bf16[32,6144]{1,0:T(8,128)(2,1)}, u32[]{:S(2)}, u32[]{:S(2)}) collective-permute-start(bf16[32,6144]{1,0:T(8,128)(2,1)} %get-tuple-element.220), channel_id=1, source_target_pairs={{0,8},{8,16},{24,0},{1,9},{9,17},{25,1},{2,10},{10,18},{26,2},{3,1... | collective-permute-start | bytes 1179656 | tf_op jit(solution)/shard_map/ppermute | solution.py:78
  85.5 52.8 %collective-permute-start.15 = (bf16[32,6144]{1,0:T(8,128)(2,1)}, bf16[32,6144]{1,0:T(8,128)(2,1)}, u32[]{:S(2)}, u32[]{:S(2)}) collective-permute-start(bf16[32,6144]{1,0:T(8,128)(2,1)} %get-tuple-element.220), channel_id=1, source_target_pairs={{0,16},{16,0},{24,8},{1,17},{17,1},{25,9},{2,18},{18,2},{26,10},{3... | collective-permute-start | bytes 1179656 | tf_op jit(solution)/shard_map/ppermute | solution.py:78
  91.6 46.7 %collective-permute-start.16 = (bf16[32,6144]{1,0:T(8,128)(2,1)}, bf16[32,6144]{1,0:T(8,128)(2,1)}, u32[]{:S(2)}, u32[]{:S(2)}) collective-permute-start(bf16[32,6144]{1,0:T(8,128)(2,1)} %get-tuple-element.220), channel_id=1, source_target_pairs={{8,0},{16,8},{24,16},{9,1},{17,9},{25,17},{10,2},{18,10},{26,18},{... | collective-permute-start | bytes 1179656 | tf_op jit(solution)/shard_map/ppermute | solution.py:78
  102.2 131.1 %all-gather.8.cloned.1.call-start = ((), (), s32[]{:S(2)}) async-start(), calls=%async_computation.5 | async-start | bytes 14155776 | tf_op jit(solution)/shard_map/all_gather | solution.py:252
  116.3 22.0 %collective-permute-start.13 = (bf16[2,512,128]{2,1,0:T(8,128)(2,1)S(1)}, bf16[2,512,128]{2,1,0:T(8,128)(2,1)S(1)}, u32[]{:S(2)}, u32[]{:S(2)}) collective-permute-start(bf16[2,512,128]{2,1,0:T(8,128)(2,1)S(1)} %maximum_select_fusion.4), channel_id=1, source_target_pairs={{0,2},{1,3},{2,0},{3,1},{4,6},{5,7},{6,4},{7,5},{8,10},{9,11},{10,... | collective-permute-start | bytes 786440 | tf_op jit(solution)/shard_map/ppermute | solution.py:56
  145.9 220.7 %reduce-scatter.4.cloned.1.call-start = ((), (), s32[]{:S(2)}) async-start(), calls=%async_computation.6 | async-start | bytes 14155776 | tf_op jit(solution)/shard_map/reduce_scatter | solution.py:248
  149.8 24.2 %collective-permute-start.19 = (bf16[128,1024]{1,0:T(8,128)(2,1)}, bf16[128,1024]{1,0:T(8,128)(2,1)}, u32[]{:S(2)}, u32[]{:S(2)}) collective-permute-start(bf16[128,1024]{1,0:T(8,128)(2,1)} %get-tuple-element.549), channel_id=1, source_target_pairs={{0,8},{8,16},{24,0},{1,9},{9,17},{25,1},{2,10},{10,18},{26,2},{3,1... | collective-permute-start | bytes 786440 | tf_op jit(solution)/shard_map/ppermute | solution.py:78
  263.7 182.2 %reduce-scatter.6.cloned.1.call-start = ((), (), s32[]{:S(2)}) async-start(), calls=%async_computation.7 | async-start | bytes 8257536 | tf_op jit(solution)/shard_map/reduce_scatter | solution.py:248
  313.0 26.2 %collective-permute-start.27 = (bf16[4,512,128]{2,1,0:T(8,128)(2,1)S(1)}, bf16[4,512,128]{2,1,0:T(8,128)(2,1)S(1)}, u32[]{:S(2)}, u32[]{:S(2)}) collective-permute-start(bf16[4,512,128]{2,1,0:T(8,128)(2,1)S(1)} %dynamic-slice_bitcast_fusion.1), channel_id=1, source_target_pairs={{0,1},{1,0},{2,3},{3,2},{4,5},{5,4},{6,7},{7,6},{8,9},{9,8},{10,11... | collective-permute-start | bytes 1572872 | tf_op jit(solution)/shard_map/ppermute | solution.py:56
  313.1 26.2 %collective-permute-start.26 = (bf16[144,1536]{1,0:T(8,128)(2,1)S(1)}, bf16[144,1536]{1,0:T(8,128)(2,1)S(1)}, u32[]{:S(2)}, u32[]{:S(2)}) collective-permute-start(bf16[144,1536]{1,0:T(8,128)(2,1)S(1)} %get-tuple-element.284), channel_id=1, source_target_pairs={{0,4},{1,5},{2,6},{3,7},{4,0},{5,1},{6,2},{7,3},{8,12},{9,13},{10,... | collective-permute-start | bytes 1327112 | tf_op jit(solution)/shard_map/ppermute | solution.py:56
  366.6 138.9 %reduce-scatter.8.cloned.1.call-start = ((), (), s32[]{:S(2)}) async-start(), calls=%async_computation.8 | async-start | bytes 6193152 | tf_op jit(solution)/shard_map/reduce_scatter | solution.py:248
  373.5 34.5 %collective-permute-start.30 = (bf16[512,256]{1,0:T(8,128)(2,1)}, bf16[512,256]{1,0:T(8,128)(2,1)}, u32[]{:S(2)}, u32[]{:S(2)}) collective-permute-start(bf16[512,256]{1,0:T(8,128)(2,1)} %get-tuple-element.519), channel_id=1, source_target_pairs={{0,4},{1,5},{2,6},{3,7},{4,0},{5,1},{6,2},{7,3},{8,12},{9,13},{10,... | collective-permute-start | bytes 786440 | tf_op jit(solution)/shard_map/ppermute | solution.py:56
  374.7 33.3 %collective-permute-start.31 = (bf16[512,256]{1,0:T(8,128)(2,1)}, bf16[512,256]{1,0:T(8,128)(2,1)}, u32[]{:S(2)}, u32[]{:S(2)}) collective-permute-start(bf16[512,256]{1,0:T(8,128)(2,1)} %get-tuple-element.517), channel_id=1, source_target_pairs={{0,6},{1,7},{2,4},{3,5},{4,2},{5,3},{6,0},{7,1},{8,14},{9,15},{10,... | collective-permute-start | bytes 786440 | tf_op jit(solution)/shard_map/ppermute | solution.py:56
  376.6 31.3 %collective-permute-start.32 = (bf16[32,6144]{1,0:T(8,128)(2,1)}, bf16[32,6144]{1,0:T(8,128)(2,1)}, u32[]{:S(2)}, u32[]{:S(2)}) collective-permute-start(bf16[32,6144]{1,0:T(8,128)(2,1)} %get-tuple-element.508), channel_id=1, source_target_pairs={{0,8},{8,16},{16,24},{1,9},{9,17},{17,25},{2,10},{10,18},{18,26},{... | collective-permute-start | bytes 1179656 | tf_op jit(solution)/shard_map/ppermute | solution.py:78
  377.9 36.2 %collective-permute-start.33 = (bf16[32,6144]{1,0:T(8,128)(2,1)}, bf16[32,6144]{1,0:T(8,128)(2,1)}, u32[]{:S(2)}, u32[]{:S(2)}) collective-permute-start(bf16[32,6144]{1,0:T(8,128)(2,1)} %get-tuple-element.507), channel_id=1, source_target_pairs={{0,16},{8,24},{16,0},{1,17},{9,25},{17,1},{2,18},{10,26},{18,2},{3... | collective-permute-start | bytes 1179656 | tf_op jit(solution)/shard_map/ppermute | solution.py:78
  381.3 32.8 %collective-permute-start.34 = (bf16[32,6144]{1,0:T(8,128)(2,1)S(1)}, bf16[32,6144]{1,0:T(8,128)(2,1)}, u32[]{:S(2)}, u32[]{:S(2)}) collective-permute-start(bf16[32,6144]{1,0:T(8,128)(2,1)S(1)} %get-tuple-element.506), channel_id=1, source_target_pairs={{0,24},{8,0},{16,8},{1,25},{9,1},{17,9},{2,26},{10,2},{18,10},{3,2... | collective-permute-start | bytes 1179656 | tf_op jit(solution)/shard_map/ppermute | solution.py:78
  421.7 24.1 %collective-permute-start.36 = (bf16[128,1024]{1,0:T(8,128)(2,1)}, bf16[128,1024]{1,0:T(8,128)(2,1)}, u32[]{:S(2)}, u32[]{:S(2)}) collective-permute-start(bf16[128,1024]{1,0:T(8,128)(2,1)} %get-tuple-element.514), channel_id=1, source_target_pairs={{0,16},{8,24},{16,0},{1,17},{9,25},{17,1},{2,18},{10,26},{18,2},{3... | collective-permute-start | bytes 786440 | tf_op jit(solution)/shard_map/ppermute | solution.py:78
  423.0 22.8 %collective-permute-start.37 = (bf16[128,1024]{1,0:T(8,128)(2,1)}, bf16[128,1024]{1,0:T(8,128)(2,1)}, u32[]{:S(2)}, u32[]{:S(2)}) collective-permute-start(bf16[128,1024]{1,0:T(8,128)(2,1)} %get-tuple-element.513), channel_id=1, source_target_pairs={{0,24},{8,0},{16,8},{1,25},{9,1},{17,9},{2,26},{10,2},{18,10},{3,2... | collective-permute-start | bytes 786440 | tf_op jit(solution)/shard_map/ppermute | solution.py:78
  481.7 23.2 %collective-permute-start.45 = (bf16[128,1024]{1,0:T(8,128)(2,1)S(1)}, bf16[128,1024]{1,0:T(8,128)(2,1)S(1)}, u32[]{:S(2)}, u32[]{:S(2)}) collective-permute-start(bf16[128,1024]{1,0:T(8,128)(2,1)S(1)} %get-tuple-element.511), channel_id=1, source_target_pairs={{0,16},{8,24},{16,0},{1,17},{9,25},{17,1},{2,18},{10,26},{18,2},{3... | collective-permute-start | bytes 786440 | tf_op jit(solution)/shard_map/ppermute | solution.py:78
  483.0 22.6 %collective-permute-start.46 = (bf16[128,1024]{1,0:T(8,128)(2,1)S(1)}, bf16[128,1024]{1,0:T(8,128)(2,1)}, u32[]{:S(2)}, u32[]{:S(2)}) collective-permute-start(bf16[128,1024]{1,0:T(8,128)(2,1)S(1)} %get-tuple-element.510), channel_id=1, source_target_pairs={{0,24},{8,0},{16,8},{1,25},{9,1},{17,9},{2,26},{10,2},{18,10},{3,2... | collective-permute-start | bytes 786440 | tf_op jit(solution)/shard_map/ppermute | solution.py:78
  (126 other events, 1457.5 us)
Sparse Core Ops, SparseCore 0:
  44.2 56.4 all-gather.3
  102.6 43.2 all-gather.5
  147.7 85.5 all-gather.7
  263.8 102.7 reduce-scatter.3
  369.8 66.9 reduce-scatter.5
  446.0 58.5 reduce-scatter.7

commit v3 on v2

--- a/solution.py
+++ b/solution.py
@@ -1143,6 +1143,35 @@
     )(d_scan, d_gate, d_query, d_kv, w, x, more, gain)
 
 
+def owned_kernel(count_ref, own_ref, a_ref, b_ref, c_ref, gain_ref, gate_ref, x_ref, bc_ref, dt_ref, query_ref, kv_ref, *outs):
+    total = own_ref[...].astype(jnp.float32) * count_ref[0].astype(jnp.float32)
+    total = total + a_ref[...].astype(jnp.float32) + b_ref[...].astype(jnp.float32) + c_ref[...].astype(jnp.float32)
+    at, inner = 0, gate_ref[...]
+    for weight_ref, out_ref in zip((x_ref, bc_ref, dt_ref, query_ref, kv_ref), outs):
+        part = total[:, at : at + out_ref.shape[1]]
+        out_ref[...] = part
+        heads = weight_ref.shape[1]
+        inner = inner + jnp.sum(weight_ref[...].astype(jnp.float32) * part[:, :heads], axis=1, keepdims=True)
+        at += out_ref.shape[1]
+    outs[-1][...] = inner / gain_ref[...].astype(jnp.float32)
+
+
+def owned_last(own, got, counts, gain, gate, weights, sizes):
+    rows = own.shape[0]
+    arrays = (own, *got, gain, gate, *weights)
+    whole = lambda dims: pl.BlockSpec(dims, lambda i: (0, 0))
+    return pl.pallas_call(
+        owned_kernel,
+        grid=(1,),
+        in_specs=[pl.BlockSpec(memory_space=pltpu.SMEM)] + [whole(array.shape) for array in arrays],
+        out_specs=[whole((rows, size)) for size in sizes] + [whole((rows, 1))],
+        out_shape=[shape((rows, size)) for size in sizes] + [shape((rows, 1))],
+        compiler_params=pltpu.CompilerParams(vmem_limit_bytes=16 * 2**20),
+        cost_estimate=guess(3),
+        name="owned_last",
+    )(counts, *arrays)
+
+
 def tap_marks(starts, first, length, taps):
     ext = doc_index(starts, first - (taps - 1) + jnp.arange(length + taps - 1, dtype=jnp.int32))
     return jnp.stack([(ext[i : i + length] == ext[taps - 1 :]).astype(jnp.float32) for i in range(taps)], axis=1)
@@ -1347,6 +1376,7 @@
     ffn_in = normed_ffn.astype(LOW)
     fed, d_ffn_in, grad_ffn = feed_forward(ffn_in, d_out_low, gy_plain, w_ffn, folds, width)
     part_ffn = sum_wide(grad_ffn)
+    out_low = (resid + fed).astype(LOW)
     (d_resid_norm,) = pull_ffn(d_ffn_in)
     d_resid = d_out_low.astype(jnp.float32) + d_resid_norm
 
@@ -1390,17 +1420,16 @@
     chip_sum = ChipSum(jnp.concatenate([core_0.end(), core_1.end()], axis=2))
     early, part_ffn = tied(early, part_ffn)
     part_early = sum_wide(early)
-    out_plain = plain((resid + fed).astype(LOW))
     own_ffn = HeadSum(part_ffn, micro_count)
     d_scan, grad_skip, grad_head, grad_taps, rim_back, edge = mamba_scan_back(
         feats, raw_scan, rim, taps_ext, marks, docs_row, dy_low, entry, d_state,
         skip_row, bias_row, rate_row, cols, mats,
     )
-    chip_sum.got, own_ffn.got, d_scan, edge, rim_back, grad_taps, grad_head, grad_skip, d_query, out_plain = tied(
-        chip_sum.got, own_ffn.got, d_scan, edge, rim_back, grad_taps, grad_head, grad_skip, d_query, out_plain
+    chip_sum.got, own_ffn.got, d_scan, edge, rim_back, grad_taps, grad_head, grad_skip, d_query, out_low = tied(
+        chip_sum.got, own_ffn.got, d_scan, edge, rim_back, grad_taps, grad_head, grad_skip, d_query, out_low
     )
     rim_came = shifted(rim_back, "wide", -1)
-    out_back = FromBlocks(out_plain, micro_count)
+    out_back = FromBlocks(out_low, micro_count)
     d_kv = chip_sum.end()
     own_ffn = own_ffn.end()
     d_scan = lax.dynamic_update_slice(d_scan, (edge + rim_came).astype(LOW), (block_tok - 8, 0))
@@ -1441,8 +1470,10 @@
     totals.got, g_gate_w, g_up_w = tied(totals.got, g_gate_w, g_up_w)
     totals.end()
     totals.begin()
-    x_back.got, own_early.got, own_early.own, part_late, totals.got, g_gate_w, g_up_w = tied(
-        x_back.got, own_early.got, own_early.own, part_late, totals.got, g_gate_w, g_up_w
+    *g_out, g_gate = own_early.end((width,) * ((out_rows + attn_rows) // rows) + (inner,))
+    out_done = plain(out_back.end())
+    x_back.got, g_out, g_gate, out_done, part_late, totals.got, g_gate_w, g_up_w = tied(
+        x_back.got, g_out, g_gate, out_done, part_late, totals.got, g_gate_w, g_up_w
     )
     totals.end()
     own_late = HeadSum(part_late, micro_count)
@@ -1450,10 +1481,18 @@
     results = x_back.end()
     own_late.got, results = tied(own_late.got, results)
     per_head = summed[: 3 * heads].reshape(3, heads)
-    g_x, g_bc, g_dt, g_small, _, g_q, g_kv = own_late.end(
-        (inner, bc_cols, heads, small_cols, LANES - heads - small_cols, query_cols, kv_cols)
-    )
-    *g_out, g_gate = own_early.end((width,) * ((out_rows + attn_rows) // rows) + (inner,))
+    gate_sum = jnp.sum(mamba_gate_w.astype(jnp.float32) * g_gate, axis=1, keepdims=True)
+    summing = (lax.axis_index("head") < micro_count).astype(jnp.int32).reshape(1)
+    g_x, g_bc, g_tail, g_q, g_kv, o_gain_in = owned_last(
+        own_late.own,
+        own_late.got,
+        summing,
+        gain_in[:, None],
+        gate_sum,
+        (mamba_in_w, mamba_bc_w, mamba_dt_w, attn_q_w, attention_key_value_weight),
+        (inner, bc_cols, LANES, query_cols, kv_cols),
+    )
+    g_dt, g_small, _ = split_at(g_tail, (heads, small_cols, LANES - heads - small_cols), 1)
     o_conv_x, o_conv_bc, _ = split_at(
         g_small.reshape(-1), (taps * chan, taps * chan_bc, rows * small_cols - taps * (chan + chan_bc)), 0
     )
@@ -1464,23 +1503,12 @@
             total = total + jnp.sum(weight.astype(jnp.float32) * grad, axis=1)
         return total / gain.astype(jnp.float32)
 
-    o_gain_in = gain_grad(
-        gain_in,
-        (
-            (mamba_in_w, g_x),
-            (mamba_bc_w, g_bc),
-            (mamba_dt_w, g_dt),
-            (mamba_gate_w, g_gate),
-            (attn_q_w, g_q),
-            (attention_key_value_weight, g_kv),
-        ),
-    )
     o_gain_ffn = gain_grad(gain_ffn, ((ffn_gate_w, g_gate_w), (ffn_up_w, g_up_w)))
     o_gain_m = gain_grad(mamba_gain, ((mamba_out_w, g_mamba_out),))
     return (
-        out_back.end()[:, None],
+        out_done[:, None],
         results[:, None],
-        o_gain_in,
+        o_gain_in[:, 0],
         g_gate,
         g_x,
         g_bc,

time: 554 us -> 548 us (0.989)
  starting transfers between devices: 109 us -> 116 us
  waiting for transfers between devices: 127 us -> 120 us
    ppermute x30, waiting for transfers between devices: 52.4 us -> 39.4 us  [sent_on(): got.append(lax.ppermute(pieces((place + step) % count), 'head', pairs))]
    ppermute x21, starting transfers between devices: 29 us -> 36.2 us  [swapped(): return lax.ppermute(value, axis, [(i, i ^ bit) for i in range(count)])]
    ppermute x21, waiting for transfers between devices: 45.6 us -> 51.5 us  [swapped(): return lax.ppermute(value, axis, [(i, i ^ bit) for i in range(count)])]
    unnamed x189 -> x167, local copies, waits for them, and re-layouts: 16.1 us -> 15.8 us
  transfers between devices with their start and end apart: 59 -> 59, of which waited for: 20 -> 19; matrix products, arithmetic and copies ran while one was open for 23% -> 23% of each run, Pallas kernels for 19% -> 20%
where the time goes in v3:
time: 548 us; the launch traced here: 539 us
  Pallas kernels  138 us (25%)
  waiting for transfers between devices  120 us (22%)
  starting transfers between devices  116 us (21%)
  local copies, waits for them, and re-layouts  65.6 us (12%)
  matrix products  45.9 us (8%)
  other arithmetic  36.9 us (7%)
  between operations  16.5 us (3%)
    ppermute x30, starting transfers between devices, sent_on(): got.append(lax.ppermute(pieces((place + step) % count), 'head', pairs))  76.9 us
    pallas_call x4, Pallas kernels, call(): pl.pallas_call(kernel, grid=(parts,), in_specs=[spec(block, how) for _, b...  59.3 us
    ppermute x21, waiting for transfers between devices, swapped(): return lax.ppermute(value, axis, [(i, i ^ bit) for i in range(count)])  51.5 us
    ppermute x30, waiting for transfers between devices, sent_on(): got.append(lax.ppermute(pieces((place + step) % count), 'head', pairs))  39.4 us
    ppermute x21, starting transfers between devices, swapped(): return lax.ppermute(value, axis, [(i, i ^ bit) for i in range(count)])  36.2 us
    pallas_call x1, Pallas kernels, feed_forward(): pl.pallas_call(feed_kernel, grid=(folds,), in_specs=[whole, whole, whole,...  30.4 us
    dot_general x12, matrix products, nn(): return jnp.dot(left, right, preferred_element_type=jnp.float32)  28.5 us
    all_gather x3, waiting for transfers between devices, gather_wide(): return lax.all_gather(array, 'wide', axis=0, tiled=True)  15.8 us
  transfers between devices with their start and end apart: 59, of which 19 were waited for; matrix products, arithmetic and copies ran while one was open for 23% of the time, Pallas kernels for 20%

profile of v3, /device:TPU:24, one launch (start us, length us, event | category | flops | bytes accessed | tf_op | source)
XLA Modules:
  0.0 538.6 jit_solution(9193537052951607328)
XLA Ops:
  55.4 6.7 %collective-permute-start.6 = (bf16[128,1024]{1,0:T(8,128)(2,1)S(1)}, bf16[128,1024]{1,0:T(8,128)(2,1)S(1)}, u32[]{:S(2)}, u32[]{:S(2)}) collective-permute-start(bf16[128,1024]{1,0:T(8,128)(2,1)S(1)} %get-tuple-element.554), channel_id=1, source_target_pairs={{0,8},{8,16},{24,0},{1,9},{9,17},{25,1},{2,10},{10,18},{26,2},{3,1... | collective-permute-start | bytes 786440 | tf_op jit(solution)/shard_map/ppermute | solution.py:78
  78.0 7.5 %collective-permute-start.14 = (bf16[32,6144]{1,0:T(8,128)(2,1)}, bf16[32,6144]{1,0:T(8,128)(2,1)}, u32[]{:S(2)}, u32[]{:S(2)}) collective-permute-start(bf16[32,6144]{1,0:T(8,128)(2,1)} %get-tuple-element.226), channel_id=1, source_target_pairs={{0,8},{8,16},{24,0},{1,9},{9,17},{25,1},{2,10},{10,18},{26,2},{3,1... | collective-permute-start | bytes 1179656 | tf_op jit(solution)/shard_map/ppermute | solution.py:78
  85.5 6.1 %collective-permute-start.15 = (bf16[32,6144]{1,0:T(8,128)(2,1)}, bf16[32,6144]{1,0:T(8,128)(2,1)}, u32[]{:S(2)}, u32[]{:S(2)}) collective-permute-start(bf16[32,6144]{1,0:T(8,128)(2,1)} %get-tuple-element.226), channel_id=1, source_target_pairs={{0,16},{16,0},{24,8},{1,17},{17,1},{25,9},{2,18},{18,2},{26,10},{3... | collective-permute-start | bytes 1179656 | tf_op jit(solution)/shard_map/ppermute | solution.py:78
  127.2 11.0 %mamba_local.1 = (f32[512,1536]{1,0:T(8,128)}, bf16[512,1536]{1,0:T(8,128)(2,1)}, bf16[512,256]{1,0:T(8,128)(2,1)}, bf16[512,256]{1,0:T(8,128)(2,1)}, f32[512,12...) custom-call(f32[512,1920]{1,0:T(8,128)} %copy-done.70, ...), custom_call_target="tpu_custom_call" | custom-call | flops 11000000512 | bytes 33000000 | tf_op jit(solution)/shard_map/mamba_local/pallas_call | solution.py:652
  172.9 12.1 %collective-permute-done.18.got_ref = bf16[144,1536]{1,0:T(8,128)(2,1)S(1)} collective-permute-done((bf16[144,1536]{1,0:T(8,128)(2,1)S(1)}, bf16[144,1536]{1,0:T(8,128)(2,1)S(1)}, u32[]{:S(2)}, u32[]{:S(2)}) %collective-permute-start.18) | collective-permute-done | bytes 442400 | tf_op jit(solution)/shard_map/ppermute | solution.py:56
  196.2 5.6 %collective-permute-done.23.got_ref = bf16[144,1536]{1,0:T(8,128)(2,1)S(1)} collective-permute-done((bf16[144,1536]{1,0:T(8,128)(2,1)S(1)}, bf16[144,1536]{1,0:T(8,128)(2,1)S(1)}, u32[]{:S(2)}, u32[]{:S(2)}) %collective-permute-start.23) | collective-permute-done | bytes 442400 | tf_op jit(solution)/shard_map/ppermute | solution.py:56
  204.4 11.2 %mamba_mix.1 = (bf16[512,1536]{1,0:T(8,128)(2,1)}, f32[512,1536]{1,0:T(8,128)}, bf16[4,128,1536]{2,1,0:T(8,128)(2,1)}) custom-call(f32[512,1536]{1,0:T(8,128)} %get-tuple-element.238.act_ref, bf16[512,256]{1,0:T(8,128)(2,1)} %get-tuple-element.239.bcact_ref, f32[512,1536]{1,0:T(8,128)} %fusion.26.z_ref, f32[512,128]{1,0:T(8,128)} %get-tuple-element.241.step_ref, ...), custom_call_target="tpu_custom_call" | custom-call | flops 11000000512 | bytes 33000000 | tf_op jit(solution)/shard_map/mamba_mix/pallas_call | solution.py:652
  224.2 8.0 %all-gather.8.cloned.1.call-done.w_ref = bf16[1024,6144]{1,0:T(8,128)(2,1)} async-done(((bf16[128,6144]{1,0:T(8,128)(2,1)}), bf16[1024,6144]{1,0:T(8,128)(2,1)}) %all-gather.8.cloned.1.call-update) | async-done | bytes 12582928 | tf_op jit(solution)/shard_map/all_gather | solution.py:252
  232.1 30.4 %feed_forward.1 = (f32[512,1024]{1,0:T(8,128)}, f32[512,1024]{1,0:T(8,128)}, bf16[1024,6144]{1,0:T(8,128)(2,1)}) custom-call(bf16[512,1024]{1,0:T(8,128)(2,1)} %multiply_convert_fusion.x_ref, bf16[512,1024]{1,0:T(8,128)(2,1)} %fusion.43.gy_ref, bf16[512,1024]{1,0:T(8,128)(2,1)} %bitcast.338, bf16[1024,6144]{1,0:T(8,128)(2,1)} %all-gather.8.cloned.1.call-done.w_ref), custom_call_target="tpu_custom_call" | custom-call | flops 35000000512 | bytes 105000000 | tf_op jit(solution)/shard_map/feed_forward/pallas_call | solution.py:1077
  272.9 12.8 %mamba_gate_back.1 = (bf16[512,1536]{1,0:T(8,128)(2,1)}, f32[512,1536]{1,0:T(8,128)}, bf16[144,1536]{1,0:T(8,128)(2,1)}, f32[128,1536]{1,0:T(8,128)}, f32[8,1536]{1,0:T(8,128)}) custom-call(f32[512,1536]{1,0:T(8,128)} %fusion.171.dym_ref, f32[512,1536]{1,0:T(8,128)} %get-tuple-element.270.y_ref, f32[512,1536]{1,0:T(8,128)} %fusion.26.z_ref, ...), custom_call_target="tpu_custom_call" | custom-call | flops 11000000512 | bytes 33000000 | tf_op jit(solution)/shard_map/mamba_gate_back/pallas_call | solution.py:652
  293.8 7.2 %attend_back.2 = (bf16[4,64,512]{2,1,0:T(8,128)(2,1)}, bf16[4096,128]{1,0:T(8,128)(2,1)}) custom-call(s32[1]{0:T(128)} %bitcast.56.place_ref, bf16[4,128,512]{2,1,0:T(8,128)(2,1)} %get-tuple-element.281.qb_ref, bf16[8,64,512]{2,1,0:T(8,128)(2,1)} %bitcast.380, f32[4,64,512]{2,1,0:T(8,128)} %get-tuple-element.266.o_ref, bf16[4096,256]{1,0:T(8,128)(2,1)} %bitcast.329, ...), custom_call_target="tpu_custom_call" | custom-call | flops 27000000512 | bytes 81000000 | tf_op jit(solution)/shard_map/attend_back/pallas_call | solution.py:1017
  301.1 12.8 %collective-permute-done.25.got_ref = bf16[144,1536]{1,0:T(8,128)(2,1)S(1)} collective-permute-done((bf16[144,1536]{1,0:T(8,128)(2,1)S(1)}, bf16[144,1536]{1,0:T(8,128)(2,1)S(1)}, u32[]{:S(2)}, u32[]{:S(2)}) %collective-permute-start.25) | collective-permute-done | bytes 442400 | tf_op jit(solution)/shard_map/ppermute | solution.py:56
  319.6 6.7 %attend_back.3 = (bf16[4,64,512]{2,1,0:T(8,128)(2,1)}, bf16[4096,128]{1,0:T(8,128)(2,1)}) custom-call(s32[1]{0:T(128)} %bitcast.56.place_ref, bf16[4,128,512]{2,1,0:T(8,128)(2,1)} %get-tuple-element.291.qb_ref, bf16[8,64,512]{2,1,0:T(8,128)(2,1)} %bitcast.381, f32[4,64,512]{2,1,0:T(8,128)} %get-tuple-element.267.o_ref, bf16[4096,256]{1,0:T(8,128)(2,1)} %bitcast.330, ...), custom_call_target="tpu_custom_call" | custom-call | flops 27000000512 | bytes 81000000 | tf_op jit(solution)/shard_map/attend_back/pallas_call | solution.py:1017
  326.3 12.2 %collective-permute-done.26.got_ref = bf16[144,1536]{1,0:T(8,128)(2,1)S(1)} collective-permute-done((bf16[144,1536]{1,0:T(8,128)(2,1)S(1)}, bf16[144,1536]{1,0:T(8,128)(2,1)S(1)}, u32[]{:S(2)}, u32[]{:S(2)}) %collective-permute-start.26) | collective-permute-done | bytes 442400 | tf_op jit(solution)/shard_map/ppermute | solution.py:56
  353.4 12.9 %reduce-scatter.4.cloned.1.call-done = bf16[128,6144]{1,0:T(8,128)(2,1)} async-done(((bf16[1024,6144]{1,0:T(8,128)(2,1)}), bf16[128,6144]{1,0:T(8,128)(2,1)}) %reduce-scatter.4.cloned.1.call-update) | async-done | bytes 1572880 | tf_op jit(solution)/shard_map/reduce_scatter | solution.py:248
  378.9 24.3 %mamba_scan_back.1 = (bf16[512,1920]{1,0:T(8,128)(2,1)}, f32[8,1536]{1,0:T(8,128)}, f32[8,128]{1,0:T(8,128)}, f32[8,1792]{1,0:T(8,128)}, f32[8,1792]{1,0:T(8,128)}, /*index=5*/f32[8,1792]{1,0:T(8,128)}) custom-call(f32[512,1536]{1,0:T(8,128)} %get-tuple-element.238.act_ref, bf16[512,1536]{1,0:T(8,128)(2,1)} %get-tuple-element.309.slope_ref, ...), custom_call_target="tpu_custom_call" | custom-call | flops 23000000512 | bytes 69000000 | tf_op jit(solution)/shard_map/mamba_scan_back/pallas_call | solution.py:652
  404.3 5.9 %collective-permute-done.33 = bf16[32,6144]{1,0:T(8,128)(2,1)} collective-permute-done((bf16[32,6144]{1,0:T(8,128)(2,1)S(1)}, bf16[32,6144]{1,0:T(8,128)(2,1)}, u32[]{:S(2)}, u32[]{:S(2)}) %collective-permute-start.33) | collective-permute-done | bytes 393248 | tf_op jit(solution)/shard_map/ppermute | solution.py:78
  426.2 7.8 %last_grads.1 = bf16[1024,2688]{1,0:T(8,128)(2,1)} custom-call(bf16[512,1024]{1,0:T(8,128)(2,1)} %copy-done.35, bf16[512,1920]{1,0:T(8,128)(2,1)} %fusion.106.scan_ref, bf16[512,512]{1,0:T(8,128)(2,1)} %bitcast.352, bf16[512,256]{1,0:T(8,128)(2,1)} %fusion.60.kv_ref, f32[1024,128]{1,0:T(8,128)} %pad.33.small_ref), custom_call_target="tpu_custom_call" | custom-call | flops 8000000000 | bytes 24000000 | tf_op jit(solution)/shard_map/last_grads/pallas_call | solution.py:1107
  434.0 10.8 %collective-permute-done.36 = bf16[128,1024]{1,0:T(8,128)(2,1)} collective-permute-done((bf16[128,1024]{1,0:T(8,128)(2,1)}, bf16[128,1024]{1,0:T(8,128)(2,1)}, u32[]{:S(2)}, u32[]{:S(2)}) %collective-permute-start.36) | collective-permute-done | bytes 262176 | tf_op jit(solution)/shard_map/ppermute | solution.py:78
  457.4 12.3 %input_back.1 = bf16[512,1024]{1,0:T(8,128)(2,1)} custom-call(bf16[512,1920]{1,0:T(8,128)(2,1)} %fusion.106.scan_ref, bf16[512,1536]{1,0:T(8,128)(2,1)} %get-tuple-element.304.gate_ref, bf16[512,512]{1,0:T(8,128)(2,1)} %bitcast.353, bf16[512,256]{1,0:T(8,128)(2,1)} %fusion.60.kv_ref, bf16[1024,4224]{1,0:T(8,128)(2,1)} %all-gather.4.cloned.1.call-done.w_ref, ...), custom_call_target="tpu_custom_call" | custom-call | flops 10000000000 | bytes 30000000 | tf_op jit(solution)/shard_map/input_back/pallas_call | solution.py:1134
  469.8 5.7 %collective-permute-done.41 = bf16[32,3584]{1,0:T(8,128)(2,1)S(1)} collective-permute-done((bf16[32,3584]{1,0:T(8,128)(2,1)S(1)}, bf16[32,3584]{1,0:T(8,128)(2,1)S(1)}, u32[]{:S(2)}, u32[]{:S(2)}) %collective-permute-start.41) | collective-permute-done | bytes 229408 | tf_op jit(solution)/shard_map/ppermute | solution.py:78
  499.4 5.5 %collective-permute-done.45 = bf16[128,1024]{1,0:T(8,128)(2,1)S(1)} collective-permute-done((bf16[128,1024]{1,0:T(8,128)(2,1)S(1)}, bf16[128,1024]{1,0:T(8,128)(2,1)S(1)}, u32[]{:S(2)}, u32[]{:S(2)}) %collective-permute-start.45) | collective-permute-done | bytes 262176 | tf_op jit(solution)/shard_map/ppermute | solution.py:78
  512.2 6.9 %collective-permute-start.52 = (f32[72]{0:T(128)S(1)}, f32[72]{0:T(128)S(1)}, u32[]{:S(2)}, u32[]{:S(2)}) collective-permute-start(f32[72]{0:T(128)S(1)} %add.645), channel_id=1, source_target_pairs={{0,16},{8,24},{16,0},{24,8},{1,17},{9,25},{17,1},{25,9},{2,18},{10... | collective-permute-start | bytes 872 | tf_op jit(solution)/shard_map/ppermute | solution.py:56
  519.8 7.4 %collective-permute-done.52 = f32[72]{0:T(128)S(1)} collective-permute-done((f32[72]{0:T(128)S(1)}, f32[72]{0:T(128)S(1)}, u32[]{:S(2)}, u32[]{:S(2)}) %collective-permute-start.52) | collective-permute-done | bytes 320 | tf_op jit(solution)/shard_map/ppermute | solution.py:56
  (510 shorter events, 272.6 us)
Async XLA Ops:
  7.2 93.5 %all-gather.4.cloned.1.call-start = ((), (), s32[]{:S(2)}) async-start(), calls=%async_computation.3 | async-start | bytes 9732096 | tf_op jit(solution)/shard_map/all_gather | solution.py:252
  13.0 27.5 %collective-permute-start = (bf16[32,4224]{1,0:T(8,128)(2,1)S(1)}, bf16[32,4224]{1,0:T(8,128)(2,1)S(1)}, u32[]{:S(2)}, u32[]{:S(2)}) collective-permute-start(bf16[32,4224]{1,0:T(8,128)(2,1)S(1)} %concatenate.103), channel_id=1, source_target_pairs={{0,8},{8,16},{24,0},{1,9},{9,17},{25,1},{2,10},{10,18},{26,2},{3,1... | collective-permute-start | bytes 811016 | tf_op jit(solution)/shard_map/ppermute | solution.py:78
  14.3 26.2 %collective-permute-start.1 = (bf16[32,4224]{1,0:T(8,128)(2,1)S(1)}, bf16[32,4224]{1,0:T(8,128)(2,1)}, u32[]{:S(2)}, u32[]{:S(2)}) collective-permute-start(bf16[32,4224]{1,0:T(8,128)(2,1)S(1)} %concatenate.103), channel_id=1, source_target_pairs={{0,16},{16,0},{24,8},{1,17},{17,1},{25,9},{2,18},{18,2},{26,10},{3... | collective-permute-start | bytes 811016 | tf_op jit(solution)/shard_map/ppermute | solution.py:78
  44.1 101.6 %all-gather.6.cloned.1.call-start = ((), (), s32[]{:S(2)}) async-start(), calls=%async_computation.4 | async-start | bytes 4718592 | tf_op jit(solution)/shard_map/all_gather | solution.py:252
  78.0 60.2 %collective-permute-start.14 = (bf16[32,6144]{1,0:T(8,128)(2,1)}, bf16[32,6144]{1,0:T(8,128)(2,1)}, u32[]{:S(2)}, u32[]{:S(2)}) collective-permute-start(bf16[32,6144]{1,0:T(8,128)(2,1)} %get-tuple-element.226), channel_id=1, source_target_pairs={{0,8},{8,16},{24,0},{1,9},{9,17},{25,1},{2,10},{10,18},{26,2},{3,1... | collective-permute-start | bytes 1179656 | tf_op jit(solution)/shard_map/ppermute | solution.py:78
  85.5 52.7 %collective-permute-start.15 = (bf16[32,6144]{1,0:T(8,128)(2,1)}, bf16[32,6144]{1,0:T(8,128)(2,1)}, u32[]{:S(2)}, u32[]{:S(2)}) collective-permute-start(bf16[32,6144]{1,0:T(8,128)(2,1)} %get-tuple-element.226), channel_id=1, source_target_pairs={{0,16},{16,0},{24,8},{1,17},{17,1},{25,9},{2,18},{18,2},{26,10},{3... | collective-permute-start | bytes 1179656 | tf_op jit(solution)/shard_map/ppermute | solution.py:78
  91.6 46.6 %collective-permute-start.16 = (bf16[32,6144]{1,0:T(8,128)(2,1)}, bf16[32,6144]{1,0:T(8,128)(2,1)}, u32[]{:S(2)}, u32[]{:S(2)}) collective-permute-start(bf16[32,6144]{1,0:T(8,128)(2,1)} %get-tuple-element.226), channel_id=1, source_target_pairs={{8,0},{16,8},{24,16},{9,1},{17,9},{25,17},{10,2},{18,10},{26,18},{... | collective-permute-start | bytes 1179656 | tf_op jit(solution)/shard_map/ppermute | solution.py:78
  102.3 129.8 %all-gather.8.cloned.1.call-start = ((), (), s32[]{:S(2)}) async-start(), calls=%async_computation.5 | async-start | bytes 14155776 | tf_op jit(solution)/shard_map/all_gather | solution.py:252
  116.0 22.2 %collective-permute-start.13 = (bf16[2,512,128]{2,1,0:T(8,128)(2,1)S(1)}, bf16[2,512,128]{2,1,0:T(8,128)(2,1)S(1)}, u32[]{:S(2)}, u32[]{:S(2)}) collective-permute-start(bf16[2,512,128]{2,1,0:T(8,128)(2,1)S(1)} %maximum_select_fusion.4), channel_id=1, source_target_pairs={{0,2},{1,3},{2,0},{3,1},{4,6},{5,7},{6,4},{7,5},{8,10},{9,11},{10,... | collective-permute-start | bytes 786440 | tf_op jit(solution)/shard_map/ppermute | solution.py:56
  145.7 220.6 %reduce-scatter.4.cloned.1.call-start = ((), (), s32[]{:S(2)}) async-start(), calls=%async_computation.6 | async-start | bytes 14155776 | tf_op jit(solution)/shard_map/reduce_scatter | solution.py:248
  148.5 24.4 %collective-permute-start.19 = (bf16[128,1024]{1,0:T(8,128)(2,1)}, bf16[128,1024]{1,0:T(8,128)(2,1)}, u32[]{:S(2)}, u32[]{:S(2)}) collective-permute-start(bf16[128,1024]{1,0:T(8,128)(2,1)} %get-tuple-element.550), channel_id=1, source_target_pairs={{0,8},{8,16},{24,0},{1,9},{9,17},{25,1},{2,10},{10,18},{26,2},{3,1... | collective-permute-start | bytes 786440 | tf_op jit(solution)/shard_map/ppermute | solution.py:78
  262.5 182.3 %reduce-scatter.6.cloned.1.call-start = ((), (), s32[]{:S(2)}) async-start(), calls=%async_computation.7 | async-start | bytes 8257536 | tf_op jit(solution)/shard_map/reduce_scatter | solution.py:248
  291.4 22.4 %collective-permute-start.25 = (bf16[144,1536]{1,0:T(8,128)(2,1)S(1)}, bf16[144,1536]{1,0:T(8,128)(2,1)S(1)}, u32[]{:S(2)}, u32[]{:S(2)}) collective-permute-start(bf16[144,1536]{1,0:T(8,128)(2,1)S(1)} %get-tuple-element.280), channel_id=1, source_target_pairs={{0,2},{1,3},{2,0},{3,1},{4,6},{5,7},{6,4},{7,5},{8,10},{9,11},{10,... | collective-permute-start | bytes 1327112 | tf_op jit(solution)/shard_map/ppermute | solution.py:56
  315.2 23.3 %collective-permute-start.27 = (bf16[4,512,128]{2,1,0:T(8,128)(2,1)S(1)}, bf16[4,512,128]{2,1,0:T(8,128)(2,1)S(1)}, u32[]{:S(2)}, u32[]{:S(2)}) collective-permute-start(bf16[4,512,128]{2,1,0:T(8,128)(2,1)S(1)} %dynamic-slice_bitcast_fusion.1), channel_id=1, source_target_pairs={{0,1},{1,0},{2,3},{3,2},{4,5},{5,4},{6,7},{7,6},{8,9},{9,8},{10,11... | collective-permute-start | bytes 1572872 | tf_op jit(solution)/shard_map/ppermute | solution.py:56
  315.2 23.2 %collective-permute-start.26 = (bf16[144,1536]{1,0:T(8,128)(2,1)S(1)}, bf16[144,1536]{1,0:T(8,128)(2,1)S(1)}, u32[]{:S(2)}, u32[]{:S(2)}) collective-permute-start(bf16[144,1536]{1,0:T(8,128)(2,1)S(1)} %get-tuple-element.290), channel_id=1, source_target_pairs={{0,4},{1,5},{2,6},{3,7},{4,0},{5,1},{6,2},{7,3},{8,12},{9,13},{10,... | collective-permute-start | bytes 1327112 | tf_op jit(solution)/shard_map/ppermute | solution.py:56
  366.3 138.5 %reduce-scatter.8.cloned.1.call-start = ((), (), s32[]{:S(2)}) async-start(), calls=%async_computation.8 | async-start | bytes 6193152 | tf_op jit(solution)/shard_map/reduce_scatter | solution.py:248
  370.2 34.1 %collective-permute-start.30 = (bf16[512,256]{1,0:T(8,128)(2,1)}, bf16[512,256]{1,0:T(8,128)(2,1)}, u32[]{:S(2)}, u32[]{:S(2)}) collective-permute-start(bf16[512,256]{1,0:T(8,128)(2,1)} %get-tuple-element.520), channel_id=1, source_target_pairs={{0,4},{1,5},{2,6},{3,7},{4,0},{5,1},{6,2},{7,3},{8,12},{9,13},{10,... | collective-permute-start | bytes 786440 | tf_op jit(solution)/shard_map/ppermute | solution.py:56
  374.3 30.0 %collective-permute-start.31 = (bf16[512,256]{1,0:T(8,128)(2,1)}, bf16[512,256]{1,0:T(8,128)(2,1)}, u32[]{:S(2)}, u32[]{:S(2)}) collective-permute-start(bf16[512,256]{1,0:T(8,128)(2,1)} %get-tuple-element.518), channel_id=1, source_target_pairs={{0,6},{1,7},{2,4},{3,5},{4,2},{5,3},{6,0},{7,1},{8,14},{9,15},{10,... | collective-permute-start | bytes 786440 | tf_op jit(solution)/shard_map/ppermute | solution.py:56
  374.4 29.9 %collective-permute-start.32 = (bf16[32,6144]{1,0:T(8,128)(2,1)S(1)}, bf16[32,6144]{1,0:T(8,128)(2,1)}, u32[]{:S(2)}, u32[]{:S(2)}) collective-permute-start(bf16[32,6144]{1,0:T(8,128)(2,1)S(1)} %get-tuple-element.509), channel_id=1, source_target_pairs={{0,8},{8,16},{16,24},{1,9},{9,17},{17,25},{2,10},{10,18},{18,26},{... | collective-permute-start | bytes 1179656 | tf_op jit(solution)/shard_map/ppermute | solution.py:78
  375.7 34.5 %collective-permute-start.33 = (bf16[32,6144]{1,0:T(8,128)(2,1)S(1)}, bf16[32,6144]{1,0:T(8,128)(2,1)}, u32[]{:S(2)}, u32[]{:S(2)}) collective-permute-start(bf16[32,6144]{1,0:T(8,128)(2,1)S(1)} %get-tuple-element.508), channel_id=1, source_target_pairs={{0,16},{8,24},{16,0},{1,17},{9,25},{17,1},{2,18},{10,26},{18,2},{3... | collective-permute-start | bytes 1179656 | tf_op jit(solution)/shard_map/ppermute | solution.py:78
  377.4 32.8 %collective-permute-start.34 = (bf16[32,6144]{1,0:T(8,128)(2,1)S(1)}, bf16[32,6144]{1,0:T(8,128)(2,1)}, u32[]{:S(2)}, u32[]{:S(2)}) collective-permute-start(bf16[32,6144]{1,0:T(8,128)(2,1)S(1)} %get-tuple-element.507), channel_id=1, source_target_pairs={{0,24},{8,0},{16,8},{1,25},{9,1},{17,9},{2,26},{10,2},{18,10},{3,2... | collective-permute-start | bytes 1179656 | tf_op jit(solution)/shard_map/ppermute | solution.py:78
  419.3 25.5 %collective-permute-start.36 = (bf16[128,1024]{1,0:T(8,128)(2,1)}, bf16[128,1024]{1,0:T(8,128)(2,1)}, u32[]{:S(2)}, u32[]{:S(2)}) collective-permute-start(bf16[128,1024]{1,0:T(8,128)(2,1)} %get-tuple-element.516), channel_id=1, source_target_pairs={{0,16},{8,24},{16,0},{1,17},{9,25},{17,1},{2,18},{10,26},{18,2},{3... | collective-permute-start | bytes 786440 | tf_op jit(solution)/shard_map/ppermute | solution.py:78
  420.6 24.2 %collective-permute-start.37 = (bf16[128,1024]{1,0:T(8,128)(2,1)}, bf16[128,1024]{1,0:T(8,128)(2,1)}, u32[]{:S(2)}, u32[]{:S(2)}) collective-permute-start(bf16[128,1024]{1,0:T(8,128)(2,1)} %get-tuple-element.515), channel_id=1, source_target_pairs={{0,24},{8,0},{16,8},{1,25},{9,1},{17,9},{2,26},{10,2},{18,10},{3,2... | collective-permute-start | bytes 786440 | tf_op jit(solution)/shard_map/ppermute | solution.py:78
  481.8 23.1 %collective-permute-start.45 = (bf16[128,1024]{1,0:T(8,128)(2,1)S(1)}, bf16[128,1024]{1,0:T(8,128)(2,1)S(1)}, u32[]{:S(2)}, u32[]{:S(2)}) collective-permute-start(bf16[128,1024]{1,0:T(8,128)(2,1)S(1)} %get-tuple-element.512), channel_id=1, source_target_pairs={{0,16},{8,24},{16,0},{1,17},{9,25},{17,1},{2,18},{10,26},{18,2},{3... | collective-permute-start | bytes 786440 | tf_op jit(solution)/shard_map/ppermute | solution.py:78
  (115 other events, 1366.7 us)
Sparse Core Ops, SparseCore 0:
  44.2 56.4 all-gather.3
  102.6 42.9 all-gather.5
  147.6 84.5 all-gather.7
  262.6 103.5 reduce-scatter.3
  369.5 66.9 reduce-scatter.5
  445.0 59.6 reduce-scatter.7

commit v4 on v3

--- a/solution.py
+++ b/solution.py
@@ -1431,7 +1431,6 @@
     rim_came = shifted(rim_back, "wide", -1)
     out_back = FromBlocks(out_low, micro_count)
     d_kv = chip_sum.end()
-    own_ffn = own_ffn.end()
     d_scan = lax.dynamic_update_slice(d_scan, (edge + rim_came).astype(LOW), (block_tok - 8, 0))
     grad_small = jnp.concatenate(
         [
@@ -1446,13 +1445,13 @@
     )
     late = last_grads(block_in, d_scan, d_query, d_kv, grad_small)
 
+    out_back.got, late, part_early, d_scan, grad_head, grad_skip, own_ffn.got, own_ffn.own = tied(
+        out_back.got, late, part_early, d_scan, grad_head, grad_skip, own_ffn.got, own_ffn.own
+    )
+    part_late = sum_wide(late)
     head_sums = jnp.concatenate(
         [grad_head[:2, :heads].reshape(-1), jnp.sum(grad_skip[0].reshape(heads, -1), axis=1)]
     )
-    out_back.got, late, part_early, d_scan, own_ffn, head_sums = tied(
-        out_back.got, late, part_early, d_scan, own_ffn, head_sums
-    )
-    part_late = sum_wide(late)
     totals = EverySum(head_sums)
     totals.begin()
     totals.got, part_early, d_scan = tied(totals.got, part_early, d_scan)
@@ -1462,7 +1461,8 @@
     grad_x = input_back(d_scan, d_gate_z, d_query, d_kv, w_in, x_tokens, d_resid, gain_in_all[None])
     own_early.got, own_early.own, totals.got, grad_x = tied(own_early.got, own_early.own, totals.got, grad_x)
     totals.end()
-    x_plain, own_ffn = tied(plain(grad_x), own_ffn)
+    x_plain, own_ffn.got, own_ffn.own = tied(plain(grad_x), own_ffn.got, own_ffn.own)
+    own_ffn = own_ffn.end()
     x_back = FromBlocks(x_plain, micro_count)
     totals.begin()
     g_ffn = split_at(own_ffn, (width,) * (3 * folds), 1)

time: 548 us -> 546 us (level)
    unnamed x167 -> x189, local copies, waits for them, and re-layouts: 15.8 us -> 17.7 us
  transfers between devices with their start and end apart: 59 -> 59, of which waited for: 19 -> 18; matrix products, arithmetic and copies ran while one was open for 23% -> 22% of each run, Pallas kernels for 20% -> 20%
where the time goes in v4:
time: 546 us; the launch traced here: 537 us
  Pallas kernels  138 us (25%)
  waiting for transfers between devices  119 us (22%)
  starting transfers between devices  116 us (21%)
  local copies, waits for them, and re-layouts  65.2 us (12%)
  matrix products  45.9 us (8%)
  other arithmetic  36.6 us (7%)
  between operations  16.6 us (3%)
    ppermute x30, starting transfers between devices, sent_on(): got.append(lax.ppermute(pieces((place + step) % count), 'head', pairs))  76.7 us
    pallas_call x4, Pallas kernels, call(): pl.pallas_call(kernel, grid=(parts,), in_specs=[spec(block, how) for _, b...  59.2 us
    ppermute x21, waiting for transfers between devices, swapped(): return lax.ppermute(value, axis, [(i, i ^ bit) for i in range(count)])  49.9 us
    ppermute x30, waiting for transfers between devices, sent_on(): got.append(lax.ppermute(pieces((place + step) % count), 'head', pairs))  39.7 us
    ppermute x21, starting transfers between devices, swapped(): return lax.ppermute(value, axis, [(i, i ^ bit) for i in range(count)])  36.2 us
    pallas_call x1, Pallas kernels, feed_forward(): pl.pallas_call(feed_kernel, grid=(folds,), in_specs=[whole, whole, whole,...  30.4 us
    dot_general x12, matrix products, nn(): return jnp.dot(left, right, preferred_element_type=jnp.float32)  28.5 us
    unnamed x189, local copies, waits for them, and re-layouts  17.7 us
  transfers between devices with their start and end apart: 59, of which 18 were waited for; matrix products, arithmetic and copies ran while one was open for 22% of the time, Pallas kernels for 20%

profile of v4, /device:TPU:24, one launch (start us, length us, event | category | flops | bytes accessed | tf_op | source)
XLA Modules:
  0.0 536.8 jit_solution(8060026241202048621)
XLA Ops:
  55.4 6.7 %collective-permute-start.6 = (bf16[128,1024]{1,0:T(8,128)(2,1)S(1)}, bf16[128,1024]{1,0:T(8,128)(2,1)S(1)}, u32[]{:S(2)}, u32[]{:S(2)}) collective-permute-start(bf16[128,1024]{1,0:T(8,128)(2,1)S(1)} %get-tuple-element.569), channel_id=1, source_target_pairs={{0,8},{8,16},{24,0},{1,9},{9,17},{25,1},{2,10},{10,18},{26,2},{3,1... | collective-permute-start | bytes 786440 | tf_op jit(solution)/shard_map/ppermute | solution.py:78
  78.0 7.5 %collective-permute-start.14 = (bf16[32,6144]{1,0:T(8,128)(2,1)}, bf16[32,6144]{1,0:T(8,128)(2,1)}, u32[]{:S(2)}, u32[]{:S(2)}) collective-permute-start(bf16[32,6144]{1,0:T(8,128)(2,1)} %get-tuple-element.233), channel_id=1, source_target_pairs={{0,8},{8,16},{24,0},{1,9},{9,17},{25,1},{2,10},{10,18},{26,2},{3,1... | collective-permute-start | bytes 1179656 | tf_op jit(solution)/shard_map/ppermute | solution.py:78
  85.5 6.1 %collective-permute-start.15 = (bf16[32,6144]{1,0:T(8,128)(2,1)}, bf16[32,6144]{1,0:T(8,128)(2,1)}, u32[]{:S(2)}, u32[]{:S(2)}) collective-permute-start(bf16[32,6144]{1,0:T(8,128)(2,1)} %get-tuple-element.233), channel_id=1, source_target_pairs={{0,16},{16,0},{24,8},{1,17},{17,1},{25,9},{2,18},{18,2},{26,10},{3... | collective-permute-start | bytes 1179656 | tf_op jit(solution)/shard_map/ppermute | solution.py:78
  118.5 5.3 fusion.26.z_ref
  127.2 10.9 %mamba_local.1 = (f32[512,1536]{1,0:T(8,128)}, bf16[512,1536]{1,0:T(8,128)(2,1)}, bf16[512,256]{1,0:T(8,128)(2,1)}, bf16[512,256]{1,0:T(8,128)(2,1)}, f32[512,12...) custom-call(f32[512,1920]{1,0:T(8,128)} %copy-done.80, ...), custom_call_target="tpu_custom_call" | custom-call | flops 11000000512 | bytes 33000000 | tf_op jit(solution)/shard_map/mamba_local/pallas_call | solution.py:652
  172.8 12.1 %collective-permute-done.18.got_ref = bf16[144,1536]{1,0:T(8,128)(2,1)S(1)} collective-permute-done((bf16[144,1536]{1,0:T(8,128)(2,1)S(1)}, bf16[144,1536]{1,0:T(8,128)(2,1)S(1)}, u32[]{:S(2)}, u32[]{:S(2)}) %collective-permute-start.18) | collective-permute-done | bytes 442400 | tf_op jit(solution)/shard_map/ppermute | solution.py:56
  196.1 5.6 %collective-permute-done.23.got_ref = bf16[144,1536]{1,0:T(8,128)(2,1)S(1)} collective-permute-done((bf16[144,1536]{1,0:T(8,128)(2,1)S(1)}, bf16[144,1536]{1,0:T(8,128)(2,1)S(1)}, u32[]{:S(2)}, u32[]{:S(2)}) %collective-permute-start.23) | collective-permute-done | bytes 442400 | tf_op jit(solution)/shard_map/ppermute | solution.py:56
  204.3 11.2 %mamba_mix.1 = (bf16[512,1536]{1,0:T(8,128)(2,1)}, f32[512,1536]{1,0:T(8,128)}, bf16[4,128,1536]{2,1,0:T(8,128)(2,1)}) custom-call(f32[512,1536]{1,0:T(8,128)} %get-tuple-element.245.act_ref, bf16[512,256]{1,0:T(8,128)(2,1)} %get-tuple-element.246.bcact_ref, f32[512,1536]{1,0:T(8,128)} %fusion.26.z_ref, f32[512,128]{1,0:T(8,128)} %get-tuple-element.248.step_ref, ...), custom_call_target="tpu_custom_call" | custom-call | flops 11000000512 | bytes 33000000 | tf_op jit(solution)/shard_map/mamba_mix/pallas_call | solution.py:652
  224.1 8.0 %all-gather.8.cloned.1.call-done.w_ref = bf16[1024,6144]{1,0:T(8,128)(2,1)} async-done(((bf16[128,6144]{1,0:T(8,128)(2,1)}), bf16[1024,6144]{1,0:T(8,128)(2,1)}) %all-gather.8.cloned.1.call-update) | async-done | bytes 12582928 | tf_op jit(solution)/shard_map/all_gather | solution.py:252
  232.1 30.4 %feed_forward.1 = (f32[512,1024]{1,0:T(8,128)}, f32[512,1024]{1,0:T(8,128)}, bf16[1024,6144]{1,0:T(8,128)(2,1)}) custom-call(bf16[512,1024]{1,0:T(8,128)(2,1)} %multiply_convert_fusion.x_ref, bf16[512,1024]{1,0:T(8,128)(2,1)} %fusion.43.gy_ref, bf16[512,1024]{1,0:T(8,128)(2,1)} %bitcast.333, bf16[1024,6144]{1,0:T(8,128)(2,1)} %all-gather.8.cloned.1.call-done.w_ref), custom_call_target="tpu_custom_call" | custom-call | flops 35000000512 | bytes 105000000 | tf_op jit(solution)/shard_map/feed_forward/pallas_call | solution.py:1077
  272.9 12.7 %mamba_gate_back.1 = (bf16[512,1536]{1,0:T(8,128)(2,1)}, f32[512,1536]{1,0:T(8,128)}, bf16[144,1536]{1,0:T(8,128)(2,1)}, f32[128,1536]{1,0:T(8,128)}, f32[8,1536]{1,0:T(8,128)}) custom-call(f32[512,1536]{1,0:T(8,128)} %fusion.169.dym_ref, f32[512,1536]{1,0:T(8,128)} %get-tuple-element.277.y_ref, f32[512,1536]{1,0:T(8,128)} %fusion.26.z_ref, ...), custom_call_target="tpu_custom_call" | custom-call | flops 11000000512 | bytes 33000000 | tf_op jit(solution)/shard_map/mamba_gate_back/pallas_call | solution.py:652
  293.8 7.2 %attend_back.2 = (bf16[4,64,512]{2,1,0:T(8,128)(2,1)}, bf16[4096,128]{1,0:T(8,128)(2,1)}) custom-call(s32[1]{0:T(128)} %bitcast.56.place_ref, bf16[4,128,512]{2,1,0:T(8,128)(2,1)} %get-tuple-element.288.qb_ref, bf16[8,64,512]{2,1,0:T(8,128)(2,1)} %bitcast.375, f32[4,64,512]{2,1,0:T(8,128)} %get-tuple-element.273.o_ref, bf16[4096,256]{1,0:T(8,128)(2,1)} %bitcast.325, ...), custom_call_target="tpu_custom_call" | custom-call | flops 27000000512 | bytes 81000000 | tf_op jit(solution)/shard_map/attend_back/pallas_call | solution.py:1017
  300.9 12.8 %collective-permute-done.25.got_ref = bf16[144,1536]{1,0:T(8,128)(2,1)S(1)} collective-permute-done((bf16[144,1536]{1,0:T(8,128)(2,1)S(1)}, bf16[144,1536]{1,0:T(8,128)(2,1)S(1)}, u32[]{:S(2)}, u32[]{:S(2)}) %collective-permute-start.25) | collective-permute-done | bytes 442400 | tf_op jit(solution)/shard_map/ppermute | solution.py:56
  319.5 6.7 %attend_back.3 = (bf16[4,64,512]{2,1,0:T(8,128)(2,1)}, bf16[4096,128]{1,0:T(8,128)(2,1)}) custom-call(s32[1]{0:T(128)} %bitcast.56.place_ref, bf16[4,128,512]{2,1,0:T(8,128)(2,1)} %get-tuple-element.298.qb_ref, bf16[8,64,512]{2,1,0:T(8,128)(2,1)} %bitcast.376, f32[4,64,512]{2,1,0:T(8,128)} %get-tuple-element.274.o_ref, bf16[4096,256]{1,0:T(8,128)(2,1)} %bitcast.326, ...), custom_call_target="tpu_custom_call" | custom-call | flops 27000000512 | bytes 81000000 | tf_op jit(solution)/shard_map/attend_back/pallas_call | solution.py:1017
  326.2 12.2 %collective-permute-done.26.got_ref = bf16[144,1536]{1,0:T(8,128)(2,1)S(1)} collective-permute-done((bf16[144,1536]{1,0:T(8,128)(2,1)S(1)}, bf16[144,1536]{1,0:T(8,128)(2,1)S(1)}, u32[]{:S(2)}, u32[]{:S(2)}) %collective-permute-start.26) | collective-permute-done | bytes 442400 | tf_op jit(solution)/shard_map/ppermute | solution.py:56
  353.3 12.9 %reduce-scatter.4.cloned.1.call-done = bf16[128,6144]{1,0:T(8,128)(2,1)} async-done(((bf16[1024,6144]{1,0:T(8,128)(2,1)}), bf16[128,6144]{1,0:T(8,128)(2,1)}) %reduce-scatter.4.cloned.1.call-update) | async-done | bytes 1572880 | tf_op jit(solution)/shard_map/reduce_scatter | solution.py:248
  379.5 24.3 %mamba_scan_back.1 = (bf16[512,1920]{1,0:T(8,128)(2,1)}, f32[8,1536]{1,0:T(8,128)}, f32[8,128]{1,0:T(8,128)}, f32[8,1792]{1,0:T(8,128)}, f32[8,1792]{1,0:T(8,128)}, /*index=5*/f32[8,1792]{1,0:T(8,128)}) custom-call(f32[512,1536]{1,0:T(8,128)} %get-tuple-element.245.act_ref, bf16[512,1536]{1,0:T(8,128)(2,1)} %get-tuple-element.316.slope_ref, ...), custom_call_target="tpu_custom_call" | custom-call | flops 23000000512 | bytes 69000000 | tf_op jit(solution)/shard_map/mamba_scan_back/pallas_call | solution.py:652
  404.9 6.5 %collective-permute-done.33 = bf16[32,6144]{1,0:T(8,128)(2,1)} collective-permute-done((bf16[32,6144]{1,0:T(8,128)(2,1)}, bf16[32,6144]{1,0:T(8,128)(2,1)}, u32[]{:S(2)}, u32[]{:S(2)}) %collective-permute-start.33) | collective-permute-done | bytes 393248 | tf_op jit(solution)/shard_map/ppermute | solution.py:78
  422.4 8.4 %last_grads.1 = bf16[1024,2688]{1,0:T(8,128)(2,1)} custom-call(bf16[512,1024]{1,0:T(8,128)(2,1)} %copy-done.36, bf16[512,1920]{1,0:T(8,128)(2,1)} %fusion.104.scan_ref, bf16[512,512]{1,0:T(8,128)(2,1)} %bitcast.347, bf16[512,256]{1,0:T(8,128)(2,1)} %fusion.58.kv_ref, f32[1024,128]{1,0:T(8,128)} %pad.33.small_ref), custom_call_target="tpu_custom_call" | custom-call | flops 8000000000 | bytes 24000000 | tf_op jit(solution)/shard_map/last_grads/pallas_call | solution.py:1107
  430.8 11.5 %collective-permute-done.36 = bf16[128,1024]{1,0:T(8,128)(2,1)S(1)} collective-permute-done((bf16[128,1024]{1,0:T(8,128)(2,1)}, bf16[128,1024]{1,0:T(8,128)(2,1)S(1)}, u32[]{:S(2)}, u32[]{:S(2)}) %collective-permute-start.36) | collective-permute-done | bytes 262176 | tf_op jit(solution)/shard_map/ppermute | solution.py:78
  456.8 12.0 %input_back.1 = bf16[512,1024]{1,0:T(8,128)(2,1)} custom-call(bf16[512,1920]{1,0:T(8,128)(2,1)} %fusion.104.scan_ref, bf16[512,1536]{1,0:T(8,128)(2,1)} %get-tuple-element.311.gate_ref, bf16[512,512]{1,0:T(8,128)(2,1)} %bitcast.348, bf16[512,256]{1,0:T(8,128)(2,1)} %fusion.58.kv_ref, bf16[1024,4224]{1,0:T(8,128)(2,1)} %all-gather.4.cloned.1.call-done.w_ref, ...), custom_call_target="tpu_custom_call" | custom-call | flops 10000000000 | bytes 30000000 | tf_op jit(solution)/shard_map/input_back/pallas_call | solution.py:1134
  468.9 6.1 %collective-permute-done.41 = bf16[32,3584]{1,0:T(8,128)(2,1)S(1)} collective-permute-done((bf16[32,3584]{1,0:T(8,128)(2,1)S(1)}, bf16[32,3584]{1,0:T(8,128)(2,1)S(1)}, u32[]{:S(2)}, u32[]{:S(2)}) %collective-permute-start.41) | collective-permute-done | bytes 229408 | tf_op jit(solution)/shard_map/ppermute | solution.py:78
  511.7 6.9 %collective-permute-start.52 = (f32[72]{0:T(128)S(1)}, f32[72]{0:T(128)S(1)}, u32[]{:S(2)}, u32[]{:S(2)}) collective-permute-start(f32[72]{0:T(128)S(1)} %add.645), channel_id=1, source_target_pairs={{0,16},{8,24},{16,0},{24,8},{1,17},{9,25},{17,1},{25,9},{2,18},{10... | collective-permute-start | bytes 872 | tf_op jit(solution)/shard_map/ppermute | solution.py:56
  519.3 6.1 %collective-permute-done.52 = f32[72]{0:T(128)S(1)} collective-permute-done((f32[72]{0:T(128)S(1)}, f32[72]{0:T(128)S(1)}, u32[]{:S(2)}, u32[]{:S(2)}) %collective-permute-start.52) | collective-permute-done | bytes 320 | tf_op jit(solution)/shard_map/ppermute | solution.py:56
  (532 shorter events, 270.0 us)
Async XLA Ops:
  7.2 93.5 %all-gather.4.cloned.1.call-start = ((), (), s32[]{:S(2)}) async-start(), calls=%async_computation.3 | async-start | bytes 9732096 | tf_op jit(solution)/shard_map/all_gather | solution.py:252
  13.0 27.5 %collective-permute-start = (bf16[32,4224]{1,0:T(8,128)(2,1)S(1)}, bf16[32,4224]{1,0:T(8,128)(2,1)S(1)}, u32[]{:S(2)}, u32[]{:S(2)}) collective-permute-start(bf16[32,4224]{1,0:T(8,128)(2,1)S(1)} %concatenate.103), channel_id=1, source_target_pairs={{0,8},{8,16},{24,0},{1,9},{9,17},{25,1},{2,10},{10,18},{26,2},{3,1... | collective-permute-start | bytes 811016 | tf_op jit(solution)/shard_map/ppermute | solution.py:78
  14.3 26.2 %collective-permute-start.1 = (bf16[32,4224]{1,0:T(8,128)(2,1)S(1)}, bf16[32,4224]{1,0:T(8,128)(2,1)}, u32[]{:S(2)}, u32[]{:S(2)}) collective-permute-start(bf16[32,4224]{1,0:T(8,128)(2,1)S(1)} %concatenate.103), channel_id=1, source_target_pairs={{0,16},{16,0},{24,8},{1,17},{17,1},{25,9},{2,18},{18,2},{26,10},{3... | collective-permute-start | bytes 811016 | tf_op jit(solution)/shard_map/ppermute | solution.py:78
  44.1 101.6 %all-gather.6.cloned.1.call-start = ((), (), s32[]{:S(2)}) async-start(), calls=%async_computation.4 | async-start | bytes 4718592 | tf_op jit(solution)/shard_map/all_gather | solution.py:252
  78.0 60.2 %collective-permute-start.14 = (bf16[32,6144]{1,0:T(8,128)(2,1)}, bf16[32,6144]{1,0:T(8,128)(2,1)}, u32[]{:S(2)}, u32[]{:S(2)}) collective-permute-start(bf16[32,6144]{1,0:T(8,128)(2,1)} %get-tuple-element.233), channel_id=1, source_target_pairs={{0,8},{8,16},{24,0},{1,9},{9,17},{25,1},{2,10},{10,18},{26,2},{3,1... | collective-permute-start | bytes 1179656 | tf_op jit(solution)/shard_map/ppermute | solution.py:78
  85.5 52.7 %collective-permute-start.15 = (bf16[32,6144]{1,0:T(8,128)(2,1)}, bf16[32,6144]{1,0:T(8,128)(2,1)}, u32[]{:S(2)}, u32[]{:S(2)}) collective-permute-start(bf16[32,6144]{1,0:T(8,128)(2,1)} %get-tuple-element.233), channel_id=1, source_target_pairs={{0,16},{16,0},{24,8},{1,17},{17,1},{25,9},{2,18},{18,2},{26,10},{3... | collective-permute-start | bytes 1179656 | tf_op jit(solution)/shard_map/ppermute | solution.py:78
  91.6 46.6 %collective-permute-start.16 = (bf16[32,6144]{1,0:T(8,128)(2,1)}, bf16[32,6144]{1,0:T(8,128)(2,1)}, u32[]{:S(2)}, u32[]{:S(2)}) collective-permute-start(bf16[32,6144]{1,0:T(8,128)(2,1)} %get-tuple-element.233), channel_id=1, source_target_pairs={{8,0},{16,8},{24,16},{9,1},{17,9},{25,17},{10,2},{18,10},{26,18},{... | collective-permute-start | bytes 1179656 | tf_op jit(solution)/shard_map/ppermute | solution.py:78
  102.3 129.8 %all-gather.8.cloned.1.call-start = ((), (), s32[]{:S(2)}) async-start(), calls=%async_computation.5 | async-start | bytes 14155776 | tf_op jit(solution)/shard_map/all_gather | solution.py:252
  116.0 22.2 %collective-permute-start.13 = (bf16[2,512,128]{2,1,0:T(8,128)(2,1)S(1)}, bf16[2,512,128]{2,1,0:T(8,128)(2,1)S(1)}, u32[]{:S(2)}, u32[]{:S(2)}) collective-permute-start(bf16[2,512,128]{2,1,0:T(8,128)(2,1)S(1)} %maximum_select_fusion.4), channel_id=1, source_target_pairs={{0,2},{1,3},{2,0},{3,1},{4,6},{5,7},{6,4},{7,5},{8,10},{9,11},{10,... | collective-permute-start | bytes 786440 | tf_op jit(solution)/shard_map/ppermute | solution.py:56
  145.7 220.5 %reduce-scatter.4.cloned.1.call-start = ((), (), s32[]{:S(2)}) async-start(), calls=%async_computation.6 | async-start | bytes 14155776 | tf_op jit(solution)/shard_map/reduce_scatter | solution.py:248
  148.5 24.3 %collective-permute-start.19 = (bf16[128,1024]{1,0:T(8,128)(2,1)}, bf16[128,1024]{1,0:T(8,128)(2,1)}, u32[]{:S(2)}, u32[]{:S(2)}) collective-permute-start(bf16[128,1024]{1,0:T(8,128)(2,1)} %get-tuple-element.565), channel_id=1, source_target_pairs={{0,8},{8,16},{24,0},{1,9},{9,17},{25,1},{2,10},{10,18},{26,2},{3,1... | collective-permute-start | bytes 786440 | tf_op jit(solution)/shard_map/ppermute | solution.py:78
  262.5 179.9 %reduce-scatter.6.cloned.1.call-start = ((), (), s32[]{:S(2)}) async-start(), calls=%async_computation.7 | async-start | bytes 8257536 | tf_op jit(solution)/shard_map/reduce_scatter | solution.py:248
  291.4 22.4 %collective-permute-start.25 = (bf16[144,1536]{1,0:T(8,128)(2,1)S(1)}, bf16[144,1536]{1,0:T(8,128)(2,1)S(1)}, u32[]{:S(2)}, u32[]{:S(2)}) collective-permute-start(bf16[144,1536]{1,0:T(8,128)(2,1)S(1)} %get-tuple-element.287), channel_id=1, source_target_pairs={{0,2},{1,3},{2,0},{3,1},{4,6},{5,7},{6,4},{7,5},{8,10},{9,11},{10,... | collective-permute-start | bytes 1327112 | tf_op jit(solution)/shard_map/ppermute | solution.py:56
  315.1 23.3 %collective-permute-start.27 = (bf16[4,512,128]{2,1,0:T(8,128)(2,1)S(1)}, bf16[4,512,128]{2,1,0:T(8,128)(2,1)S(1)}, u32[]{:S(2)}, u32[]{:S(2)}) collective-permute-start(bf16[4,512,128]{2,1,0:T(8,128)(2,1)S(1)} %dynamic-slice_bitcast_fusion.1), channel_id=1, source_target_pairs={{0,1},{1,0},{2,3},{3,2},{4,5},{5,4},{6,7},{7,6},{8,9},{9,8},{10,11... | collective-permute-start | bytes 1572872 | tf_op jit(solution)/shard_map/ppermute | solution.py:56
  315.1 23.2 %collective-permute-start.26 = (bf16[144,1536]{1,0:T(8,128)(2,1)S(1)}, bf16[144,1536]{1,0:T(8,128)(2,1)S(1)}, u32[]{:S(2)}, u32[]{:S(2)}) collective-permute-start(bf16[144,1536]{1,0:T(8,128)(2,1)S(1)} %get-tuple-element.297), channel_id=1, source_target_pairs={{0,4},{1,5},{2,6},{3,7},{4,0},{5,1},{6,2},{7,3},{8,12},{9,13},{10,... | collective-permute-start | bytes 1327112 | tf_op jit(solution)/shard_map/ppermute | solution.py:56
  366.2 138.1 %reduce-scatter.8.cloned.1.call-start = ((), (), s32[]{:S(2)}) async-start(), calls=%async_computation.8 | async-start | bytes 6193152 | tf_op jit(solution)/shard_map/reduce_scatter | solution.py:248
  370.0 34.9 %collective-permute-start.30 = (bf16[512,256]{1,0:T(8,128)(2,1)}, bf16[512,256]{1,0:T(8,128)(2,1)}, u32[]{:S(2)}, u32[]{:S(2)}) collective-permute-start(bf16[512,256]{1,0:T(8,128)(2,1)} %get-tuple-element.535), channel_id=1, source_target_pairs={{0,4},{1,5},{2,6},{3,7},{4,0},{5,1},{6,2},{7,3},{8,12},{9,13},{10,... | collective-permute-start | bytes 786440 | tf_op jit(solution)/shard_map/ppermute | solution.py:56
  374.2 30.7 %collective-permute-start.31 = (bf16[512,256]{1,0:T(8,128)(2,1)}, bf16[512,256]{1,0:T(8,128)(2,1)}, u32[]{:S(2)}, u32[]{:S(2)}) collective-permute-start(bf16[512,256]{1,0:T(8,128)(2,1)} %get-tuple-element.533), channel_id=1, source_target_pairs={{0,6},{1,7},{2,4},{3,5},{4,2},{5,3},{6,0},{7,1},{8,14},{9,15},{10,... | collective-permute-start | bytes 786440 | tf_op jit(solution)/shard_map/ppermute | solution.py:56
  375.4 29.5 %collective-permute-start.32 = (bf16[32,6144]{1,0:T(8,128)(2,1)}, bf16[32,6144]{1,0:T(8,128)(2,1)S(1)}, u32[]{:S(2)}, u32[]{:S(2)}) collective-permute-start(bf16[32,6144]{1,0:T(8,128)(2,1)} %get-tuple-element.524), channel_id=1, source_target_pairs={{0,8},{8,16},{16,24},{1,9},{9,17},{17,25},{2,10},{10,18},{18,26},{... | collective-permute-start | bytes 1179656 | tf_op jit(solution)/shard_map/ppermute | solution.py:78
  376.7 34.8 %collective-permute-start.33 = (bf16[32,6144]{1,0:T(8,128)(2,1)}, bf16[32,6144]{1,0:T(8,128)(2,1)}, u32[]{:S(2)}, u32[]{:S(2)}) collective-permute-start(bf16[32,6144]{1,0:T(8,128)(2,1)} %get-tuple-element.523), channel_id=1, source_target_pairs={{0,16},{8,24},{16,0},{1,17},{9,25},{17,1},{2,18},{10,26},{18,2},{3... | collective-permute-start | bytes 1179656 | tf_op jit(solution)/shard_map/ppermute | solution.py:78
  378.0 33.4 %collective-permute-start.34 = (bf16[32,6144]{1,0:T(8,128)(2,1)}, bf16[32,6144]{1,0:T(8,128)(2,1)}, u32[]{:S(2)}, u32[]{:S(2)}) collective-permute-start(bf16[32,6144]{1,0:T(8,128)(2,1)} %get-tuple-element.522), channel_id=1, source_target_pairs={{0,24},{8,0},{16,8},{1,25},{9,1},{17,9},{2,26},{10,2},{18,10},{3,2... | collective-permute-start | bytes 1179656 | tf_op jit(solution)/shard_map/ppermute | solution.py:78
  417.3 25.0 %collective-permute-start.36 = (bf16[128,1024]{1,0:T(8,128)(2,1)}, bf16[128,1024]{1,0:T(8,128)(2,1)S(1)}, u32[]{:S(2)}, u32[]{:S(2)}) collective-permute-start(bf16[128,1024]{1,0:T(8,128)(2,1)} %get-tuple-element.531), channel_id=1, source_target_pairs={{0,16},{8,24},{16,0},{1,17},{9,25},{17,1},{2,18},{10,26},{18,2},{3... | collective-permute-start | bytes 786440 | tf_op jit(solution)/shard_map/ppermute | solution.py:78
  418.6 23.7 %collective-permute-start.37 = (bf16[128,1024]{1,0:T(8,128)(2,1)}, bf16[128,1024]{1,0:T(8,128)(2,1)S(1)}, u32[]{:S(2)}, u32[]{:S(2)}) collective-permute-start(bf16[128,1024]{1,0:T(8,128)(2,1)} %get-tuple-element.530), channel_id=1, source_target_pairs={{0,24},{8,0},{16,8},{1,25},{9,1},{17,9},{2,26},{10,2},{18,10},{3,2... | collective-permute-start | bytes 786440 | tf_op jit(solution)/shard_map/ppermute | solution.py:78
  481.3 23.0 %collective-permute-start.45 = (bf16[128,1024]{1,0:T(8,128)(2,1)S(1)}, bf16[128,1024]{1,0:T(8,128)(2,1)S(1)}, u32[]{:S(2)}, u32[]{:S(2)}) collective-permute-start(bf16[128,1024]{1,0:T(8,128)(2,1)S(1)} %get-tuple-element.527), channel_id=1, source_target_pairs={{0,16},{8,24},{16,0},{1,17},{9,25},{17,1},{2,18},{10,26},{18,2},{3... | collective-permute-start | bytes 786440 | tf_op jit(solution)/shard_map/ppermute | solution.py:78
  (126 other events, 1392.8 us)
Sparse Core Ops, SparseCore 0:
  44.2 56.4 all-gather.3
  102.6 42.9 all-gather.5
  147.6 84.4 all-gather.7
  262.6 103.5 reduce-scatter.3
  369.4 66.9 reduce-scatter.5
  443.3 59.5 reduce-scatter.7

commit v5 on v4

--- a/solution.py
+++ b/solution.py
@@ -1030,7 +1030,7 @@
             ],
         ),
         out_shape=[shape((GROUP, HEAD_SIZE, blk), LOW), shape((total, LANES), LOW)],
-        compiler_params=pltpu.CompilerParams(vmem_limit_bytes=60 * 2**20),
+        compiler_params=pltpu.CompilerParams(vmem_limit_bytes=16 * 2**20 + 2816 * total),
         cost_estimate=guess(27),
         name="attend_back",
     )(place, q_back, d_rows, out, key_all, masks[1])

time: 546 us -> 545 us (level)
  waiting for transfers between devices: 119 us -> 129 us
  Pallas kernels: 138 us -> 132 us
    ppermute x21, waiting for transfers between devices: 49.9 us -> 58 us  [swapped(): return lax.ppermute(value, axis, [(i, i ^ bit) for i in range(count)])]
    pallas_call x2, Pallas kernels: 13.8 us -> 8.2 us  [attend_back(): pl.pallas_call(attend_back_kernel, grid_spec=pltpu.PrefetchScalarGridSpec...]
    unnamed x189 -> x181, local copies, waits for them, and re-layouts: 17.7 us -> 16.1 us
  transfers between devices with their start and end apart: 59 -> 59, of which waited for: 18 -> 19; matrix products, arithmetic and copies ran while one was open for 22% -> 22% of each run, Pallas kernels for 20% -> 19%
where the time goes in v5:
time: 545 us; the launch traced here: 536 us
  Pallas kernels  132 us (24%)
  waiting for transfers between devices  129 us (24%)
  starting transfers between devices  112 us (21%)
  local copies, waits for them, and re-layouts  62.5 us (11%)
  matrix products  43.9 us (8%)
  other arithmetic  39.9 us (7%)
  between operations  16.6 us (3%)
    ppermute x30, starting transfers between devices, sent_on(): got.append(lax.ppermute(pieces((place + step) % count), 'head', pairs))  76.8 us
    pallas_call x4, Pallas kernels, call(): pl.pallas_call(kernel, grid=(parts,), in_specs=[spec(block, how) for _, b...  59.1 us
    ppermute x21, waiting for transfers between devices, swapped(): return lax.ppermute(value, axis, [(i, i ^ bit) for i in range(count)])  58 us
    ppermute x30, waiting for transfers between devices, sent_on(): got.append(lax.ppermute(pieces((place + step) % count), 'head', pairs))  38.3 us
    ppermute x21, starting transfers between devices, swapped(): return lax.ppermute(value, axis, [(i, i ^ bit) for i in range(count)])  32.2 us
    pallas_call x1, Pallas kernels, feed_forward(): pl.pallas_call(feed_kernel, grid=(folds,), in_specs=[whole, whole, whole,...  30.5 us
    dot_general x12, matrix products, nn(): return jnp.dot(left, right, preferred_element_type=jnp.float32)  28.6 us
    reduce_scatter x3, waiting for transfers between devices, sum_wide(): return lax.psum_scatter(array, 'wide', scatter_dimension=0, tiled=True)  18.2 us
  transfers between devices with their start and end apart: 59, of which 19 were waited for; matrix products, arithmetic and copies ran while one was open for 22% of the time, Pallas kernels for 19%

profile of v5, /device:TPU:24, one launch (start us, length us, event | category | flops | bytes accessed | tf_op | source)
XLA Modules:
  0.0 536.3 jit_solution(17890121539126704476)
XLA Ops:
  55.4 6.7 %collective-permute-start.6 = (bf16[128,1024]{1,0:T(8,128)(2,1)S(1)}, bf16[128,1024]{1,0:T(8,128)(2,1)S(1)}, u32[]{:S(2)}, u32[]{:S(2)}) collective-permute-start(bf16[128,1024]{1,0:T(8,128)(2,1)S(1)} %get-tuple-element.569), channel_id=1, source_target_pairs={{0,8},{8,16},{24,0},{1,9},{9,17},{25,1},{2,10},{10,18},{26,2},{3,1... | collective-permute-start | bytes 786440 | tf_op jit(solution)/shard_map/ppermute | solution.py:78
  68.8 5.2 collective-permute-done.7
  78.0 7.5 %collective-permute-start.14 = (bf16[32,6144]{1,0:T(8,128)(2,1)}, bf16[32,6144]{1,0:T(8,128)(2,1)}, u32[]{:S(2)}, u32[]{:S(2)}) collective-permute-start(bf16[32,6144]{1,0:T(8,128)(2,1)} %get-tuple-element.233), channel_id=1, source_target_pairs={{0,8},{8,16},{24,0},{1,9},{9,17},{25,1},{2,10},{10,18},{26,2},{3,1... | collective-permute-start | bytes 1179656 | tf_op jit(solution)/shard_map/ppermute | solution.py:78
  85.5 6.1 %collective-permute-start.15 = (bf16[32,6144]{1,0:T(8,128)(2,1)}, bf16[32,6144]{1,0:T(8,128)(2,1)}, u32[]{:S(2)}, u32[]{:S(2)}) collective-permute-start(bf16[32,6144]{1,0:T(8,128)(2,1)} %get-tuple-element.233), channel_id=1, source_target_pairs={{0,16},{16,0},{24,8},{1,17},{17,1},{25,9},{2,18},{18,2},{26,10},{3... | collective-permute-start | bytes 1179656 | tf_op jit(solution)/shard_map/ppermute | solution.py:78
  109.3 5.2 fusion.24.x_ref.xp_ref.bc_ref.bcp_ref.dt_ref
  118.8 5.3 fusion.26.z_ref
  127.4 11.0 %mamba_local.1 = (f32[512,1536]{1,0:T(8,128)}, bf16[512,1536]{1,0:T(8,128)(2,1)}, bf16[512,256]{1,0:T(8,128)(2,1)}, bf16[512,256]{1,0:T(8,128)(2,1)}, f32[512,12...) custom-call(f32[512,1920]{1,0:T(8,128)} %copy-done.76, ...), custom_call_target="tpu_custom_call" | custom-call | flops 11000000512 | bytes 33000000 | tf_op jit(solution)/shard_map/mamba_local/pallas_call | solution.py:652
  173.9 11.3 %collective-permute-done.18.got_ref = bf16[144,1536]{1,0:T(8,128)(2,1)S(1)} collective-permute-done((bf16[144,1536]{1,0:T(8,128)(2,1)S(1)}, bf16[144,1536]{1,0:T(8,128)(2,1)S(1)}, u32[]{:S(2)}, u32[]{:S(2)}) %collective-permute-start.18) | collective-permute-done | bytes 442400 | tf_op jit(solution)/shard_map/ppermute | solution.py:56
  196.9 6.1 %collective-permute-done.23.got_ref = bf16[144,1536]{1,0:T(8,128)(2,1)S(1)} collective-permute-done((bf16[144,1536]{1,0:T(8,128)(2,1)S(1)}, bf16[144,1536]{1,0:T(8,128)(2,1)S(1)}, u32[]{:S(2)}, u32[]{:S(2)}) %collective-permute-start.23) | collective-permute-done | bytes 442400 | tf_op jit(solution)/shard_map/ppermute | solution.py:56
  205.7 11.2 %mamba_mix.1 = (bf16[512,1536]{1,0:T(8,128)(2,1)}, f32[512,1536]{1,0:T(8,128)}, bf16[4,128,1536]{2,1,0:T(8,128)(2,1)}) custom-call(f32[512,1536]{1,0:T(8,128)} %get-tuple-element.245.act_ref, bf16[512,256]{1,0:T(8,128)(2,1)} %get-tuple-element.246.bcact_ref, f32[512,1536]{1,0:T(8,128)} %fusion.26.z_ref, f32[512,128]{1,0:T(8,128)} %get-tuple-element.248.step_ref, ...), custom_call_target="tpu_custom_call" | custom-call | flops 11000000512 | bytes 33000000 | tf_op jit(solution)/shard_map/mamba_mix/pallas_call | solution.py:652
  227.0 6.4 %all-gather.8.cloned.1.call-done.w_ref = bf16[1024,6144]{1,0:T(8,128)(2,1)} async-done(((bf16[128,6144]{1,0:T(8,128)(2,1)}), bf16[1024,6144]{1,0:T(8,128)(2,1)}) %all-gather.8.cloned.1.call-update) | async-done | bytes 12582928 | tf_op jit(solution)/shard_map/all_gather | solution.py:252
  233.4 30.5 %feed_forward.1 = (f32[512,1024]{1,0:T(8,128)}, f32[512,1024]{1,0:T(8,128)}, bf16[1024,6144]{1,0:T(8,128)(2,1)}) custom-call(bf16[512,1024]{1,0:T(8,128)(2,1)} %multiply_convert_fusion.x_ref, bf16[512,1024]{1,0:T(8,128)(2,1)} %fusion.43.gy_ref, bf16[512,1024]{1,0:T(8,128)(2,1)} %bitcast.339, bf16[1024,6144]{1,0:T(8,128)(2,1)} %all-gather.8.cloned.1.call-done.w_ref), custom_call_target="tpu_custom_call" | custom-call | flops 35000000512 | bytes 105000000 | tf_op jit(solution)/shard_map/feed_forward/pallas_call | solution.py:1077
  275.7 12.7 %mamba_gate_back.1 = (bf16[512,1536]{1,0:T(8,128)(2,1)}, f32[512,1536]{1,0:T(8,128)}, bf16[144,1536]{1,0:T(8,128)(2,1)}, f32[128,1536]{1,0:T(8,128)}, f32[8,1536]{1,0:T(8,128)}) custom-call(f32[512,1536]{1,0:T(8,128)} %fusion.169.dym_ref, f32[512,1536]{1,0:T(8,128)} %get-tuple-element.277.y_ref, f32[512,1536]{1,0:T(8,128)} %fusion.26.z_ref, ...), custom_call_target="tpu_custom_call" | custom-call | flops 11000000512 | bytes 33000000 | tf_op jit(solution)/shard_map/mamba_gate_back/pallas_call | solution.py:652
  298.6 15.0 %collective-permute-done.25.got_ref = bf16[144,1536]{1,0:T(8,128)(2,1)S(1)} collective-permute-done((bf16[144,1536]{1,0:T(8,128)(2,1)S(1)}, bf16[144,1536]{1,0:T(8,128)(2,1)S(1)}, u32[]{:S(2)}, u32[]{:S(2)}) %collective-permute-start.25) | collective-permute-done | bytes 442400 | tf_op jit(solution)/shard_map/ppermute | solution.py:56
  321.1 16.3 %collective-permute-done.26.got_ref = bf16[144,1536]{1,0:T(8,128)(2,1)S(1)} collective-permute-done((bf16[144,1536]{1,0:T(8,128)(2,1)S(1)}, bf16[144,1536]{1,0:T(8,128)(2,1)S(1)}, u32[]{:S(2)}, u32[]{:S(2)}) %collective-permute-start.26) | collective-permute-done | bytes 442400 | tf_op jit(solution)/shard_map/ppermute | solution.py:56
  349.9 18.2 %reduce-scatter.4.cloned.1.call-done = bf16[128,6144]{1,0:T(8,128)(2,1)} async-done(((bf16[1024,6144]{1,0:T(8,128)(2,1)}), bf16[128,6144]{1,0:T(8,128)(2,1)}) %reduce-scatter.4.cloned.1.call-update) | async-done | bytes 1572880 | tf_op jit(solution)/shard_map/reduce_scatter | solution.py:248
  382.3 24.2 %mamba_scan_back.1 = (bf16[512,1920]{1,0:T(8,128)(2,1)}, f32[8,1536]{1,0:T(8,128)}, f32[8,128]{1,0:T(8,128)}, f32[8,1792]{1,0:T(8,128)}, f32[8,1792]{1,0:T(8,128)}, /*index=5*/f32[8,1792]{1,0:T(8,128)}) custom-call(f32[512,1536]{1,0:T(8,128)} %get-tuple-element.245.act_ref, bf16[512,1536]{1,0:T(8,128)(2,1)} %get-tuple-element.316.slope_ref, ...), custom_call_target="tpu_custom_call" | custom-call | flops 23000000512 | bytes 69000000 | tf_op jit(solution)/shard_map/mamba_scan_back/pallas_call | solution.py:652
  407.6 6.2 %collective-permute-done.33 = bf16[32,6144]{1,0:T(8,128)(2,1)} collective-permute-done((bf16[32,6144]{1,0:T(8,128)(2,1)}, bf16[32,6144]{1,0:T(8,128)(2,1)}, u32[]{:S(2)}, u32[]{:S(2)}) %collective-permute-start.33) | collective-permute-done | bytes 393248 | tf_op jit(solution)/shard_map/ppermute | solution.py:78
  423.9 8.5 %last_grads.1 = bf16[1024,2688]{1,0:T(8,128)(2,1)} custom-call(bf16[512,1024]{1,0:T(8,128)(2,1)} %copy-done.43, bf16[512,1920]{1,0:T(8,128)(2,1)} %fusion.104.scan_ref, bf16[512,512]{1,0:T(8,128)(2,1)} %bitcast.349, bf16[512,256]{1,0:T(8,128)(2,1)} %fusion.58.kv_ref, f32[1024,128]{1,0:T(8,128)} %pad.33.small_ref), custom_call_target="tpu_custom_call" | custom-call | flops 8000000000 | bytes 24000000 | tf_op jit(solution)/shard_map/last_grads/pallas_call | solution.py:1107
  432.4 10.2 %collective-permute-done.36 = bf16[128,1024]{1,0:T(8,128)(2,1)S(1)} collective-permute-done((bf16[128,1024]{1,0:T(8,128)(2,1)S(1)}, bf16[128,1024]{1,0:T(8,128)(2,1)S(1)}, u32[]{:S(2)}, u32[]{:S(2)}) %collective-permute-start.36) | collective-permute-done | bytes 262176 | tf_op jit(solution)/shard_map/ppermute | solution.py:78
  457.4 11.7 %input_back.1 = bf16[512,1024]{1,0:T(8,128)(2,1)} custom-call(bf16[512,1920]{1,0:T(8,128)(2,1)} %fusion.104.scan_ref, bf16[512,1536]{1,0:T(8,128)(2,1)} %get-tuple-element.311.gate_ref, bf16[512,512]{1,0:T(8,128)(2,1)} %bitcast.350, bf16[512,256]{1,0:T(8,128)(2,1)} %fusion.58.kv_ref, bf16[1024,4224]{1,0:T(8,128)(2,1)} %all-gather.4.cloned.1.call-done.w_ref, ...), custom_call_target="tpu_custom_call" | custom-call | flops 10000000000 | bytes 30000000 | tf_op jit(solution)/shard_map/input_back/pallas_call | solution.py:1134
  469.1 6.4 %collective-permute-done.41 = bf16[32,3584]{1,0:T(8,128)(2,1)S(1)} collective-permute-done((bf16[32,3584]{1,0:T(8,128)(2,1)S(1)}, bf16[32,3584]{1,0:T(8,128)(2,1)S(1)}, u32[]{:S(2)}, u32[]{:S(2)}) %collective-permute-start.41) | collective-permute-done | bytes 229408 | tf_op jit(solution)/shard_map/ppermute | solution.py:78
  511.0 6.9 %collective-permute-start.52 = (f32[72]{0:T(128)S(1)}, f32[72]{0:T(128)S(1)}, u32[]{:S(2)}, u32[]{:S(2)}) collective-permute-start(f32[72]{0:T(128)S(1)} %add.645), channel_id=1, source_target_pairs={{0,16},{8,24},{16,0},{24,8},{1,17},{9,25},{17,1},{25,9},{2,18},{10... | collective-permute-start | bytes 872 | tf_op jit(solution)/shard_map/ppermute | solution.py:56
  518.6 6.3 %collective-permute-done.52 = f32[72]{0:T(128)S(1)} collective-permute-done((f32[72]{0:T(128)S(1)}, f32[72]{0:T(128)S(1)}, u32[]{:S(2)}, u32[]{:S(2)}) %collective-permute-start.52) | collective-permute-done | bytes 320 | tf_op jit(solution)/shard_map/ppermute | solution.py:56
  (524 shorter events, 264.6 us)
Async XLA Ops:
  7.2 93.5 %all-gather.4.cloned.1.call-start = ((), (), s32[]{:S(2)}) async-start(), calls=%async_computation.3 | async-start | bytes 9732096 | tf_op jit(solution)/shard_map/all_gather | solution.py:252
  13.0 27.5 %collective-permute-start = (bf16[32,4224]{1,0:T(8,128)(2,1)S(1)}, bf16[32,4224]{1,0:T(8,128)(2,1)S(1)}, u32[]{:S(2)}, u32[]{:S(2)}) collective-permute-start(bf16[32,4224]{1,0:T(8,128)(2,1)S(1)} %concatenate.103), channel_id=1, source_target_pairs={{0,8},{8,16},{24,0},{1,9},{9,17},{25,1},{2,10},{10,18},{26,2},{3,1... | collective-permute-start | bytes 811016 | tf_op jit(solution)/shard_map/ppermute | solution.py:78
  14.3 26.2 %collective-permute-start.1 = (bf16[32,4224]{1,0:T(8,128)(2,1)S(1)}, bf16[32,4224]{1,0:T(8,128)(2,1)}, u32[]{:S(2)}, u32[]{:S(2)}) collective-permute-start(bf16[32,4224]{1,0:T(8,128)(2,1)S(1)} %concatenate.103), channel_id=1, source_target_pairs={{0,16},{16,0},{24,8},{1,17},{17,1},{25,9},{2,18},{18,2},{26,10},{3... | collective-permute-start | bytes 811016 | tf_op jit(solution)/shard_map/ppermute | solution.py:78
  44.1 101.8 %all-gather.6.cloned.1.call-start = ((), (), s32[]{:S(2)}) async-start(), calls=%async_computation.4 | async-start | bytes 4718592 | tf_op jit(solution)/shard_map/all_gather | solution.py:252
  78.0 60.4 %collective-permute-start.14 = (bf16[32,6144]{1,0:T(8,128)(2,1)}, bf16[32,6144]{1,0:T(8,128)(2,1)}, u32[]{:S(2)}, u32[]{:S(2)}) collective-permute-start(bf16[32,6144]{1,0:T(8,128)(2,1)} %get-tuple-element.233), channel_id=1, source_target_pairs={{0,8},{8,16},{24,0},{1,9},{9,17},{25,1},{2,10},{10,18},{26,2},{3,1... | collective-permute-start | bytes 1179656 | tf_op jit(solution)/shard_map/ppermute | solution.py:78
  85.5 52.9 %collective-permute-start.15 = (bf16[32,6144]{1,0:T(8,128)(2,1)}, bf16[32,6144]{1,0:T(8,128)(2,1)}, u32[]{:S(2)}, u32[]{:S(2)}) collective-permute-start(bf16[32,6144]{1,0:T(8,128)(2,1)} %get-tuple-element.233), channel_id=1, source_target_pairs={{0,16},{16,0},{24,8},{1,17},{17,1},{25,9},{2,18},{18,2},{26,10},{3... | collective-permute-start | bytes 1179656 | tf_op jit(solution)/shard_map/ppermute | solution.py:78
  91.6 46.8 %collective-permute-start.16 = (bf16[32,6144]{1,0:T(8,128)(2,1)}, bf16[32,6144]{1,0:T(8,128)(2,1)}, u32[]{:S(2)}, u32[]{:S(2)}) collective-permute-start(bf16[32,6144]{1,0:T(8,128)(2,1)} %get-tuple-element.233), channel_id=1, source_target_pairs={{8,0},{16,8},{24,16},{9,1},{17,9},{25,17},{10,2},{18,10},{26,18},{... | collective-permute-start | bytes 1179656 | tf_op jit(solution)/shard_map/ppermute | solution.py:78
  102.2 131.2 %all-gather.8.cloned.1.call-start = ((), (), s32[]{:S(2)}) async-start(), calls=%async_computation.5 | async-start | bytes 14155776 | tf_op jit(solution)/shard_map/all_gather | solution.py:252
  116.3 22.1 %collective-permute-start.13 = (bf16[2,512,128]{2,1,0:T(8,128)(2,1)S(1)}, bf16[2,512,128]{2,1,0:T(8,128)(2,1)S(1)}, u32[]{:S(2)}, u32[]{:S(2)}) collective-permute-start(bf16[2,512,128]{2,1,0:T(8,128)(2,1)S(1)} %maximum_select_fusion.4), channel_id=1, source_target_pairs={{0,2},{1,3},{2,0},{3,1},{4,6},{5,7},{6,4},{7,5},{8,10},{9,11},{10,... | collective-permute-start | bytes 786440 | tf_op jit(solution)/shard_map/ppermute | solution.py:56
  145.9 222.2 %reduce-scatter.4.cloned.1.call-start = ((), (), s32[]{:S(2)}) async-start(), calls=%async_computation.6 | async-start | bytes 14155776 | tf_op jit(solution)/shard_map/reduce_scatter | solution.py:248
  149.8 24.1 %collective-permute-start.19 = (bf16[128,1024]{1,0:T(8,128)(2,1)}, bf16[128,1024]{1,0:T(8,128)(2,1)}, u32[]{:S(2)}, u32[]{:S(2)}) collective-permute-start(bf16[128,1024]{1,0:T(8,128)(2,1)} %get-tuple-element.565), channel_id=1, source_target_pairs={{0,8},{8,16},{24,0},{1,9},{9,17},{25,1},{2,10},{10,18},{26,2},{3,1... | collective-permute-start | bytes 786440 | tf_op jit(solution)/shard_map/ppermute | solution.py:78
  264.0 178.7 %reduce-scatter.6.cloned.1.call-start = ((), (), s32[]{:S(2)}) async-start(), calls=%async_computation.7 | async-start | bytes 8257536 | tf_op jit(solution)/shard_map/reduce_scatter | solution.py:248
  314.0 23.5 %collective-permute-start.27 = (bf16[4,512,128]{2,1,0:T(8,128)(2,1)S(1)}, bf16[4,512,128]{2,1,0:T(8,128)(2,1)S(1)}, u32[]{:S(2)}, u32[]{:S(2)}) collective-permute-start(bf16[4,512,128]{2,1,0:T(8,128)(2,1)S(1)} %dynamic-slice_bitcast_fusion.1), channel_id=1, source_target_pairs={{0,1},{1,0},{2,3},{3,2},{4,5},{5,4},{6,7},{7,6},{8,9},{9,8},{10,11... | collective-permute-start | bytes 1572872 | tf_op jit(solution)/shard_map/ppermute | solution.py:56
  314.0 23.4 %collective-permute-start.26 = (bf16[144,1536]{1,0:T(8,128)(2,1)S(1)}, bf16[144,1536]{1,0:T(8,128)(2,1)S(1)}, u32[]{:S(2)}, u32[]{:S(2)}) collective-permute-start(bf16[144,1536]{1,0:T(8,128)(2,1)S(1)} %get-tuple-element.297), channel_id=1, source_target_pairs={{0,4},{1,5},{2,6},{3,7},{4,0},{5,1},{6,2},{7,3},{8,12},{9,13},{10,... | collective-permute-start | bytes 1327112 | tf_op jit(solution)/shard_map/ppermute | solution.py:56
  368.1 135.4 %reduce-scatter.8.cloned.1.call-start = ((), (), s32[]{:S(2)}) async-start(), calls=%async_computation.8 | async-start | bytes 6193152 | tf_op jit(solution)/shard_map/reduce_scatter | solution.py:248
  372.9 34.6 %collective-permute-start.30 = (bf16[512,256]{1,0:T(8,128)(2,1)}, bf16[512,256]{1,0:T(8,128)(2,1)}, u32[]{:S(2)}, u32[]{:S(2)}) collective-permute-start(bf16[512,256]{1,0:T(8,128)(2,1)} %get-tuple-element.535), channel_id=1, source_target_pairs={{0,4},{1,5},{2,6},{3,7},{4,0},{5,1},{6,2},{7,3},{8,12},{9,13},{10,... | collective-permute-start | bytes 786440 | tf_op jit(solution)/shard_map/ppermute | solution.py:56
  373.6 33.9 %collective-permute-start.31 = (bf16[512,256]{1,0:T(8,128)(2,1)}, bf16[512,256]{1,0:T(8,128)(2,1)}, u32[]{:S(2)}, u32[]{:S(2)}) collective-permute-start(bf16[512,256]{1,0:T(8,128)(2,1)} %get-tuple-element.533), channel_id=1, source_target_pairs={{0,6},{1,7},{2,4},{3,5},{4,2},{5,3},{6,0},{7,1},{8,14},{9,15},{10,... | collective-permute-start | bytes 786440 | tf_op jit(solution)/shard_map/ppermute | solution.py:56
  376.3 31.3 %collective-permute-start.32 = (bf16[32,6144]{1,0:T(8,128)(2,1)}, bf16[32,6144]{1,0:T(8,128)(2,1)}, u32[]{:S(2)}, u32[]{:S(2)}) collective-permute-start(bf16[32,6144]{1,0:T(8,128)(2,1)} %get-tuple-element.524), channel_id=1, source_target_pairs={{0,8},{8,16},{16,24},{1,9},{9,17},{17,25},{2,10},{10,18},{18,26},{... | collective-permute-start | bytes 1179656 | tf_op jit(solution)/shard_map/ppermute | solution.py:78
  377.6 36.2 %collective-permute-start.33 = (bf16[32,6144]{1,0:T(8,128)(2,1)}, bf16[32,6144]{1,0:T(8,128)(2,1)}, u32[]{:S(2)}, u32[]{:S(2)}) collective-permute-start(bf16[32,6144]{1,0:T(8,128)(2,1)} %get-tuple-element.523), channel_id=1, source_target_pairs={{0,16},{8,24},{16,0},{1,17},{9,25},{17,1},{2,18},{10,26},{18,2},{3... | collective-permute-start | bytes 1179656 | tf_op jit(solution)/shard_map/ppermute | solution.py:78
  380.8 32.9 %collective-permute-start.34 = (bf16[32,6144]{1,0:T(8,128)(2,1)}, bf16[32,6144]{1,0:T(8,128)(2,1)}, u32[]{:S(2)}, u32[]{:S(2)}) collective-permute-start(bf16[32,6144]{1,0:T(8,128)(2,1)} %get-tuple-element.522), channel_id=1, source_target_pairs={{0,24},{8,0},{16,8},{1,25},{9,1},{17,9},{2,26},{10,2},{18,10},{3,2... | collective-permute-start | bytes 1179656 | tf_op jit(solution)/shard_map/ppermute | solution.py:78
  418.8 23.8 %collective-permute-start.36 = (bf16[128,1024]{1,0:T(8,128)(2,1)S(1)}, bf16[128,1024]{1,0:T(8,128)(2,1)S(1)}, u32[]{:S(2)}, u32[]{:S(2)}) collective-permute-start(bf16[128,1024]{1,0:T(8,128)(2,1)S(1)} %get-tuple-element.531), channel_id=1, source_target_pairs={{0,16},{8,24},{16,0},{1,17},{9,25},{17,1},{2,18},{10,26},{18,2},{3... | collective-permute-start | bytes 786440 | tf_op jit(solution)/shard_map/ppermute | solution.py:78
  420.1 22.5 %collective-permute-start.37 = (bf16[128,1024]{1,0:T(8,128)(2,1)S(1)}, bf16[128,1024]{1,0:T(8,128)(2,1)S(1)}, u32[]{:S(2)}, u32[]{:S(2)}) collective-permute-start(bf16[128,1024]{1,0:T(8,128)(2,1)S(1)} %get-tuple-element.530), channel_id=1, source_target_pairs={{0,24},{8,0},{16,8},{1,25},{9,1},{17,9},{2,26},{10,2},{18,10},{3,2... | collective-permute-start | bytes 786440 | tf_op jit(solution)/shard_map/ppermute | solution.py:78
  480.5 23.1 %collective-permute-start.45 = (bf16[128,1024]{1,0:T(8,128)(2,1)S(1)}, bf16[128,1024]{1,0:T(8,128)(2,1)S(1)}, u32[]{:S(2)}, u32[]{:S(2)}) collective-permute-start(bf16[128,1024]{1,0:T(8,128)(2,1)S(1)} %get-tuple-element.527), channel_id=1, source_target_pairs={{0,16},{8,24},{16,0},{1,17},{9,25},{17,1},{2,18},{10,26},{18,2},{3... | collective-permute-start | bytes 786440 | tf_op jit(solution)/shard_map/ppermute | solution.py:78
  481.8 21.8 %collective-permute-start.46 = (bf16[128,1024]{1,0:T(8,128)(2,1)S(1)}, bf16[128,1024]{1,0:T(8,128)(2,1)S(1)}, u32[]{:S(2)}, u32[]{:S(2)}) collective-permute-start(bf16[128,1024]{1,0:T(8,128)(2,1)S(1)} %get-tuple-element.526), channel_id=1, source_target_pairs={{0,24},{8,0},{16,8},{1,25},{9,1},{17,9},{2,26},{10,2},{18,10},{3,2... | collective-permute-start | bytes 786440 | tf_op jit(solution)/shard_map/ppermute | solution.py:78
  (122 other events, 1286.9 us)
Sparse Core Ops, SparseCore 0:
  44.2 56.4 all-gather.3
  102.6 43.2 all-gather.5
  147.8 85.5 all-gather.7
  264.1 103.9 reduce-scatter.3
  371.3 66.8 reduce-scatter.5
  443.6 58.6 reduce-scatter.7
